TPU v7x, 32 devices: a whole 2x2x4 slice. The times are simulated.
32 devices in a mesh: half: 2 (over x), mp: 4 (over y, core), batch: 4 (over z).
Axes of the slice: x: 2, y: 2, z: 4, core: 2. Of those that a mesh axis runs over, the one named last changes fastest.
Arguments:
- tokens: int32 [2, 4, 4, 256], replicated, may hold values from 0 to 151935
- lengths: int32 [2, 4], replicated, may hold values from 512 to 1024
- labels: int32 [2, 4], replicated, may hold values 0 or 1
- scored: int32 [2, 4, 4, 16], replicated, may hold values from 0 to 254, as said below
- qkv_weight: float32 [896, 1152], P(('half', 'mp', 'batch')), may hold values from -0.1875 to 0.1875
- out_weight: float32 [896, 896], P(('half', 'mp', 'batch')), may hold values from -0.75 to 0.75
- gu_weight: float32 [896, 9728], P(('half', 'mp', 'batch')), may hold values from -0.1875 to 0.1875
- down_weight: float32 [4864, 896], P(('half', 'mp', 'batch')), may hold values from -0.078125 to 0.078125
- embed_weight: float32 [151936, 896], P(('half', 'mp', 'batch')), may hold values from -0.25 to 0.25
- small_params: float32 [30, 128], P(None, ('half', 'mp', 'batch'))
- moment_qkv: float32 [896, 1152], P(('half', 'mp', 'batch')), may hold values from -4.5776367e-05 to 4.5776367e-05
- moment_out: float32 [896, 896], P(('half', 'mp', 'batch')), may hold values from -4.5776367e-05 to 4.5776367e-05
- moment_gu: float32 [896, 9728], P(('half', 'mp', 'batch')), may hold values from -4.5776367e-05 to 4.5776367e-05
- moment_down: float32 [4864, 896], P(('half', 'mp', 'batch')), may hold values from -4.5776367e-05 to 4.5776367e-05
- moment_embed: float32 [151936, 896], P(('half', 'mp', 'batch')), may hold values from -4.5776367e-05 to 4.5776367e-05
- moment_small: float32 [30, 128], P(None, ('half', 'mp', 'batch')), may hold values from -0.00018310547 to 0.00018310547
- square_qkv: float32 [896, 1152], P(('half', 'mp', 'batch')), may hold values from 6.5e-11 to 2.6e-10
- square_out: float32 [896, 896], P(('half', 'mp', 'batch')), may hold values from 6.5e-11 to 2.6e-10
- square_gu: float32 [896, 9728], P(('half', 'mp', 'batch')), may hold values from 6.5e-11 to 2.6e-10
- square_down: float32 [4864, 896], P(('half', 'mp', 'batch')), may hold values from 6.5e-11 to 2.6e-10
- square_embed: float32 [151936, 896], P(('half', 'mp', 'batch')), may hold values from 6.5e-11 to 2.6e-10
- square_small: float32 [30, 128], P(None, ('half', 'mp', 'batch')), may hold values from 1e-09 to 4e-09
- ref_qkv: bfloat16 [896, 1152], P(('half', 'mp', 'batch')), may hold values from -0.1875 to 0.1875
- ref_out: bfloat16 [896, 896], P(('half', 'mp', 'batch')), may hold values from -0.75 to 0.75
- ref_gu: bfloat16 [896, 9728], P(('half', 'mp', 'batch')), may hold values from -0.1875 to 0.1875
- ref_down: bfloat16 [4864, 896], P(('half', 'mp', 'batch')), may hold values from -0.078125 to 0.078125
- ref_embed: bfloat16 [151936, 896], P(('half', 'mp', 'batch')), may hold values from -0.25 to 0.25
- ref_small: bfloat16 [30, 128], P(None, ('half', 'mp', 'batch'))
Outputs:
- new_qkv: float32 [896, 1152], P(('half', 'mp', 'batch'))
- new_out: float32 [896, 896], P(('half', 'mp', 'batch'))
- new_gu: float32 [896, 9728], P(('half', 'mp', 'batch'))
- new_down: float32 [4864, 896], P(('half', 'mp', 'batch'))
- new_embed: float32 [151936, 896], P(('half', 'mp', 'batch'))
- clipped_small: float32 [30, 128], P(None, ('half', 'mp', 'batch'))
- next_moment_qkv: float32 [896, 1152], P(('half', 'mp', 'batch'))
- next_moment_out: float32 [896, 896], P(('half', 'mp', 'batch'))
- next_moment_gu: float32 [896, 9728], P(('half', 'mp', 'batch'))
- next_moment_down: float32 [4864, 896], P(('half', 'mp', 'batch'))
- next_moment_embed: float32 [151936, 896], P(('half', 'mp', 'batch'))
- next_moment_small: float32 [30, 128], P(None, ('half', 'mp', 'batch'))
- next_square_qkv: float32 [896, 1152], P(('half', 'mp', 'batch'))
- next_square_out: float32 [896, 896], P(('half', 'mp', 'batch'))
- next_square_gu: float32 [896, 9728], P(('half', 'mp', 'batch'))
- next_square_down: float32 [4864, 896], P(('half', 'mp', 'batch'))
- next_square_embed: float32 [151936, 896], P(('half', 'mp', 'batch'))
- next_square_small: float32 [30, 128], P(None, ('half', 'mp', 'batch'))
- low_qkv: bfloat16 [896, 1152], P(('half', 'mp', 'batch'))
- low_out: bfloat16 [896, 896], P(('half', 'mp', 'batch'))
- low_gu: bfloat16 [896, 9728], P(('half', 'mp', 'batch'))
- low_down: bfloat16 [4864, 896], P(('half', 'mp', 'batch'))
- low_embed: bfloat16 [151936, 896], P(('half', 'mp', 'batch'))
- grad_norm: float32 [], replicated
Inputs may be any that keep to these rules, and one draw needn't show every extreme that they name: `scored`: the 16 entries of each block are distinct and increasing.
All inputs are finite; a program needn't handle non-finite values.
Results may differ from a plain program's by a relative error of at most 0.018.
Values may be sent and summed in bfloat16 or wider, within the bound.
A program may use at most 512 MiB of HBM per device.

v0:
```python
import jax
import jax.numpy as jnp
from jax import lax
from jax.sharding import PartitionSpec as P

MODEL_WIDTH = 896
QUERY_HEADS = 14
KEY_VALUE_HEADS = 2
HEAD_SIZE = 64
FF = 4864
VOC = 151936
TOK = 256
P_SIZE = 16
MICRO = 2
STEP = 5


EPS_NORM = 1e-06
THETA = 1000000.0
BETA = 0.05
CLIP = 0.1
RATE = 0.03
DECAY = 0.01
MOM1 = 0.5
MOM2 = 0.5
EPS_ADAM = 1e-08


def merged(array, axis, combine):
    everything = jax.tree.map(lambda part: lax.all_gather(part, axis), array)
    initial = jax.tree.map(lambda part: part[0], everything)

    def step(k, so_far):
        return combine(so_far, jax.tree.map(lambda part: part[k], everything))

    return lax.fori_loop(1, lax.axis_size(axis), step, initial)


def outer(left, right):
    return lax.dot_general(
        left, right, (((0,), (0,)), ((), ())), preferred_element_type=jnp.float32
    )


def inner_t(left, right):
    return lax.dot_general(
        left, right, (((1,), (1,)), ((), ())), preferred_element_type=jnp.float32
    )


def norm_forward(x, gain):
    scale = lax.rsqrt(jnp.mean(x * x, axis=-1, keepdims=True) + EPS_NORM)
    return (x * scale * gain, scale)


def norm_backward(d_out, x, scale, gain):
    d_gain = jnp.sum(d_out * x * scale, axis=0)
    d_hat = d_out * gain
    d_x = scale * (d_hat - x * scale * scale * jnp.mean(d_hat * x, axis=-1, keepdims=True))
    return (d_x, d_gain)


def angles(token_positions):
    half_size = HEAD_SIZE // 2
    freq = THETA ** (-(jnp.arange(half_size, dtype=jnp.float32) * 2.0) / HEAD_SIZE)
    angle = token_positions.astype(jnp.float32)[:, None] * freq[None, :]
    return (jnp.cos(angle)[:, None, :], jnp.sin(angle)[:, None, :])


def apply_rotary(x, cosine_table, sine_table):
    half_size = x.shape[-1] // 2
    first = x[..., :half_size]
    second = x[..., half_size:]
    return jnp.concatenate(
        [first * cosine_table - second * sine_table, second * cosine_table + first * sine_table],
        axis=-1,
    )


def inverse_rotary(grad, cosine_table, sine_table):
    half_size = grad.shape[-1] // 2
    first = grad[..., :half_size]
    second = grad[..., half_size:]
    return jnp.concatenate(
        [first * cosine_table + second * sine_table, second * cosine_table - first * sine_table],
        axis=-1,
    )


def attend_scores(query_rows, every_key, token_positions, length):
    row_count = query_rows.shape[0]
    block_span = every_key.shape[0]
    grouped_heads = query_rows.reshape(
        row_count, KEY_VALUE_HEADS, QUERY_HEADS // KEY_VALUE_HEADS, HEAD_SIZE
    )
    key_rows = every_key.reshape(block_span, KEY_VALUE_HEADS, HEAD_SIZE)
    scores = jnp.einsum(
        "tkgd,skd->kgts", grouped_heads, key_rows, preferred_element_type=jnp.float32
    ) * HEAD_SIZE ** (-0.5)
    places = jnp.arange(block_span)
    allowed = (places[None, :] <= token_positions[:, None]) & (places[None, :] < length)
    return (jnp.where(allowed, scores, -1e30), allowed)


def attend_forward(query_rows, every_key, every_value, token_positions, length):
    row_count = query_rows.shape[0]
    block_span = every_key.shape[0]
    scores, allowed = attend_scores(query_rows, every_key, token_positions, length)
    top = jnp.max(scores, axis=-1, keepdims=True)
    expo = jnp.exp(scores - top)
    total = jnp.sum(expo, axis=-1, keepdims=True)
    probs = (expo / total).astype(jnp.bfloat16)
    lse = top[..., 0] + jnp.log(total[..., 0])
    out = jnp.einsum(
        "kgts,skd->tkgd",
        probs,
        every_value.reshape(block_span, KEY_VALUE_HEADS, HEAD_SIZE),
        preferred_element_type=jnp.float32,
    )
    return (out.reshape(row_count, QUERY_HEADS * HEAD_SIZE), lse)


def attend_backward(
    attended_gradient, query_rows, every_key, every_value, lse, token_positions, length
):
    row_count = query_rows.shape[0]
    block_span = every_key.shape[0]
    scores, allowed = attend_scores(query_rows, every_key, token_positions, length)
    probs = jnp.where(allowed, jnp.exp(scores - lse[..., None]), 0.0)
    grouped_gradient = attended_gradient.reshape(
        row_count, KEY_VALUE_HEADS, QUERY_HEADS // KEY_VALUE_HEADS, HEAD_SIZE
    )
    grouped_query = query_rows.reshape(
        row_count, KEY_VALUE_HEADS, QUERY_HEADS // KEY_VALUE_HEADS, HEAD_SIZE
    )
    key_rows = every_key.reshape(block_span, KEY_VALUE_HEADS, HEAD_SIZE)
    value_rows = every_value.reshape(block_span, KEY_VALUE_HEADS, HEAD_SIZE)
    d_probs = jnp.einsum(
        "tkgd,skd->kgts", grouped_gradient, value_rows, preferred_element_type=jnp.float32
    )
    delta = jnp.sum(probs * d_probs, axis=-1, keepdims=True)
    d_scores = (probs * (d_probs - delta)).astype(jnp.bfloat16)
    d_queries = jnp.einsum(
        "kgts,skd->tkgd", d_scores, key_rows, preferred_element_type=jnp.float32
    ).reshape(row_count, QUERY_HEADS, HEAD_SIZE) * HEAD_SIZE ** (-0.5)
    keys_gradient = jnp.einsum(
        "kgts,tkgd->skd", d_scores, grouped_query, preferred_element_type=jnp.float32
    ).reshape(block_span, KEY_VALUE_HEADS * HEAD_SIZE) * HEAD_SIZE ** (-0.5)
    d_values = jnp.einsum(
        "kgts,tkgd->skd",
        probs.astype(jnp.bfloat16),
        grouped_gradient,
        preferred_element_type=jnp.float32,
    ).reshape(block_span, KEY_VALUE_HEADS * HEAD_SIZE)
    return (d_queries, keys_gradient, d_values)


def layer_forward(x, weights, gains, turns, length):
    w_qkv, w_out, w_gu, w_down = weights
    gain_attn, gain_mlp, bias = gains
    cosine_table, sine_table, token_positions = turns
    row_count = x.shape[0]
    normed, scale_one = norm_forward(x, gain_attn)
    normed_low = normed.astype(jnp.bfloat16)
    mixed_heads = jnp.dot(normed_low, w_qkv, preferred_element_type=jnp.float32) + bias
    query_rows = apply_rotary(
        mixed_heads[:, :MODEL_WIDTH].reshape(row_count, QUERY_HEADS, HEAD_SIZE),
        cosine_table,
        sine_table,
    ).astype(jnp.bfloat16)
    key_rows = (
        apply_rotary(
            mixed_heads[:, MODEL_WIDTH : MODEL_WIDTH + KEY_VALUE_HEADS * HEAD_SIZE].reshape(
                row_count, KEY_VALUE_HEADS, HEAD_SIZE
            ),
            cosine_table,
            sine_table,
        )
        .reshape(row_count, KEY_VALUE_HEADS * HEAD_SIZE)
        .astype(jnp.bfloat16)
    )
    value_rows = mixed_heads[:, MODEL_WIDTH + KEY_VALUE_HEADS * HEAD_SIZE :].astype(jnp.bfloat16)
    every_key, every_value = (
        lax.all_gather(key_rows, "mp", axis=0, tiled=True),
        lax.all_gather(value_rows, "mp", axis=0, tiled=True),
    )
    attended, lse = attend_forward(query_rows, every_key, every_value, token_positions, length)
    attended_low = attended.astype(jnp.bfloat16)
    middle = x + jnp.dot(attended_low, w_out, preferred_element_type=jnp.float32)
    normed_two, scale_two = norm_forward(middle, gain_mlp)
    normed_two_low = normed_two.astype(jnp.bfloat16)
    gate_up = jnp.dot(normed_two_low, w_gu, preferred_element_type=jnp.float32)
    hidden_low = (jax.nn.silu(gate_up[:, :FF]) * gate_up[:, FF:]).astype(jnp.bfloat16)
    out = middle + jnp.dot(hidden_low, w_down, preferred_element_type=jnp.float32)
    kept = (
        x,
        scale_one,
        normed_low,
        query_rows,
        every_key,
        every_value,
        lse,
        attended_low,
        middle,
        scale_two,
        normed_two_low,
        gate_up,
        hidden_low,
    )
    return (out, kept)


def layer_backward(d_out, kept, weights, gains, turns, length):
    w_qkv, w_out, w_gu, w_down = weights
    gain_attn, gain_mlp, bias = gains
    cosine_table, sine_table, token_positions = turns
    (
        x,
        scale_one,
        normed_low,
        query_rows,
        every_key,
        every_value,
        lse,
        attended_low,
        middle,
        scale_two,
        normed_two_low,
        gate_up,
        hidden_low,
    ) = kept
    row_count = x.shape[0]
    d_branch = d_out.astype(jnp.bfloat16)
    g_down = outer(hidden_low, d_branch)
    d_hidden = inner_t(d_branch, w_down)
    gate = gate_up[:, :FF]
    up_part = gate_up[:, FF:]
    sigma = jax.nn.sigmoid(gate)
    d_gate = d_hidden * up_part * sigma * (1.0 + gate * (1.0 - sigma))
    d_up = d_hidden * gate * sigma
    d_gate_up = jnp.concatenate([d_gate, d_up], axis=1).astype(jnp.bfloat16)
    g_gu = outer(normed_two_low, d_gate_up)
    d_normed_two = inner_t(d_gate_up, w_gu)
    d_middle, g_gain_mlp = norm_backward(d_normed_two, middle, scale_two, gain_mlp)
    d_middle = d_middle + d_out
    d_attn = d_middle.astype(jnp.bfloat16)
    g_out = outer(attended_low, d_attn)
    attended_gradient = inner_t(d_attn, w_out).astype(jnp.bfloat16)
    d_queries, d_keys_all, d_values_all = attend_backward(
        attended_gradient, query_rows, every_key, every_value, lse, token_positions, length
    )
    keys_gradient, d_values = (
        lax.psum_scatter(
            d_keys_all.astype(jnp.bfloat16), "mp", scatter_dimension=0, tiled=True
        ).astype(jnp.float32),
        lax.psum_scatter(
            d_values_all.astype(jnp.bfloat16), "mp", scatter_dimension=0, tiled=True
        ).astype(jnp.float32),
    )
    d_q = inverse_rotary(d_queries, cosine_table, sine_table).reshape(row_count, MODEL_WIDTH)
    key_gradient = inverse_rotary(
        keys_gradient.reshape(row_count, KEY_VALUE_HEADS, HEAD_SIZE), cosine_table, sine_table
    ).reshape(row_count, KEY_VALUE_HEADS * HEAD_SIZE)
    d_mixed = jnp.concatenate([d_q, key_gradient, d_values], axis=1).astype(jnp.bfloat16)
    g_bias = jnp.sum(d_mixed.astype(jnp.float32), axis=0)
    g_qkv = outer(normed_low, d_mixed)
    d_normed = inner_t(d_mixed, w_qkv)
    d_x, g_gain_attn = norm_backward(d_normed, x, scale_one, gain_attn)
    return (d_x + d_middle, (g_qkv, g_out, g_gu, g_down), (g_gain_attn, g_gain_mlp, g_bias))


def combine_parts(first, second):
    top = jnp.maximum(first[0], second[0])
    return (
        top,
        first[1] * jnp.exp(first[0] - top) + second[1] * jnp.exp(second[0] - top),
        first[2] + second[2],
    )


def reduce_grads(parts):
    return (
        lax.psum_scatter(parts[0], ("half", "mp", "batch"), scatter_dimension=0, tiled=True),
        lax.psum_scatter(parts[1], ("half", "mp", "batch"), scatter_dimension=0, tiled=True),
        lax.psum_scatter(parts[2], ("half", "mp", "batch"), scatter_dimension=0, tiled=True),
        lax.psum_scatter(parts[3], ("half", "mp", "batch"), scatter_dimension=0, tiled=True),
        lax.psum_scatter(parts[4], ("half", "mp", "batch"), scatter_dimension=1, tiled=True),
    )


def body(
    tokens,
    lengths,
    labels,
    scored,
    qkv_weight,
    out_weight,
    gu_weight,
    down_weight,
    embed_weight,
    small_params,
    moment_qkv,
    moment_out,
    moment_gu,
    moment_down,
    moment_embed,
    moment_small,
    square_qkv,
    square_out,
    square_gu,
    square_down,
    square_embed,
    square_small,
    ref_qkv,
    ref_out,
    ref_gu,
    ref_down,
    ref_embed,
    ref_small,
):
    masters = (qkv_weight, out_weight, gu_weight, down_weight, embed_weight, small_params)
    firsts = (moment_qkv, moment_out, moment_gu, moment_down, moment_embed, moment_small)
    seconds = (square_qkv, square_out, square_gu, square_down, square_embed, square_small)
    bf16 = jnp.bfloat16
    which = lax.axis_index("half")
    n_mp = lax.axis_size("mp")
    n_batch = lax.axis_size("batch")
    groups = lax.axis_size(("mp", "batch"))
    spots = 2 * groups
    block = embed_weight.shape[0]
    col_width = MODEL_WIDTH // groups
    gathered = (
        lax.all_gather(qkv_weight.astype(bf16), ("half", "mp", "batch"), axis=0, tiled=True),
        lax.all_gather(out_weight.astype(bf16), ("half", "mp", "batch"), axis=0, tiled=True),
        lax.all_gather(gu_weight.astype(bf16), ("half", "mp", "batch"), axis=0, tiled=True),
        lax.all_gather(down_weight.astype(bf16), ("half", "mp", "batch"), axis=0, tiled=True),
        lax.all_gather(small_params.astype(bf16), ("half", "mp", "batch"), axis=1, tiled=True),
        lax.all_gather(ref_qkv, ("half", "mp", "batch"), axis=0, tiled=True),
        lax.all_gather(ref_out, ("half", "mp", "batch"), axis=0, tiled=True),
        lax.all_gather(ref_gu, ("half", "mp", "batch"), axis=0, tiled=True),
        lax.all_gather(ref_down, ("half", "mp", "batch"), axis=0, tiled=True),
        lax.all_gather(ref_small, ("half", "mp", "batch"), axis=1, tiled=True),
    )
    weights = [
        jnp.where(which == 0, mine, theirs) for mine, theirs in zip(gathered[:5], gathered[5:])
    ]
    prm_block = embed_weight.astype(bf16)
    both_tables = (
        jnp.stack([prm_block, ref_embed]).transpose(0, 2, 1).reshape(spots, col_width, block)
    )
    table_t = lax.all_to_all(
        both_tables, ("half", "mp", "batch"), split_axis=0, concat_axis=2, tiled=True
    )[0]
    ids_all = tokens.reshape(MICRO, groups * TOK)
    picks_all = scored.reshape(MICRO, groups * P_SIZE)
    picks_local = scored[:, lax.axis_index("mp"), lax.axis_index("batch")]
    ids_blocks = ids_all.reshape(MICRO, groups, TOK)
    picks_blocks = picks_all.reshape(MICRO, groups, P_SIZE)
    targets = jnp.take_along_axis(ids_blocks, picks_blocks + 1, axis=2).reshape(
        MICRO, groups * P_SIZE
    )
    block_ids = jnp.arange(groups)
    block_pos = block_ids // n_batch
    block_roll = block_ids % n_batch
    places = picks_blocks + (block_pos * TOK)[None, :, None]
    valid = (places + 1 < lengths[:, block_roll][:, :, None]).astype(jnp.float32)
    count = jnp.sum(valid)
    total = MICRO * groups * P_SIZE
    looked = jnp.take(table_t, ids_all.reshape(-1), axis=1).reshape(col_width, MICRO, groups, TOK)
    starts = lax.all_to_all(looked, ("mp", "batch"), split_axis=2, concat_axis=0, tiled=True)[
        :, :, 0
    ].transpose(1, 2, 0)
    vocab_ids = lax.axis_index(("half", "mp", "batch")) * block + jnp.arange(block)
    layer_mats = (weights[0], weights[1], weights[2], weights[3])
    flat = weights[4].astype(jnp.float32).reshape(-1)
    gain_final = flat[2 * MODEL_WIDTH : 3 * MODEL_WIDTH]
    gains = (flat[:MODEL_WIDTH], flat[MODEL_WIDTH : 2 * MODEL_WIDTH], flat[3 * MODEL_WIDTH :])
    token_positions = lax.axis_index("mp") * TOK + jnp.arange(TOK)
    cosine_table, sine_table = angles(token_positions)
    turns = (cosine_table, sine_table, token_positions)
    rollout = lax.axis_index("batch")
    scored_count = groups * P_SIZE
    saved = []
    own_list = []
    other_list = []
    for micro in range(MICRO):
        length = lengths[micro, rollout]
        x_last, kept = layer_forward(
            starts[micro].astype(jnp.float32), layer_mats, gains, turns, length
        )
        final, scale_final = norm_forward(x_last, gain_final)
        row_count = final.astype(bf16)[picks_local[micro]]
        all_rows = lax.all_gather(row_count, ("half", "mp", "batch"), axis=0, tiled=True)
        prm_rows = all_rows[:scored_count]
        logits = jnp.concatenate(
            [inner_t(prm_rows, prm_block), inner_t(all_rows[scored_count:], ref_embed)], axis=0
        )
        both_targets = jnp.concatenate([targets[micro], targets[micro]])
        hit = vocab_ids[None, :] == both_targets[:, None]
        top = jnp.max(logits, axis=-1)
        total_exp = jnp.sum(jnp.exp(logits - top[:, None]), axis=-1)
        target_logit = jnp.sum(jnp.where(hit, logits, 0.0), axis=-1)
        top, total_exp, target_logit = merged(
            (top, total_exp, target_logit), ("half", "mp", "batch"), combine_parts
        )
        lse = top + jnp.log(total_exp)
        logprob = target_logit - lse
        own_list.append(logprob[:scored_count])
        other_list.append(logprob[scored_count:])
        saved.append(
            (
                kept,
                x_last,
                scale_final,
                prm_rows,
                logits[:scored_count],
                hit[:scored_count],
                lse[:scored_count],
                length,
            )
        )
    own_lp = jnp.stack(own_list)
    other_lp = jnp.stack(other_list)
    ratio = (own_lp - other_lp).reshape(MICRO, groups, P_SIZE)
    per_block = jnp.sum(valid * ratio, axis=-1)
    sums = jnp.sum(per_block.reshape(MICRO, n_mp, n_batch), axis=1)
    scale = BETA * total / count
    reward = scale * sums
    outcome = labels.astype(jnp.float32)
    d_reward = (jax.nn.sigmoid(reward) - outcome) / (MICRO * n_batch)
    d_lp = (valid * (d_reward * scale)[:, block_roll][:, :, None]).reshape(MICRO, groups * P_SIZE)
    totals = None
    d_table = jnp.zeros((block, MODEL_WIDTH), jnp.float32)
    d_starts = []
    for micro in range(MICRO):
        kept, x_last, scale_final, prm_rows, logits, hit, lse, length = saved[micro]
        probs = jnp.exp(logits - lse[:, None])
        d_logits = (d_lp[micro][:, None] * (hit.astype(jnp.float32) - probs)).astype(bf16)
        d_all = jnp.dot(d_logits, prm_block, preferred_element_type=jnp.float32)
        d_table = d_table + outer(d_logits, prm_rows)
        padded = jnp.concatenate([d_all, jnp.zeros_like(d_all)], axis=0)
        d_rows = lax.psum_scatter(padded, ("half", "mp", "batch"), scatter_dimension=0, tiled=True)
        d_final = jnp.zeros((TOK, MODEL_WIDTH), jnp.float32).at[picks_local[micro]].add(d_rows)
        d_last, g_gain_final = norm_backward(d_final, x_last, scale_final, gain_final)
        d_start, mats_grad, small_grad = layer_backward(
            d_last, kept, layer_mats, gains, turns, length
        )
        d_starts.append(d_start)
        packed = jnp.concatenate(
            [small_grad[0], small_grad[1], g_gain_final, small_grad[2]]
        ).reshape(-1, 128)
        local = (mats_grad[0], mats_grad[1], mats_grad[2], mats_grad[3], packed)
        totals = local if totals is None else tuple((a + b for a, b in zip(totals, local)))
    totals = reduce_grads(totals)
    start_grads = jnp.stack(d_starts).transpose(2, 0, 1)[:, :, None, :]
    d_look = lax.all_to_all(
        start_grads.astype(jnp.bfloat16), ("mp", "batch"), split_axis=0, concat_axis=2, tiled=True
    ).astype(start_grads.dtype)
    col_grad = (
        jnp.zeros((col_width, VOC), jnp.float32)
        .at[:, ids_all.reshape(-1)]
        .add(d_look.reshape(col_width, -1))
    )
    back = lax.all_to_all(
        col_grad[None].astype(jnp.bfloat16),
        ("half", "mp", "batch"),
        split_axis=2,
        concat_axis=0,
        tiled=True,
    ).astype(jnp.float32)
    embed_grad = d_table + back[:groups].reshape(MODEL_WIDTH, block).T
    owned = (totals[0], totals[1], totals[2], totals[3], embed_grad, totals[4])
    square_sum = sum((jnp.sum(g * g) for g in owned))
    norm = jnp.sqrt(lax.psum(square_sum, ("half", "mp", "batch")))
    factor = jnp.minimum(1.0, CLIP / (norm + 1e-06))
    new_weights, new_firsts, new_seconds, new_lows, clipped_list = ([], [], [], [], [])
    for w, g, m, v in zip(masters, owned, firsts, seconds):
        g = g * factor
        m_new = MOM1 * m + (1.0 - MOM1) * g
        v_new = MOM2 * v + (1.0 - MOM2) * g * g
        update = m_new / (1.0 - MOM1**STEP) / (jnp.sqrt(v_new / (1.0 - MOM2**STEP)) + EPS_ADAM)
        w_new = w - RATE * (update + DECAY * w)
        new_weights.append(w_new)
        new_firsts.append(m_new)
        new_seconds.append(v_new)
        clipped_list.append(g)
        new_lows.append(w_new.astype(bf16))
    return (
        new_weights[0],
        new_weights[1],
        new_weights[2],
        new_weights[3],
        new_weights[4],
        clipped_list[5],
        new_firsts[0],
        new_firsts[1],
        new_firsts[2],
        new_firsts[3],
        new_firsts[4],
        new_firsts[5],
        new_seconds[0],
        new_seconds[1],
        new_seconds[2],
        new_seconds[3],
        new_seconds[4],
        new_seconds[5],
        new_lows[0],
        new_lows[1],
        new_lows[2],
        new_lows[3],
        new_lows[4],
        norm,
    )


def solution(mesh):
    in_specs = (
        P(),
        P(),
        P(),
        P(),
        P(("half", "mp", "batch"), None),
        P(("half", "mp", "batch"), None),
        P(("half", "mp", "batch"), None),
        P(("half", "mp", "batch"), None),
        P(("half", "mp", "batch"), None),
        P(None, ("half", "mp", "batch")),
        P(("half", "mp", "batch"), None),
        P(("half", "mp", "batch"), None),
        P(("half", "mp", "batch"), None),
        P(("half", "mp", "batch"), None),
        P(("half", "mp", "batch"), None),
        P(None, ("half", "mp", "batch")),
        P(("half", "mp", "batch"), None),
        P(("half", "mp", "batch"), None),
        P(("half", "mp", "batch"), None),
        P(("half", "mp", "batch"), None),
        P(("half", "mp", "batch"), None),
        P(None, ("half", "mp", "batch")),
        P(("half", "mp", "batch"), None),
        P(("half", "mp", "batch"), None),
        P(("half", "mp", "batch"), None),
        P(("half", "mp", "batch"), None),
        P(("half", "mp", "batch"), None),
        P(None, ("half", "mp", "batch")),
    )
    out_specs = (
        P(("half", "mp", "batch"), None),
        P(("half", "mp", "batch"), None),
        P(("half", "mp", "batch"), None),
        P(("half", "mp", "batch"), None),
        P(("half", "mp", "batch"), None),
        P(None, ("half", "mp", "batch")),
        P(("half", "mp", "batch"), None),
        P(("half", "mp", "batch"), None),
        P(("half", "mp", "batch"), None),
        P(("half", "mp", "batch"), None),
        P(("half", "mp", "batch"), None),
        P(None, ("half", "mp", "batch")),
        P(("half", "mp", "batch"), None),
        P(("half", "mp", "batch"), None),
        P(("half", "mp", "batch"), None),
        P(("half", "mp", "batch"), None),
        P(("half", "mp", "batch"), None),
        P(None, ("half", "mp", "batch")),
        P(("half", "mp", "batch"), None),
        P(("half", "mp", "batch"), None),
        P(("half", "mp", "batch"), None),
        P(("half", "mp", "batch"), None),
        P(("half", "mp", "batch"), None),
        P(),
    )
    return jax.shard_map(body, mesh=mesh, in_specs=in_specs, out_specs=out_specs, check_vma=False)
```

profile of v0, /device:TPU:0, one launch (start us, length us, event | category | flops | bytes accessed | tf_op | source)
XLA Modules:
  0.0 5663.6 jit_solution(12482869404545939145)
XLA Ops:
  66.1 471.3 %all-gather.8 = bf16[32,4,30]{2,1,0:T(4,128)(2,1)S(1)} all-gather(bf16[1,4,30]{2,1,0:T(4,128)(2,1)S(1)} %convert_bitcast_fusion.6), channel_id=1, replica_groups=mesh['half'=2,'mp'=4,'batch'=4] {'half','mp','batch'}, dimensions={0}, use_global_device_ids=true | all-gather | bytes 7920 | tf_op jit(solution)/shard_map/all_gather | solution.py:337
  537.4 63.9 %all-gather.9 = bf16[32,4,30]{2,1,0:T(4,128)(2,1)S(1)} all-gather(bf16[1,4,30]{2,1,0:T(4,128)(2,1)S(1)} %bitcast.483), channel_id=1, replica_groups=mesh['half'=2,'mp'=4,'batch'=4] {'half','mp','batch'}, dimensions={0}, use_global_device_ids=true | all-gather | bytes 7920 | tf_op jit(solution)/shard_map/all_gather | solution.py:342
  723.1 125.9 %gather_fusion = bf16[8192,56]{1,0:T(8,128)(2,1)} fusion(bf16[56,151936]{0,1:T(8,128)(2,1)} %reshape.791, s32[8192]{0:T(1024)S(1)} %broadcast_clamp_fusion.1), kind=kCustom, calls=%fused_computation | custom fusion | bytes 1867776 | tf_op jit(solution)/shard_map/jit(_take)/gather | solution.py:369
  856.8 67.2 %all-gather.45.cloned.1.call-done = bf16[32,28,9728]{2,1,0:T(8,128)(2,1)} async-done(((bf16[1,28,9728]{2,1,0:T(8,128)(2,1)}), bf16[32,28,9728]{2,1,0:T(8,128)(2,1)}) %all-gather.45.cloned.1.call-update) | async-done | bytes 17432592 | tf_op jit(solution)/shard_map/all_gather | solution.py:340
  1099.1 74.5 %all-gather = bf16[512,896]{1,0:T(8,128)(2,1)S(1)} all-gather(bf16[16,896]{1,0:T(8,128)(2,1)S(1)} %gather_fusion.2), channel_id=2, replica_groups=mesh['half'=2,'mp'=4,'batch'=4] {'half','mp','batch'}, dimensions={0}, use_global_device_ids=true | all-gather | bytes 946176 | tf_op jit(solution)/shard_map/all_gather | solution.py:393
  1193.5 71.5 %all-gather.4 = bf16[512,896]{1,0:T(8,128)(2,1)S(1)} all-gather(bf16[16,896]{1,0:T(8,128)(2,1)S(1)} %gather_fusion.3), channel_id=6, replica_groups=mesh['half'=2,'mp'=4,'batch'=4] {'half','mp','batch'}, dimensions={0}, use_global_device_ids=true | all-gather | bytes 946176 | tf_op jit(solution)/shard_map/all_gather | solution.py:393
  1280.7 65.9 %all-gather.16 = f32[32,1,512]{2,1,0:T(1,128)S(1)} all-gather(f32[1,1,512]{2,1,0:T(1,128)S(1)} %bitcast.475), channel_id=3, replica_groups=mesh['half'=2,'mp'=4,'batch'=4] {'half','mp','batch'}, dimensions={0}, use_global_device_ids=true | all-gather | bytes 67584 | tf_op jit(solution)/shard_map/all_gather | solution.py:30
  1357.8 64.6 %all-gather.17 = f32[32,1,512]{2,1,0:T(1,128)S(1)} all-gather(f32[1,1,512]{2,1,0:T(1,128)S(1)} %bitcast.482), channel_id=4, replica_groups=mesh['half'=2,'mp'=4,'batch'=4] {'half','mp','batch'}, dimensions={0}, use_global_device_ids=true | all-gather | bytes 67584 | tf_op jit(solution)/shard_map/all_gather | solution.py:30
  1422.4 65.2 %all-gather.18 = f32[32,1,512]{2,1,0:T(1,128)S(1)} all-gather(f32[1,1,512]{2,1,0:T(1,128)S(1)} %bitcast.481), channel_id=5, replica_groups=mesh['half'=2,'mp'=4,'batch'=4] {'half','mp','batch'}, dimensions={0}, use_global_device_ids=true | all-gather | bytes 67584 | tf_op jit(solution)/shard_map/all_gather | solution.py:30
  1487.7 64.7 %all-gather.19 = f32[32,1,512]{2,1,0:T(1,128)S(1)} all-gather(f32[1,1,512]{2,1,0:T(1,128)S(1)} %bitcast.474), channel_id=7, replica_groups=mesh['half'=2,'mp'=4,'batch'=4] {'half','mp','batch'}, dimensions={0}, use_global_device_ids=true | all-gather | bytes 67584 | tf_op jit(solution)/shard_map/all_gather | solution.py:30
  1552.4 65.2 %all-gather.20 = f32[32,1,512]{2,1,0:T(1,128)S(1)} all-gather(f32[1,1,512]{2,1,0:T(1,128)S(1)} %bitcast.480), channel_id=8, replica_groups=mesh['half'=2,'mp'=4,'batch'=4] {'half','mp','batch'}, dimensions={0}, use_global_device_ids=true | all-gather | bytes 67584 | tf_op jit(solution)/shard_map/all_gather | solution.py:30
  1617.6 64.7 %all-gather.21 = f32[32,1,512]{2,1,0:T(1,128)S(1)} all-gather(f32[1,1,512]{2,1,0:T(1,128)S(1)} %bitcast.479), channel_id=9, replica_groups=mesh['half'=2,'mp'=4,'batch'=4] {'half','mp','batch'}, dimensions={0}, use_global_device_ids=true | all-gather | bytes 67584 | tf_op jit(solution)/shard_map/all_gather | solution.py:30
  1720.1 117.0 %reduce-scatter.24.cloned.1.call-done = f32[16,896]{1,0:T(8,128)} async-done(((f32[512,896]{1,0:T(8,128)}), f32[16,896]{1,0:T(8,128)}) %reduce-scatter.24.cloned.1.call-update) | async-done | bytes 57360 | tf_op jit(solution)/shard_map/reduce_scatter | solution.py:442
  1841.1 134.1 %reduce-scatter.18.cloned.1.call-done = f32[16,896]{1,0:T(8,128)} async-done(((f32[512,896]{1,0:T(8,128)}), f32[16,896]{1,0:T(8,128)}) %reduce-scatter.18.cloned.1.call-update) | async-done | bytes 57360 | tf_op jit(solution)/shard_map/reduce_scatter | solution.py:442
  2210.6 131.4 %scatter_custom_fusion.2 = f32[56,151936]{0,1:T(8,128)} fusion(s32[8192]{0:T(1024)} %get-tuple-element.482, f32[]{:T(128)} %constant.223.clone.1, f32[8192,56]{1,0:T(8,128)} %copy.254, s32[8192]{0:T(1024)} %broadcast_clamp_fusion), kind=kCustom, calls=%fused_computation.19 | custom fusion | flops 458752 | bytes 34034176 | tf_op jit(solution)/shard_map/scatter-add | solution.py:462
  2380.5 327.7 %copy.305 = bf16[1,56,151936]{1,0,2:T(2,128)(2,1)} copy(bf16[1,56,151936]{1,2,0:T(8,128)(2,1)} %convert_bitcast_fusion) | data formatting | bytes 34033664 | tf_op jit(solution)/shard_map/convert_element_type | solution.py:465
  2708.7 823.1 %reduce.4 = bf16[151936,56]{1,0:T(8,128)(2,1)} reduce(bf16[151936,1,56]{2,1,0:T(2,128)(2,1)} %bitcast.331, bf16[]{:T(256)} %broadcast.670), dimensions={1}, to_apply=%bitcast.331.reduce_sub_computation | reduce | bytes 34033664
  3531.8 71.7 %reshape.800 = bf16[32,2,132944]{2,1,0:T(2,128)(2,1)} reshape(bf16[151936,56]{1,0:T(8,128)(2,1)} %reduce.4) | data formatting | bytes 34033664
  3661.3 1308.5 %fusion.149 = (f32[32,1152]{1,0:T(8,128)S(1)}, f32[32,896]{1,0:T(8,128)S(1)}, f32[32,9728]{1,0:T(8,128)S(1)}) fusion(f32[896,1152]{1,0:T(8,128)} %convolution_add_fusion.2, f32[896,896]{1,0:T(8,128)} %convolution_add_fusion.5, f32[896,9728]{1,0:T(8,128)} %convolution_add_fusion), kind=kCustom, calls=%all-reduce-scatter.3 | all-reduce-scatter fusion | flops 12058625 | bytes 43712512
  5046.8 55.4 collective-permute-done.1
  5136.1 40.5 all-reduce.6
  5224.4 86.3 %reshape.801 = bf16[151936,1,56]{2,1,0:T(2,128)(2,1)} reshape(bf16[32,2,132944]{2,1,0:T(2,128)(2,1)} %all-to-all-done.3) | data formatting | bytes 34033664
  5310.7 142.3 %copy.256 = bf16[1,56,151936]{2,1,0:T(8,128)(2,1)} copy(bf16[1,56,151936]{1,0,2:T(2,128)(2,1)} %bitcast.277) | data formatting | bytes 34033664 | tf_op jit(solution)/shard_map/all_to_all | solution.py:464
  5609.5 44.7 fusion.150
  (882 shorter events, 1096.9 us)
Async XLA Ops:
  7.2 613.9 %all-gather.39.cloned.1.call-start = ((), (), s32[]{:S(2)}) async-start(), calls=%async_computation.21 | async-start | bytes 1892352 | tf_op jit(solution)/shard_map/all_gather | solution.py:334
  8.8 612.3 %all-gather.41.cloned.1.call-start = ((), (), s32[]{:S(2)}) async-start(), calls=%async_computation.22 | async-start | bytes 1892352 | tf_op jit(solution)/shard_map/all_gather | solution.py:339
  9.5 617.0 %all-gather.35.cloned.1.call-start = ((), (), s32[]{:S(2)}) async-start(), calls=%async_computation.19 | async-start | bytes 2433024 | tf_op jit(solution)/shard_map/all_gather | solution.py:333
  11.2 615.4 %all-gather.37.cloned.1.call-start = ((), (), s32[]{:S(2)}) async-start(), calls=%async_computation.20 | async-start | bytes 2433024 | tf_op jit(solution)/shard_map/all_gather | solution.py:338
  11.8 622.1 %all-gather.31.cloned.1.call-start = ((), (), s32[]{:S(2)}) async-start(), calls=%async_computation.11 | async-start | bytes 8988672 | tf_op jit(solution)/shard_map/all_gather | solution.py:336
  13.6 631.3 %all-gather.33.cloned.1.call-start = ((), (), s32[]{:S(2)}) async-start(), calls=%async_computation.12 | async-start | bytes 8988672 | tf_op jit(solution)/shard_map/all_gather | solution.py:341
  14.2 842.6 %all-gather.43.cloned.1.call-start = ((), (), s32[]{:S(2)}) async-start(), calls=%async_computation.23 | async-start | bytes 20545536 | tf_op jit(solution)/shard_map/all_gather | solution.py:335
  16.4 907.5 %all-gather.45.cloned.1.call-start = ((), (), s32[]{:S(2)}) async-start(), calls=%async_computation.24 | async-start | bytes 20545536 | tf_op jit(solution)/shard_map/all_gather | solution.py:340
  58.6 593.7 %all-to-all-start = ((bf16[32,56,4748]{2,1,0:T(8,128)(2,1)}), bf16[32,56,4748]{2,1,0:T(8,128)(2,1)}, u32[]{:S(2)}, u32[]{:S(2)}) async-start(bf16[32,56,4748]{2,1,0:T(8,128)(2,1)} %bitcast.357), calls=%async_computation | async-start | bytes 34865152 | tf_op jit(solution)/shard_map/all_to_all | solution.py:351
  852.0 108.4 %all-to-all-start.1 = ((bf16[56,2,16,256]{3,0,1,2:T(8,128)(2,1)}), bf16[56,2,16,256]{3,0,1,2:T(8,128)(2,1)S(1)}, u32[]{:S(2)}, u32[]{:S(2)}) async-start(bf16[56,2,16,256]{3,0,1,2:T(8,128)(2,1)} %broadcast_select_fusion.4), calls=%async_computation.1 | async-start | bytes 1835008 | tf_op jit(solution)/shard_map/all_to_all | solution.py:370
  856.3 980.8 %reduce-scatter.24.cloned.1.call-start = ((), (), s32[]{:S(2)}) async-start(), calls=%async_computation.16 | async-start | bytes 1892352 | tf_op jit(solution)/shard_map/reduce_scatter | solution.py:442
  1701.8 273.4 %reduce-scatter.18.cloned.1.call-start = ((), (), s32[]{:S(2)}) async-start(), calls=%async_computation.13 | async-start | bytes 1892352 | tf_op jit(solution)/shard_map/reduce_scatter | solution.py:442
  1712.8 406.3 %reduce-scatter.26.cloned.1.call-start = ((), (), s32[]{:S(2)}) async-start(), calls=%async_computation.17 | async-start | bytes 327680 | tf_op jit(solution)/shard_map/reduce_scatter | solution.py:253
  2098.8 46.0 reduce-scatter.28.cloned.1.call-start
  2106.2 61.2 %reduce-scatter.22.cloned.1.call-start = ((), (), s32[]{:S(2)}) async-start(), calls=%async_computation.15 | async-start | bytes 327680 | tf_op jit(solution)/shard_map/reduce_scatter | solution.py:256
  2178.8 3043.2 %reduce-scatter.30.cloned.1.call-start = ((), (), s32[]{:S(2)}) async-start(), calls=%async_computation.25 | async-start | bytes 17977344
  3603.5 1620.8 %all-to-all-start.3 = ((bf16[32,2,132944]{2,1,0:T(2,128)(2,1)}), bf16[32,2,132944]{2,1,0:T(2,128)(2,1)}, u32[]{:S(2)}, u32[]{:S(2)}) async-start(bf16[32,2,132944]{2,1,0:T(2,128)(2,1)} %reshape.800), calls=%async_computation.9 | async-start | bytes 34045952 | tf_op jit(solution)/shard_map/all_to_all | solution.py:464
  4969.8 46.0 collective-permute-start.6
  5015.7 171.8 %collective-permute-start.10 = (f32[32,9728]{1,0:T(8,128)S(1)}, f32[32,9728]{1,0:T(8,128)}, u32[]{:S(2)}, u32[]{:S(2)}) collective-permute-start(f32[32,9728]{1,0:T(8,128)S(1)} %get-tuple-element.541), channel_id=1, source_target_pairs={{0,3},{1,4},{2,5},{3,6},{4,7},{5,8},{6,9},{7,10},{8,11},{9,12},{10... | collective-permute-start | bytes 3735560
  5018.4 169.1 %collective-permute-start.9 = (f32[32,9728]{1,0:T(8,128)S(1)}, f32[32,9728]{1,0:T(8,128)}, u32[]{:S(2)}, u32[]{:S(2)}) collective-permute-start(f32[32,9728]{1,0:T(8,128)S(1)} %get-tuple-element.541), channel_id=1, source_target_pairs={{0,2},{1,3},{2,4},{3,5},{4,6},{5,7},{6,8},{7,9},{8,10},{9,11},{10,... | collective-permute-start | bytes 3735560
  5024.8 162.7 %collective-permute-start.8 = (f32[32,9728]{1,0:T(8,128)S(1)}, f32[32,9728]{1,0:T(8,128)}, u32[]{:S(2)}, u32[]{:S(2)}) collective-permute-start(f32[32,9728]{1,0:T(8,128)S(1)} %get-tuple-element.541), channel_id=1, source_target_pairs={{0,1},{1,2},{2,3},{3,4},{4,5},{5,6},{6,7},{7,8},{8,9},{9,10},{10,1... | collective-permute-start | bytes 3735560
  5027.5 160.0 %collective-permute-start.11 = (f32[28,9728]{1,0:T(8,128)}, f32[28,9728]{1,0:T(8,128)}, u32[]{:S(2)}, u32[]{:S(2)}) collective-permute-start(f32[28,9728]{1,0:T(8,128)} %slice.364), channel_id=1, source_target_pairs={{0,4},{1,5},{2,6},{3,7},{4,8},{5,9},{6,10},{7,11},{8,12},{9,13},{1... | collective-permute-start | bytes 3268616
  5031.3 70.9 %collective-permute-start.1 = (f32[32,1152]{1,0:T(8,128)S(1)}, f32[32,1152]{1,0:T(8,128)S(1)}, u32[]{:S(2)}, u32[]{:S(2)}) collective-permute-start(f32[32,1152]{1,0:T(8,128)S(1)} %get-tuple-element.539), channel_id=1, source_target_pairs={{0,2},{1,3},{2,4},{3,5},{4,6},{5,7},{6,8},{7,9},{8,10},{9,11},{10,... | collective-permute-start | bytes 442376
  5102.2 79.9 %collective-permute-start = (f32[32,1152]{1,0:T(8,128)S(1)}, f32[32,1152]{1,0:T(8,128)S(1)}, u32[]{:S(2)}, u32[]{:S(2)}) collective-permute-start(f32[32,1152]{1,0:T(8,128)S(1)} %get-tuple-element.539), channel_id=1, source_target_pairs={{0,1},{1,2},{2,3},{3,4},{4,5},{5,6},{6,7},{7,8},{8,9},{9,10},{10,1... | collective-permute-start | bytes 442376
  (160 other events, 15140.6 us)
Sparse Core Ops, SparseCore 0:
  11.4 58.4 all-gather.38
  72.8 178.0 all-gather.40
  254.4 143.2 all-gather.34
  400.4 83.5 all-gather.36
  487.3 77.3 all-gather.30
  567.4 77.4 all-gather.32
  648.3 128.2 all-gather.42
  779.4 144.5 all-gather.44
  1702.0 135.0 reduce-scatter.23
  1839.8 135.3 reduce-scatter.17
  2081.7 17.4 reduce-scatter.25
  2102.2 20.0 reduce-scatter.19
  2124.8 19.9 reduce-scatter.27
  2147.3 20.0 reduce-scatter.21
  2194.4 382.3 reduce-scatter.29
where the time goes:
time: 5680 us; the launch traced here: 5660 us
  blocking collectives  2480 us (44%)
  other arithmetic  1210 us (21%)
  local copies, waits for them, and re-layouts  1060 us (19%)
  waiting for transfers between devices  439 us (8%)
  matrix products  327 us (6%)
  starting transfers between devices  117 us (2%)
    unnamed x2, blocking collectives  1350 us
    unnamed x10, other arithmetic  828 us
    all_gather x1, blocking collectives, body(): lax.all_gather(small_params.astype(bf16), ('half', 'mp', 'batch'), axis=1...  471 us
    all_gather x6, blocking collectives, merged(): everything = jax.tree.map(lambda part: lax.all_gather(part, axis), array)  390 us
    convert_element_type x1, local copies, waits for them, and re-layouts, body(): col_grad[None].astype(jnp.bfloat16)  328 us
    reduce_scatter x2, waiting for transfers between devices, body(): lax.psum_scatter(padded, ('half', 'mp', 'batch'), scatter_dimension=0, ti...  251 us
    unnamed x328, local copies, waits for them, and re-layouts  246 us
    all_gather x2, blocking collectives, body(): lax.all_gather(row_count, ('half', 'mp', 'batch'), axis=0, tiled=True)  146 us
  transfers between devices with their start and end apart: 31, of which 9 were waited for; matrix products, arithmetic and copies ran while one was open for 57% of the time, Pallas kernels for 0%

commit v1 on v0

v1 whole, which is shorter than its diff:
```python
import functools

import jax
import jax.numpy as jnp
from jax import lax
from jax.experimental import pallas as pl
from jax.experimental.pallas import tpu as pltpu
from jax.sharding import PartitionSpec as P

MODEL_WIDTH = 896
QUERY_HEADS = 14
KEY_VALUE_HEADS = 2
HEAD_SIZE = 64
FF = 4864
QKV = 1152
TOK = 256
P_SIZE = 16
MICRO = 2
STEP = 5

EPS_NORM = 1e-06
THETA = 1000000.0
BETA = 0.05
CLIP = 0.1
RATE = 0.03
DECAY = 0.01
MOM1 = 0.5
MOM2 = 0.5
EPS_ADAM = 1e-08

MESH = pl.DeviceIdType.MESH

def places():
    n_mp, n_batch = lax.axis_size("mp"), lax.axis_size("batch")
    return 2, n_mp // 2, n_batch


def coords():
    mp = lax.axis_index("mp")
    return lax.axis_index("half"), mp // 2, lax.rem(mp, 2), lax.axis_index("batch")


def comm_index():
    _, n_y, n_batch = places()
    half, y, core, batch = coords()
    return ((core * 2 + half) * n_y + y) * n_batch + batch


def peers():
    _, n_y, n_batch = places()
    half, y, core, batch = coords()
    line = []
    for k in range(1, n_batch):
        to, frm = lax.rem(batch + k, n_batch), lax.rem(batch + n_batch - k, n_batch)
        line.append(({"half": half, "mp": y * 2 + core, "batch": to}, to, frm))
    plane = []
    n_plane = 2 * n_y
    spot = half * n_y + y
    for k in range(1, n_plane):
        to, frm = lax.rem(spot + k, n_plane), lax.rem(spot + n_plane - k, n_plane)
        plane.append(
            ({"half": to // n_y, "mp": lax.rem(to, n_y) * 2 + core, "batch": batch}, to, frm)
        )
    other = ({"half": half, "mp": y * 2 + (1 - core), "batch": batch}, 1 - core, 1 - core)
    return line, plane, other


def greet(line, plane, other):
    barrier = pltpu.get_barrier_semaphore()
    everyone = line + plane + [other]
    for who, _, _ in everyone:
        pl.semaphore_signal(barrier, inc=1, device_id=who, device_id_type=MESH)
    pl.semaphore_wait(barrier, len(everyone))


def push(src, dst, send_sem, recv_sem, who):
    copy = pltpu.make_async_remote_copy(
        src_ref=src,
        dst_ref=dst,
        send_sem=send_sem,
        recv_sem=recv_sem,
        device_id=who,
        device_id_type=MESH,
    )
    copy.start()
    return copy


def gather_kernel(n_arr, *refs):
    ins, outs = refs[:n_arr], refs[n_arr : 2 * n_arr]
    send_sems, recv_sems, own_sem = refs[2 * n_arr :]
    _, n_y, n_batch = places()
    half, y, core, batch = coords()
    n_plane = 2 * n_y
    spot = half * n_y + y
    line, plane, other = peers()
    greet(line, plane, other)

    def rows(i, first, count):
        size = ins[i].shape[1]
        return outs[i].at[:, pl.ds(pl.multiple_of(first * size, size), count * size), :]

    mine = (core * n_plane + spot) * n_batch + batch
    block = (core * n_plane + spot) * n_batch
    local = []
    for i in range(n_arr):
        copy = pltpu.make_async_copy(ins[i], rows(i, mine, 1), own_sem.at[i])
        copy.start()
        local.append(copy)
    pending = []
    slot = 0
    for i in range(n_arr):
        for who, _, _ in line:
            pending.append(push(ins[i], rows(i, mine, 1), send_sems.at[slot], recv_sems.at[slot], who))
            slot += 1
    for copy in local:
        copy.wait()
    for copy in pending:
        copy.wait()
    pending = []
    for i in range(n_arr):
        for who, _, _ in plane:
            pending.append(
                push(rows(i, block, n_batch), rows(i, block, n_batch), send_sems.at[slot], recv_sems.at[slot], who)
            )
            slot += 1
    last = []
    for i in range(n_arr):
        last.append(
            push(rows(i, block, n_batch), rows(i, block, n_batch), send_sems.at[slot], recv_sems.at[slot], other[0])
        )
        slot += 1
    at = 0
    for i in range(n_arr):
        for _, _, frm in plane:
            pending[at].wait_recv()
            at += 1
            first = (core * n_plane + frm) * n_batch
            last.append(
                push(rows(i, first, n_batch), rows(i, first, n_batch), send_sems.at[slot], recv_sems.at[slot], other[0])
            )
            slot += 1
    for copy in pending:
        copy.wait_send()
    for copy in last:
        copy.wait()


def gather(arrays, cid, vmem=48):
    _, n_y, n_batch = places()
    n_plane = 2 * n_y
    total = 2 * n_plane * n_batch
    n = len(arrays)
    copies = n * ((n_batch - 1) + (n_plane - 1) + n_plane)
    return pl.pallas_call(
        functools.partial(gather_kernel, n),
        out_shape=[jax.ShapeDtypeStruct((a.shape[0], a.shape[1] * total, a.shape[2]), a.dtype) for a in arrays],
        in_specs=[pl.BlockSpec(memory_space=pltpu.VMEM)] * n,
        out_specs=[pl.BlockSpec(memory_space=pltpu.VMEM)] * n,
        scratch_shapes=[
            pltpu.SemaphoreType.DMA((copies,)),
            pltpu.SemaphoreType.DMA((copies,)),
            pltpu.SemaphoreType.DMA((n,)),
        ],
        compiler_params=pltpu.CompilerParams(
            collective_id=cid, has_side_effects=True, vmem_limit_bytes=vmem * 2**20
        ),
        name=f"gather_{cid}",
    )(*arrays)


def reduce_kernel(n_arr, *refs):
    ins, outs = refs[:n_arr], refs[n_arr : 2 * n_arr]
    scr = refs[2 * n_arr : 7 * n_arr]
    send_sems, recv_sems = refs[7 * n_arr :]
    _, n_y, n_batch = places()
    half, y, core, batch = coords()
    n_plane = 2 * n_y
    spot = half * n_y + y
    line, plane, other = peers()
    greet(line, plane, other)
    f32 = jnp.float32
    slot = 0
    first = []
    for i in range(n_arr):
        core_in = scr[5 * i]
        size = core_in.shape[1]
        src = ins[i].at[:, pl.ds(pl.multiple_of((1 - core) * size, size), size), :]
        first.append(push(src, core_in, send_sems.at[slot], recv_sems.at[slot], other[0]))
        slot += 1
    pending = []
    for i in range(n_arr):
        core_in, core_sum, plane_in, plane_sum, line_in = scr[5 * i : 5 * i + 5]
        size = core_in.shape[1]
        part = plane_sum.shape[1]
        first[i].wait_recv()
        for k, (who, to, _) in enumerate(plane):
            at = pl.multiple_of(to * part, part)
            here = pl.multiple_of(core * size + to * part, part)
            core_sum[:, pl.ds(at, part), :] = (
                ins[i][:, pl.ds(here, part), :].astype(f32) + core_in[:, pl.ds(at, part), :].astype(f32)
            ).astype(core_sum.dtype)
            pending.append(
                push(core_sum.at[:, pl.ds(at, part), :], plane_in.at[k], send_sems.at[slot], recv_sems.at[slot], who)
            )
            slot += 1
    second = []
    at_copy = 0
    for i in range(n_arr):
        core_in, core_sum, plane_in, plane_sum, line_in = scr[5 * i : 5 * i + 5]
        size = core_in.shape[1]
        part = plane_sum.shape[1]
        row = line_in.shape[2]
        at = pl.multiple_of(spot * part, part)
        here = pl.multiple_of(core * size + spot * part, part)
        total = ins[i][:, pl.ds(here, part), :].astype(f32) + core_in[:, pl.ds(at, part), :].astype(f32)
        for k in range(len(plane)):
            pending[at_copy].wait_recv()
            at_copy += 1
            total = total + plane_in[k].astype(f32)
        plane_sum[...] = total.astype(plane_sum.dtype)
        for k, (who, to, _) in enumerate(line):
            src = plane_sum.at[:, pl.ds(pl.multiple_of(to * row, row), row), :]
            second.append(push(src, line_in.at[k], send_sems.at[slot], recv_sems.at[slot], who))
            slot += 1
    at_copy = 0
    for i in range(n_arr):
        core_in, core_sum, plane_in, plane_sum, line_in = scr[5 * i : 5 * i + 5]
        row = line_in.shape[2]
        total = plane_sum[:, pl.ds(pl.multiple_of(batch * row, row), row), :].astype(f32)
        for k in range(len(line)):
            second[at_copy].wait_recv()
            at_copy += 1
            total = total + line_in[k].astype(f32)
        outs[i][...] = total
    for copy in first + pending + second:
        copy.wait_send()


def reduce(arrays, cid, vmem=48):
    _, n_y, n_batch = places()
    n_plane = 2 * n_y
    total = 2 * n_plane * n_batch
    n = len(arrays)
    copies = n * (1 + (n_plane - 1) + (n_batch - 1))
    scratch = []
    for a in arrays:
        m, rows, w = a.shape
        scratch += [
            pltpu.VMEM((m, rows // 2, w), a.dtype),
            pltpu.VMEM((m, rows // 2, w), a.dtype),
            pltpu.VMEM((n_plane - 1, m, rows // (2 * n_plane), w), a.dtype),
            pltpu.VMEM((m, rows // (2 * n_plane), w), a.dtype),
            pltpu.VMEM((n_batch - 1, m, rows // total, w), a.dtype),
        ]
    return pl.pallas_call(
        functools.partial(reduce_kernel, n),
        out_shape=[jax.ShapeDtypeStruct((a.shape[0], a.shape[1] // total, a.shape[2]), jnp.float32) for a in arrays],
        in_specs=[pl.BlockSpec(memory_space=pltpu.VMEM)] * n,
        out_specs=[pl.BlockSpec(memory_space=pltpu.VMEM)] * n,
        scratch_shapes=scratch
        + [pltpu.SemaphoreType.DMA((copies,)), pltpu.SemaphoreType.DMA((copies,))],
        compiler_params=pltpu.CompilerParams(
            collective_id=cid, has_side_effects=True, vmem_limit_bytes=vmem * 2**20
        ),
        name=f"reduce_{cid}",
    )(*arrays)


HEAD_SLOTS = (0, 2, 4, 6, 1, 3, 5, 8, 10, 12, 7, 9, 11, 13)
COMBOS = ((0, 4, 0), (0, 3, 4), (4, 7, 7), (3, 7, 10))
PAIRS = QUERY_HEADS // 2
TILE = 128


def column(vector):
    return jnp.transpose(jnp.broadcast_to(vector.astype(jnp.float32), (128, 128)))


def last_last(a, b):
    return lax.dot_general(a, b, (((1,), (1,)), ((), ())), preferred_element_type=jnp.float32)


def first_first(a, b):
    return lax.dot_general(a, b, (((0,), (0,)), ((), ())), preferred_element_type=jnp.float32)


def straight(a, b):
    return jnp.dot(a, b, preferred_element_type=jnp.float32)


def lookup_kernel(
    block, span, n_ref, table_ref, frozen_ref, rows_ref, flat_ref, frow_ref,
    low_ref, picked_ref, x_ref, held, staged, sem,
):
    step = pl.program_id(0)
    f32, bf16 = jnp.float32, jnp.bfloat16
    inside = step * span + lax.broadcasted_iota(jnp.int32, (span, 1), 0) < block
    low = jnp.where(inside, table_ref[...], 0.0).astype(bf16)
    low_ref[...] = low
    at = pl.multiple_of(step * span, span)
    held[0, pl.ds(at, span), :] = low
    held[1, pl.ds(at, span), :] = jnp.where(inside, frozen_ref[...].astype(f32), 0.0).astype(bf16)

    @pl.when(step == pl.num_programs(0) - 1)
    def _():
        picked_ref[...] = jnp.zeros_like(picked_ref)
        n_rows = frow_ref.shape[0]
        n_span = held.shape[1] // span

        def tile(i, _):
            wanted = column(rows_ref[pl.ds(i, 1), :])
            match = (
                frow_ref[...].astype(f32) == jnp.broadcast_to(flat_ref[pl.ds(i, 1), :].astype(f32), (n_rows, TILE))
            )
            match = jnp.where(match, 1.0, 0.0).astype(bf16)
            wide = jnp.concatenate([wanted] * (span // 128), axis=1)
            lanes = lax.broadcasted_iota(jnp.int32, (TILE, span), 1).astype(f32)
            for model in range(2):

                def part(k, total):
                    first = pl.multiple_of(k * span, span)
                    hot = jnp.where(wide == lanes + (k * span).astype(f32), 1.0, 0.0).astype(bf16)
                    return total + straight(hot, held[model, pl.ds(first, span), :])

                found = lax.fori_loop(0, n_span, part, jnp.zeros((TILE, table_ref.shape[1]), f32)).astype(bf16)
                staged[model] = found
                picked_ref[model] = picked_ref[model] + straight(match, found).astype(bf16)
            copy = pltpu.make_async_copy(staged, x_ref.at[:, pl.ds(pl.multiple_of(i * TILE, TILE), TILE), :], sem)
            copy.start()
            copy.wait()
            return 0

        lax.fori_loop(0, (n_ref[0] + TILE - 1) // TILE, tile, 0)


def lookup(n_local, table, frozen, rows, flat, frow):
    block, width = table.shape
    span = 512
    steps = pl.cdiv(block, span)
    cap = rows.shape[0] * 128
    n_rows = frow.shape[0]
    bf16 = jnp.bfloat16
    whole = lambda shape: pl.BlockSpec(shape, lambda i: (0,) * len(shape))
    return pl.pallas_call(
        functools.partial(lookup_kernel, block, span),
        grid=(steps,),
        out_shape=[
            jax.ShapeDtypeStruct((block, width), bf16),
            jax.ShapeDtypeStruct((2, n_rows, width), bf16),
            jax.ShapeDtypeStruct((2, cap, width), bf16),
        ],
        in_specs=[
            pl.BlockSpec(memory_space=pltpu.SMEM),
            pl.BlockSpec((span, width), lambda i: (i, 0)),
            pl.BlockSpec((span, width), lambda i: (i, 0)),
            whole(rows.shape),
            whole(flat.shape),
            whole(frow.shape),
        ],
        out_specs=[
            pl.BlockSpec((span, width), lambda i: (i, 0)),
            whole((2, n_rows, width)),
            pl.BlockSpec(memory_space=pl.ANY),
        ],
        scratch_shapes=[
            pltpu.VMEM((2, steps * span, width), bf16),
            pltpu.VMEM((2, TILE, width), bf16),
            pltpu.SemaphoreType.DMA,
        ],
        compiler_params=pltpu.CompilerParams(vmem_limit_bytes=56 * 2**20),
        name="lookup",
    )(n_local, table, frozen, rows, flat, frow)


def head_pieces(both, lane):
    turned = pltpu.roll(both, 64, 1)
    low, high = lane < 64, lane >= 64
    bf16 = jnp.bfloat16
    zero = jnp.zeros_like(both)
    return (
        jnp.where(low, both, zero).astype(bf16),
        jnp.where(high, turned, zero).astype(bf16),
        jnp.where(low, turned, zero).astype(bf16),
        jnp.where(high, both, zero).astype(bf16),
    )


def turn(values, positions, freq, lane, sign):
    angle = positions * freq
    cosine, sine = jnp.cos(angle), jnp.sin(angle)
    first = lax.rem(lane, 64) < 32
    mixed = jnp.where(first, -sign * pltpu.roll(values, 96, 1), sign * pltpu.roll(values, 32, 1))
    return values * cosine + mixed * sine


def allowed_of(frow, flat, r, length):
    flat = jnp.broadcast_to(flat, frow.shape)
    return jnp.where((flat <= frow) & (flat >= r * length), 1.0, 0.0)


def attend_kernel(
    length, rp, n_ref, lo_ref, hi_ref, q_ref, x_ref, w_ref, gain_ref, bias_ref, freq_ref, frow_ref, flat_ref, pos_ref,
    o_ref, m_ref, l_ref, kv_ref, xbuf, kvbuf, m_scr, l_scr, o_scr, sem,
):
    model = pl.program_id(0)
    f32, bf16 = jnp.float32, jnp.bfloat16
    lane = lax.broadcasted_iota(jnp.int32, (TILE, 128), 1)
    lane_r = lax.broadcasted_iota(jnp.int32, (rp, 128), 1)
    m_scr[...] = jnp.full(m_scr.shape, -1e30, f32)
    l_scr[...] = jnp.zeros_like(l_scr)
    o_scr[...] = jnp.zeros_like(o_scr)

    def tile(i, _):
        at = pl.ds(pl.multiple_of(i * TILE, TILE), TILE)
        copy = pltpu.make_async_copy(x_ref.at[model, at, :], xbuf, sem.at[0])
        copy.start()
        copy.wait()
        x = xbuf[...].astype(f32)
        scale = lax.rsqrt(jnp.mean(x * x, axis=-1, keepdims=True) + EPS_NORM)
        normed = (x * scale * gain_ref[0]).astype(bf16)
        mixed = straight(normed, w_ref[0]) + bias_ref[0]
        key = turn(mixed[:, :128], column(pos_ref[pl.ds(i, 1), :]), freq_ref[...], lane, 1.0)
        key = key.astype(bf16)
        value = mixed[:, 128:].astype(bf16)
        kvbuf[...] = jnp.concatenate([key, value], axis=1)
        out = pltpu.make_async_copy(kvbuf, kv_ref.at[model, at, :], sem.at[1])
        out.start()
        keys = head_pieces(key.astype(f32), lane)
        values = head_pieces(value.astype(f32), lane)
        flat = flat_ref[pl.ds(i, 1), :]

        def rollout(r, _):
            rows = pl.ds(pl.multiple_of(r * rp, rp), rp)
            ok = allowed_of(frow_ref[rows, :], flat, r, length)[None]
            shift = (ok - 1.0) * 1e30
            alphas, adds = {}, {}
            for c, (p0, p1, s0) in enumerate(COMBOS):
                n = p1 - p0
                query = q_ref[p0:p1, rows, :].reshape(n * rp, 128)
                score = last_last(query, keys[c]).reshape(n, rp, TILE) * HEAD_SIZE ** (-0.5)
                score = score * ok + shift
                old = m_scr[s0 : s0 + n, rows, :]
                new = jnp.maximum(old, jnp.max(score, axis=-1, keepdims=True))
                m_scr[s0 : s0 + n, rows, :] = new
                alpha = jnp.exp(old - new)
                prob = jnp.exp(score - new) * ok
                l_scr[s0 : s0 + n, rows, :] = l_scr[s0 : s0 + n, rows, :] * alpha + jnp.sum(prob, axis=-1, keepdims=True)
                add = straight(prob.astype(bf16).reshape(n * rp, TILE), values[c]).reshape(n, rp, 128)
                for k in range(n):
                    alphas[p0 + k, c % 2] = alpha[k]
                    adds[p0 + k, c % 2] = add[k]
            for p in range(PAIRS):
                both = jnp.where(lane_r < 64, alphas[p, 0], alphas[p, 1])
                o_scr[p, rows, :] = o_scr[p, rows, :] * both + adds[p, 0] + adds[p, 1]
            return 0

        lax.fori_loop(lo_ref[i], hi_ref[i] + 1, rollout, 0)
        out.wait()
        return 0

    lax.fori_loop(0, (n_ref[0] + TILE - 1) // TILE, tile, 0)
    o_ref[...] = o_scr[...].astype(bf16)
    n_rows = m_scr.shape[1]
    lanes = lax.broadcasted_iota(jnp.int32, (n_rows, 128), 1)
    tops = jnp.full((n_rows, 128), -1e30, f32)
    totals = jnp.zeros((n_rows, 128), f32)
    for slot, head in enumerate(HEAD_SLOTS):
        tops = jnp.where(lanes == head, m_scr[slot], tops)
        totals = jnp.where(lanes == head, l_scr[slot], totals)
    m_ref[0] = tops
    l_ref[0] = totals


def attend(n_local, lo, hi, q, x, w, gain, bias, freq, frow, flat, pos, length, rp):
    n_rows = q.shape[1]
    width = x.shape[2]
    cap = x.shape[1]
    bf16 = jnp.bfloat16
    whole = lambda shape: pl.BlockSpec(shape, lambda i: (0,) * len(shape))
    smem = pl.BlockSpec(memory_space=pltpu.SMEM)
    anyw = pl.BlockSpec(memory_space=pl.ANY)
    model = lambda shape: pl.BlockSpec(shape, lambda i: (i, 0, 0))
    return pl.pallas_call(
        functools.partial(attend_kernel, length, rp),
        grid=(2,),
        out_shape=[
            jax.ShapeDtypeStruct((2 * PAIRS, n_rows, 128), bf16),
            jax.ShapeDtypeStruct((2, n_rows, 128), jnp.float32),
            jax.ShapeDtypeStruct((2, n_rows, 128), jnp.float32),
            jax.ShapeDtypeStruct((2, cap, 256), bf16),
        ],
        in_specs=[
            smem, smem, smem, model((PAIRS, n_rows, 128)), anyw, model((1, width, 256)), model((1, 1, width)),
            model((1, 1, 256)), whole((1, 128)), whole(frow.shape), whole(flat.shape), whole(pos.shape),
        ],
        out_specs=[model((PAIRS, n_rows, 128)), model((1, n_rows, 128)), model((1, n_rows, 128)), anyw],
        scratch_shapes=[
            pltpu.VMEM((TILE, width), bf16),
            pltpu.VMEM((TILE, 256), bf16),
            pltpu.VMEM((QUERY_HEADS, n_rows, 128), jnp.float32),
            pltpu.VMEM((QUERY_HEADS, n_rows, 128), jnp.float32),
            pltpu.VMEM((PAIRS, n_rows, 128), jnp.float32),
            pltpu.SemaphoreType.DMA((2,)),
        ],
        compiler_params=pltpu.CompilerParams(vmem_limit_bytes=60 * 2**20),
        name="attend",
    )(n_local, lo, hi, q, x, w, gain, bias, freq, frow, flat, pos)


def attend_back_kernel(
    length, rp, n_ref, lo_ref, hi_ref, q_ref, do_ref, st_ref, x_ref, kv_ref, w_ref, gain_ref, freq_ref, frow_ref, flat_ref,
    pos_ref, dq_ref, gkv_ref, gs_ref, gb_ref, dx_ref, xbuf, kvbuf, dxbuf, dq_scr, dk_scr, dv_scr, sem,
):
    f32, bf16 = jnp.float32, jnp.bfloat16
    lane = lax.broadcasted_iota(jnp.int32, (TILE, 128), 1)
    dq_scr[...] = jnp.zeros_like(dq_scr)
    gkv_ref[...] = jnp.zeros_like(gkv_ref)
    gs_ref[...] = jnp.zeros_like(gs_ref)
    gb_ref[...] = jnp.zeros_like(gb_ref)

    def tile(i, _):
        at = pl.ds(pl.multiple_of(i * TILE, TILE), TILE)
        one = pltpu.make_async_copy(x_ref.at[0, at, :], xbuf, sem.at[0])
        one.start()
        two = pltpu.make_async_copy(kv_ref.at[0, at, :], kvbuf, sem.at[1])
        two.start()
        one.wait()
        two.wait()
        keys = head_pieces(kvbuf[:, :128].astype(f32), lane)
        values = head_pieces(kvbuf[:, 128:].astype(f32), lane)
        flat = flat_ref[pl.ds(i, 1), :]
        dk_scr[...] = jnp.zeros_like(dk_scr)
        dv_scr[...] = jnp.zeros_like(dv_scr)

        def rollout(r, _):
            rows = pl.ds(pl.multiple_of(r * rp, rp), rp)
            ok = allowed_of(frow_ref[rows, :], flat, r, length)[None]
            shift = (ok - 1.0) * 1e30
            stats = st_ref[rows, :]
            adds = {}
            for c, (p0, p1, s0) in enumerate(COMBOS):
                n = p1 - p0
                heads = HEAD_SLOTS[s0 : s0 + n]
                query = q_ref[p0:p1, rows, :].reshape(n * rp, 128)
                back = do_ref[p0:p1, rows, :].reshape(n * rp, 128)
                lse = jnp.stack([stats[:, h : h + 1] for h in heads])
                delta = jnp.stack([stats[:, 16 + h : 17 + h] for h in heads])
                score = last_last(query, keys[c]).reshape(n, rp, TILE) * HEAD_SIZE ** (-0.5)
                prob = jnp.exp(score * ok + shift - lse)
                d_prob = last_last(back, values[c]).reshape(n, rp, TILE)
                d_score = (prob * (d_prob - delta)).astype(bf16).reshape(n * rp, TILE)
                add = straight(d_score, keys[c]).reshape(n, rp, 128)
                dk_scr[c] += first_first(d_score, query)
                dv_scr[c] += first_first(prob.astype(bf16).reshape(n * rp, TILE), back)
                for k in range(n):
                    adds[p0 + k, c % 2] = add[k]
            for p in range(PAIRS):
                dq_scr[p, rows, :] = dq_scr[p, rows, :] + adds[p, 0] + adds[p, 1]
            return 0

        lax.fori_loop(lo_ref[i], hi_ref[i] + 1, rollout, 0)

        def joined(scr):
            return jnp.where(lane < 64, scr[0] + pltpu.roll(scr[1], 64, 1), scr[3] + pltpu.roll(scr[2], 64, 1))

        d_key = turn(joined(dk_scr) * HEAD_SIZE ** (-0.5), column(pos_ref[pl.ds(i, 1), :]), freq_ref[...], lane, -1.0)
        d_mixed = jnp.concatenate([d_key, joined(dv_scr)], axis=1).astype(bf16)
        x = xbuf[...].astype(f32)
        scale = lax.rsqrt(jnp.mean(x * x, axis=-1, keepdims=True) + EPS_NORM)
        gain = gain_ref[0]
        normed = (x * scale * gain).astype(bf16)
        gkv_ref[...] += first_first(normed, d_mixed)
        gb_ref[...] += jnp.sum(d_mixed.astype(f32).reshape(TILE // 8, 8, 256), axis=0)
        d_normed = last_last(d_mixed, w_ref[0])
        gs_ref[...] += jnp.sum((d_normed * x * scale).reshape(TILE // 8, 8, x.shape[1]), axis=0)
        d_hat = d_normed * gain
        d_x = scale * (d_hat - x * scale * scale * jnp.mean(d_hat * x, axis=-1, keepdims=True))
        dxbuf[...] = d_x.astype(bf16)
        out = pltpu.make_async_copy(dxbuf, dx_ref.at[at, :], sem.at[2])
        out.start()
        out.wait()
        return 0

    lax.fori_loop(0, (n_ref[0] + TILE - 1) // TILE, tile, 0)
    dq_ref[...] = (dq_scr[...] * HEAD_SIZE ** (-0.5)).astype(bf16)


def attend_back(n_local, lo, hi, q, do, stats, x, kv, w, gain, freq, frow, flat, pos, length, rp):
    n_rows = q.shape[1]
    width = x.shape[2]
    cap = x.shape[1]
    bf16, f32 = jnp.bfloat16, jnp.float32
    whole = lambda shape: pl.BlockSpec(shape, lambda i: (0,) * len(shape))
    smem = pl.BlockSpec(memory_space=pltpu.SMEM)
    anyw = pl.BlockSpec(memory_space=pl.ANY)
    return pl.pallas_call(
        functools.partial(attend_back_kernel, length, rp),
        grid=(1,),
        out_shape=[
            jax.ShapeDtypeStruct((PAIRS, n_rows, 128), bf16),
            jax.ShapeDtypeStruct((width, 256), f32),
            jax.ShapeDtypeStruct((8, width), f32),
            jax.ShapeDtypeStruct((8, 256), f32),
            jax.ShapeDtypeStruct((cap, width), bf16),
        ],
        in_specs=[
            smem, smem, smem, whole((PAIRS, n_rows, 128)), whole((PAIRS, n_rows, 128)), whole((n_rows, 128)), anyw, anyw,
            whole((1, width, 256)), whole((1, 1, width)), whole((1, 128)), whole(frow.shape), whole(flat.shape),
            whole(pos.shape),
        ],
        out_specs=[
            whole((PAIRS, n_rows, 128)), whole((width, 256)), whole((8, width)), whole((8, 256)), anyw,
        ],
        scratch_shapes=[
            pltpu.VMEM((TILE, width), bf16),
            pltpu.VMEM((TILE, 256), bf16),
            pltpu.VMEM((TILE, width), bf16),
            pltpu.VMEM((PAIRS, n_rows, 128), f32),
            pltpu.VMEM((4, TILE, 128), f32),
            pltpu.VMEM((4, TILE, 128), f32),
            pltpu.SemaphoreType.DMA((3,)),
        ],
        compiler_params=pltpu.CompilerParams(vmem_limit_bytes=60 * 2**20),
        name="attend_back",
    )(n_local, lo, hi, q, do, stats, x, kv, w, gain, freq, frow, flat, pos)


def table_grad_kernel(
    block, span, kept, n_ref, dl_ref, af_ref, dxs_ref, srow_ref, rows_ref, dx_ref, g_ref, sq_ref, cache, extra, sem,
):
    step = pl.program_id(0)
    f32, bf16 = jnp.float32, jnp.bfloat16
    tiles = (n_ref[0] + TILE - 1) // TILE

    @pl.when(step == 0)
    def _():
        sq_ref[...] = jnp.zeros_like(sq_ref)

        def load(i, _):
            at = pl.ds(pl.multiple_of(i * TILE, TILE), TILE)
            copy = pltpu.make_async_copy(dx_ref.at[at, :], cache.at[at, :], sem)
            copy.start()
            copy.wait()
            return 0

        lax.fori_loop(0, jnp.minimum(tiles, kept), load, 0)

    inside = step * span + lax.broadcasted_iota(jnp.int32, (span, 1), 0) < block
    row = step * span + lax.broadcasted_iota(jnp.int32, (span, dxs_ref.shape[0]), 0)
    total = straight(jnp.where(inside, dl_ref[...].astype(f32), 0.0).astype(bf16), af_ref[...])
    hot = jnp.where(row == srow_ref[...], 1.0, 0.0).astype(bf16)
    total = total + straight(hot, dxs_ref[...])
    g_ref[...] = total
    near = step * span + lax.broadcasted_iota(jnp.int32, (span, TILE), 0)

    def tile(i, _):
        at = pl.ds(pl.multiple_of(i * TILE, TILE), TILE)
        hit = jnp.where(near == rows_ref[pl.ds(i, 1), :], 1.0, 0.0).astype(bf16)
        g_ref[...] += straight(hit, cache[at, :])
        return 0

    lax.fori_loop(0, jnp.minimum(tiles, kept), tile, 0)

    def far(i, _):
        at = pl.ds(pl.multiple_of(i * TILE, TILE), TILE)
        copy = pltpu.make_async_copy(dx_ref.at[at, :], extra, sem)
        copy.start()
        copy.wait()
        hit = jnp.where(near == rows_ref[pl.ds(i, 1), :], 1.0, 0.0).astype(bf16)
        g_ref[...] += straight(hit, extra[...])
        return 0

    lax.fori_loop(kept, tiles, far, 0)
    square = g_ref[...] * g_ref[...]
    sq_ref[...] += jnp.sum(square.reshape(span // 8, 8, square.shape[1]), axis=0)


def table_grad(n_local, dl, af, dxs, srow, rows, dx, block):
    width = af.shape[1]
    n_rows = af.shape[0]
    span = 512
    kept = min(rows.shape[0], 64)
    whole = lambda shape: pl.BlockSpec(shape, lambda i: (0,) * len(shape))
    return pl.pallas_call(
        functools.partial(table_grad_kernel, block, span, kept),
        grid=(pl.cdiv(block, span),),
        out_shape=[
            jax.ShapeDtypeStruct((block, width), jnp.float32),
            jax.ShapeDtypeStruct((8, width), jnp.float32),
        ],
        in_specs=[
            pl.BlockSpec(memory_space=pltpu.SMEM),
            pl.BlockSpec((span, n_rows), lambda i: (i, 0)),
            whole(af.shape), whole(dxs.shape), whole(srow.shape), whole(rows.shape),
            pl.BlockSpec(memory_space=pl.ANY),
        ],
        out_specs=[pl.BlockSpec((span, width), lambda i: (i, 0)), whole((8, width))],
        scratch_shapes=[
            pltpu.VMEM((kept * TILE, width), jnp.bfloat16),
            pltpu.VMEM((TILE, width), jnp.bfloat16),
            pltpu.SemaphoreType.DMA,
        ],
        compiler_params=pltpu.CompilerParams(vmem_limit_bytes=56 * 2**20),
        name="table_grad",
    )(n_local, dl, af, dxs, srow, rows, dx)


def blend(parts, lane):
    f32 = jnp.float32
    top = parts[0][1]
    for p in parts[1:]:
        top = jnp.maximum(top, p[1])
    weights = [jnp.exp(p[1] - top) for p in parts]
    total = sum(p[2] * w for p, w in zip(parts, weights))
    n_models = top.shape[0]
    planes = []
    for model in range(n_models):
        for pair in range(PAIRS):
            acc = None
            for p, w in zip(parts, weights):
                each = jnp.where(
                    lane < 64, w[model][:, 2 * pair : 2 * pair + 1], w[model][:, 2 * pair + 1 : 2 * pair + 2]
                )
                term = p[0][model * PAIRS + pair].astype(f32) * each
                acc = term if acc is None else acc + term
            planes.append(acc)
    return planes, top, total


def mix_kernel(o_ref, m_ref, l_ref, oo_ref, mo_ref, lo_ref, *rest):
    core_o, core_s, sum_o, sum_s, plane_o, plane_s, keep_o, keep_s, line_o, line_s, send_sems, recv_sems = rest
    _, n_y, n_batch = places()
    half, y, core, batch = coords()
    n_plane = 2 * n_y
    spot = half * n_y + y
    line, plane, other = peers()
    greet(line, plane, other)
    size = core_o.shape[1]
    part = keep_o.shape[1]
    row = line_o.shape[2]
    lane = lax.broadcasted_iota(jnp.int32, (part, 128), 1)
    lane_row = lax.broadcasted_iota(jnp.int32, (row, 128), 1)
    away = pl.ds(pl.multiple_of((1 - core) * size, size), size)
    slot = 0
    first = []
    for src, dst in ((o_ref.at[:, away, :], core_o), (m_ref.at[:, away, :], core_s.at[0]), (l_ref.at[:, away, :], core_s.at[1])):
        first.append(push(src, dst, send_sems.at[slot], recv_sems.at[slot], other[0]))
        slot += 1
    for copy in first:
        copy.wait_recv()

    def core_blend(to):
        at = pl.ds(pl.multiple_of(to * part, part), part)
        here = pl.ds(pl.multiple_of(core * size + to * part, part), part)
        return blend(
            [
                (o_ref[:, here, :], m_ref[:, here, :], l_ref[:, here, :]),
                (core_o[:, at, :], core_s[0, :, at, :], core_s[1, :, at, :]),
            ],
            lane,
        )

    second = []
    for k, (who, to, _) in enumerate(plane):
        planes, top, total = core_blend(to)
        for j, value in enumerate(planes):
            sum_o[k, j] = value.astype(sum_o.dtype)
        sum_s[k, 0] = top
        sum_s[k, 1] = total
        second.append(push(sum_o.at[k], plane_o.at[k], send_sems.at[slot], recv_sems.at[slot], who))
        slot += 1
        second.append(push(sum_s.at[k], plane_s.at[k], send_sems.at[slot], recv_sems.at[slot], who))
        slot += 1
    planes, top, total = core_blend(spot)
    parts = [(planes, top, total)]
    for k in range(len(plane)):
        second[2 * k].wait_recv()
        second[2 * k + 1].wait_recv()
        parts.append((plane_o[k], plane_s[k, 0], plane_s[k, 1]))
    planes, top, total = blend(parts, lane)
    for j, value in enumerate(planes):
        keep_o[j] = value.astype(keep_o.dtype)
    keep_s[0] = top
    keep_s[1] = total
    third = []
    for k, (who, to, _) in enumerate(line):
        at = pl.ds(pl.multiple_of(to * row, row), row)
        third.append(push(keep_o.at[:, at, :], line_o.at[k], send_sems.at[slot], recv_sems.at[slot], who))
        slot += 1
        third.append(push(keep_s.at[:, :, at, :], line_s.at[k], send_sems.at[slot], recv_sems.at[slot], who))
        slot += 1
    at = pl.ds(pl.multiple_of(batch * row, row), row)
    parts = [(keep_o[:, at, :], keep_s[0, :, at, :], keep_s[1, :, at, :])]
    for k in range(len(line)):
        third[2 * k].wait_recv()
        third[2 * k + 1].wait_recv()
        parts.append((line_o[k], line_s[k, 0], line_s[k, 1]))
    planes, top, total = blend(parts, lane_row)
    for j, value in enumerate(planes):
        oo_ref[j] = value
    mo_ref[...] = top
    lo_ref[...] = total
    for copy in first + second + third:
        copy.wait_send()


def mix(o, m, l, cid):
    _, n_y, n_batch = places()
    n_plane = 2 * n_y
    total = 2 * n_plane * n_batch
    planes, rows, _ = o.shape
    nm = m.shape[0]
    bf16, f32 = jnp.bfloat16, jnp.float32
    copies = 3 + 2 * (n_plane - 1) + 2 * (n_batch - 1)
    part, row = rows // (2 * n_plane), rows // total
    vm = pl.BlockSpec(memory_space=pltpu.VMEM)
    return pl.pallas_call(
        mix_kernel,
        out_shape=[
            jax.ShapeDtypeStruct((planes, row, 128), f32),
            jax.ShapeDtypeStruct((nm, row, 128), f32),
            jax.ShapeDtypeStruct((nm, row, 128), f32),
        ],
        in_specs=[vm] * 3,
        out_specs=[vm] * 3,
        scratch_shapes=[
            pltpu.VMEM((planes, rows // 2, 128), bf16),
            pltpu.VMEM((2, nm, rows // 2, 128), f32),
            pltpu.VMEM((n_plane - 1, planes, part, 128), bf16),
            pltpu.VMEM((n_plane - 1, 2, nm, part, 128), f32),
            pltpu.VMEM((n_plane - 1, planes, part, 128), bf16),
            pltpu.VMEM((n_plane - 1, 2, nm, part, 128), f32),
            pltpu.VMEM((planes, part, 128), bf16),
            pltpu.VMEM((2, nm, part, 128), f32),
            pltpu.VMEM((n_batch - 1, planes, row, 128), bf16),
            pltpu.VMEM((n_batch - 1, 2, nm, row, 128), f32),
            pltpu.SemaphoreType.DMA((copies,)),
            pltpu.SemaphoreType.DMA((copies,)),
        ],
        compiler_params=pltpu.CompilerParams(collective_id=cid, has_side_effects=True, vmem_limit_bytes=56 * 2**20),
        name="mix",
    )(o, m, l)


AXES = ("half", "mp", "batch")


def norm_forward(x, gain):
    scale = lax.rsqrt(jnp.mean(x * x, axis=-1, keepdims=True) + EPS_NORM)
    return (x * scale * gain, scale)


def norm_backward(d_out, x, scale, gain):
    d_gain = d_out * x * scale
    d_hat = d_out * gain
    d_x = scale * (d_hat - x * scale * scale * jnp.mean(d_hat * x, axis=-1, keepdims=True))
    return (d_x, d_gain)


def frequencies():
    half_size = HEAD_SIZE // 2
    return THETA ** (-(jnp.arange(half_size, dtype=jnp.float32) * 2.0) / HEAD_SIZE)


def rotate(x, cosine, sine, sign):
    half_size = HEAD_SIZE // 2
    first, second = x[..., :half_size], x[..., half_size:]
    return jnp.concatenate(
        [first * cosine - sign * second * sine, second * cosine + sign * first * sine], axis=-1
    )


def to_pairs(x):
    lead, rows = x.shape[:-2], x.shape[-2]
    x = x.reshape(lead + (rows, PAIRS, 128))
    x = jnp.moveaxis(x, -2, -3)
    return x.reshape((-1, rows, 128))


def from_pairs(x, models):
    rows = x.shape[1]
    x = x.reshape(models, PAIRS, rows, 128)
    return jnp.moveaxis(x, 1, 2).reshape(models, rows, MODEL_WIDTH)


def bmm(x, w):
    return jnp.stack([jnp.dot(x[i], w[i], preferred_element_type=jnp.float32) for i in range(2)])


def body(
    tokens, lengths, labels, scored, qkv_weight, out_weight, gu_weight, down_weight, embed_weight, small_params,
    moment_qkv, moment_out, moment_gu, moment_down, moment_embed, moment_small,
    square_qkv, square_out, square_gu, square_down, square_embed, square_small,
    ref_qkv, ref_out, ref_gu, ref_down, ref_embed, ref_small,
):
    masters = (qkv_weight, out_weight, gu_weight, down_weight, embed_weight, small_params)
    firsts = (moment_qkv, moment_out, moment_gu, moment_down, moment_embed, moment_small)
    seconds = (square_qkv, square_out, square_gu, square_down, square_embed, square_small)
    bf16, f32, i32 = jnp.bfloat16, jnp.float32, jnp.int32
    n_mp, n_batch = lax.axis_size("mp"), lax.axis_size("batch")
    devices = 2 * n_mp * n_batch
    n_y = n_mp // 2
    block = embed_weight.shape[0]
    feats = qkv_weight.shape[0]
    units = down_weight.shape[0]
    rollouts = MICRO * n_batch
    length = n_mp * TOK
    rp = n_mp * P_SIZE
    n_rows = rollouts * rp
    own_rows = n_rows // devices
    lin = lax.axis_index(AXES)
    com = comm_index()
    base = lin * block

    smalls = jnp.stack([small_params.astype(bf16).reshape(-1), ref_small.reshape(-1)])
    extra = jnp.zeros((feats, 128), bf16).at[:2, : smalls.shape[1]].set(smalls) if smalls.shape[1] <= 128 else None
    w_cat = jnp.concatenate([qkv_weight.astype(bf16), out_weight.astype(bf16), ref_qkv, ref_out, extra], axis=1)
    w_all = lax.all_gather(w_cat, AXES, axis=0, tiled=True)
    gu_both = jnp.stack([gu_weight.astype(bf16), ref_gu]).reshape(2, feats, 2, devices, units)
    gu_send = gu_both.transpose(3, 0, 1, 2, 4).reshape(devices, 2, feats, 2 * units)
    gu_cols = lax.all_to_all(gu_send, AXES, split_axis=0, concat_axis=0, tiled=True)
    gu_cols = gu_cols.transpose(1, 0, 2, 3).reshape(2, MODEL_WIDTH, 2 * units)
    w_gate, w_up = gu_cols[:, :, :units], gu_cols[:, :, units:]
    down_low = jnp.stack([down_weight.astype(bf16), ref_down])

    ids = tokens.transpose(0, 2, 1, 3).reshape(rollouts, length)
    lens = lengths.reshape(rollouts)
    spots = jnp.arange(length, dtype=i32)
    flat_ids = jnp.arange(rollouts * length, dtype=i32).reshape(rollouts, length)
    bits = max(1, (block - 1).bit_length())
    local = (ids >= base) & (ids < base + block) & (spots[None, :] < lens[:, None])
    key = jnp.where(local, (flat_ids << bits) + (ids - base), jnp.int32(2**31 - 1)).reshape(-1)
    key = lax.sort(key)
    n_local = jnp.sum(local.astype(i32))
    live = jnp.arange(rollouts * length, dtype=i32) < n_local
    row_of = jnp.where(live, key & ((1 << bits) - 1), -1).reshape(-1, TILE)
    flat_of = jnp.where(live, key >> bits, 1 << 22).reshape(-1, TILE)
    pos_of = jnp.where(live, (key >> bits) % length, 0).reshape(-1, TILE).astype(f32)
    tile_lo = flat_of[:, 0] // length
    tile_hi = jnp.max(jnp.where(live, (key >> bits) // length, -1).reshape(-1, TILE), axis=1)
    n_one = n_local.reshape(1)

    picks = scored.transpose(0, 2, 1, 3) + (jnp.arange(n_mp, dtype=i32) * TOK)[None, None, :, None]
    picks = picks.reshape(rollouts, rp)
    valid = (picks + 1 < lens[:, None]).astype(f32)
    count = jnp.sum(valid)
    here = picks[:, :, None] == spots[None, None, :]
    after = picks[:, :, None] + 1 == spots[None, None, :]
    own_ids = jnp.sum(jnp.where(here, ids[:, None, :], 0), axis=2).reshape(-1)
    targets = jnp.sum(jnp.where(after, ids[:, None, :], 0), axis=2).reshape(-1)
    owned = (own_ids >= base) & (own_ids < base + block) & (picks < lens[:, None]).reshape(-1)
    own_row = jnp.where(owned, own_ids - base, -1)
    frow = (picks + (jnp.arange(rollouts, dtype=i32) * length)[:, None]).reshape(-1)
    frow_wide = jnp.broadcast_to(frow[:, None], (n_rows, 128))

    low_table, picked, x_tok = lookup(n_one, embed_weight, ref_embed, row_of, flat_of, frow_wide)
    (x0,) = reduce([picked], 1)

    w_all3 = w_all.reshape(devices, feats, -1)
    w_qkv = jnp.stack([w_all[:, :QKV], w_all[:, QKV + MODEL_WIDTH : 2 * QKV + MODEL_WIDTH]])
    w_q, w_kv = w_qkv[:, :, :MODEL_WIDTH], w_qkv[:, :, MODEL_WIDTH:]
    w_out = jnp.stack(
        [w_all[:, QKV : QKV + MODEL_WIDTH], w_all[:, 2 * QKV + MODEL_WIDTH : 2 * QKV + 2 * MODEL_WIDTH]]
    )
    flat_small = w_all3[:, :2, 2 * QKV + 2 * MODEL_WIDTH :][:, :, : smalls.shape[1]]
    small_rows = small_params.shape[0]
    flat_small = flat_small.reshape(devices, 2, small_rows, -1).transpose(1, 2, 0, 3).reshape(2, -1).astype(f32)
    gain_attn = flat_small[:, None, :MODEL_WIDTH]
    gain_mlp = flat_small[:, None, MODEL_WIDTH : 2 * MODEL_WIDTH]
    gain_final = flat_small[:, None, 2 * MODEL_WIDTH : 3 * MODEL_WIDTH]
    bias = flat_small[:, None, 3 * MODEL_WIDTH :]

    freq = frequencies()
    my_pos = lax.dynamic_slice_in_dim(picks.reshape(-1), com * own_rows, own_rows)
    angle = my_pos.astype(f32)[:, None] * freq[None, :]
    cosine, sine = jnp.cos(angle)[:, None, :], jnp.sin(angle)[:, None, :]
    a1, scale_one = norm_forward(x0, gain_attn)
    a1 = a1.astype(bf16)
    mixed = bmm(a1, w_q) + bias[:, :, :MODEL_WIDTH]
    q = rotate(mixed.reshape(2, own_rows, QUERY_HEADS, HEAD_SIZE), cosine, sine, 1.0)
    q = to_pairs(q.reshape(2, own_rows, MODEL_WIDTH).astype(bf16))
    q_all, a1_all = gather([q, a1[:1]], 2)

    freq_wide = jnp.tile(freq, 4).reshape(1, 128)
    o_part, m_part, l_part, kv_tok = attend(
        n_one, tile_lo, tile_hi, q_all, x_tok, w_kv, gain_attn, bias[:, :, MODEL_WIDTH:], freq_wide, frow_wide, flat_of,
        pos_of, length, rp,
    )
    o_sum, top, total = mix(o_part, m_part, l_part, 3)
    lse = (top + jnp.log(total))[0]
    share = (1.0 / total)[:, :, :QUERY_HEADS]
    o = from_pairs(o_sum, 2).reshape(2, own_rows, QUERY_HEADS, HEAD_SIZE) * share[..., None]
    o = o.reshape(2, own_rows, MODEL_WIDTH).astype(bf16)
    x1 = x0 + bmm(o, w_out)
    a2, scale_two = norm_forward(x1, gain_mlp)
    a2_all, o_all = gather([a2.astype(bf16), o[:1]], 4)
    gate, up = bmm(a2_all, w_gate), bmm(a2_all, w_up)
    hidden = (jax.nn.silu(gate) * up).astype(bf16)
    (branch,) = reduce([bmm(hidden, down_low).astype(bf16)], 5)
    x2 = x1 + branch
    af, scale_final = norm_forward(x2, gain_final)
    (af_all,) = gather([af.astype(bf16)], 6)

    vocab = base + jnp.arange(block, dtype=i32)
    hit = vocab[:, None] == targets[None, :]
    tables = (low_table, ref_embed)
    logits = [
        lax.dot_general(tables[i], af_all[i], (((1,), (1,)), ((), ())), preferred_element_type=f32) for i in range(2)
    ]
    stats = []
    for i in range(2):
        peak = jnp.max(logits[i], axis=0)
        stats.append(
            jnp.stack(
                [
                    peak,
                    jnp.sum(jnp.exp(logits[i] - peak[None, :]), axis=0),
                    jnp.sum(jnp.where(hit, logits[i], 0.0), axis=0),
                ]
            )
        )
    stats = jnp.concatenate(stats, axis=0)
    stats = jnp.concatenate([stats, jnp.zeros((2, n_rows), f32)], axis=0)
    (stats_all,) = gather([stats[None]], 7)
    stats_all = stats_all.reshape(devices, 8, n_rows)
    lps, lses = [], []
    for i in range(2):
        peaks = stats_all[:, 3 * i]
        peak = jnp.max(peaks, axis=0)
        sums = jnp.sum(stats_all[:, 3 * i + 1] * jnp.exp(peaks - peak[None]), axis=0)
        lses.append(peak + jnp.log(sums))
        lps.append(jnp.sum(stats_all[:, 3 * i + 2], axis=0) - lses[i])
    ratio = (lps[0] - lps[1]).reshape(rollouts, rp)
    factor = BETA * n_rows / count
    reward = factor * jnp.sum(valid * ratio, axis=1)
    d_reward = (jax.nn.sigmoid(reward) - labels.reshape(rollouts).astype(f32)) / rollouts
    d_lp = (valid * (d_reward * factor)[:, None]).reshape(-1)

    probs = jnp.exp(logits[0] - lses[0][None, :])
    d_logits = (d_lp[None, :] * (hit.astype(f32) - probs)).astype(bf16)
    d_af = lax.dot_general(d_logits, low_table, (((0,), (0,)), ((), ())), preferred_element_type=f32)
    (d_final,) = reduce([d_af.astype(bf16)[None]], 8)
    d_out, g_gain_final = norm_backward(d_final[0], x2[0], scale_final[0], gain_final[0])
    (d_branch,) = gather([d_out.astype(bf16)[None]], 9)
    d_branch = d_branch[0]
    g_down = lax.dot_general(hidden[0], d_branch, (((0,), (0,)), ((), ())), preferred_element_type=f32)
    d_hidden = lax.dot_general(d_branch, down_low[0], (((1,), (1,)), ((), ())), preferred_element_type=f32)
    sigma = jax.nn.sigmoid(gate[0])
    d_gate = (d_hidden * up[0] * sigma * (1.0 + gate[0] * (1.0 - sigma))).astype(bf16)
    d_up = (d_hidden * gate[0] * sigma).astype(bf16)
    d_a2 = lax.dot_general(d_gate, w_gate[0], (((1,), (1,)), ((), ())), preferred_element_type=f32)
    d_a2 = d_a2 + lax.dot_general(d_up, w_up[0], (((1,), (1,)), ((), ())), preferred_element_type=f32)
    (d_normed,) = reduce([d_a2.astype(bf16)[None]], 10)
    d_mid, g_gain_mlp = norm_backward(d_normed[0], x1[0], scale_two[0], gain_mlp[0])
    d_mid = d_mid + d_out
    d_attn = d_mid.astype(bf16)
    d_o = lax.dot_general(d_attn, w_out[0], (((1,), (1,)), ((), ())), preferred_element_type=f32).astype(bf16)
    delta = jnp.sum(
        (d_o.astype(f32) * o[0].astype(f32)).reshape(own_rows, QUERY_HEADS, HEAD_SIZE), axis=-1
    )
    row_stats = jnp.concatenate(
        [lse[:, :16], delta, jnp.zeros((own_rows, 128 - 16 - QUERY_HEADS), f32)], axis=1
    )
    d_attn_all, d_o_all, row_stats_all = gather([d_attn[None], to_pairs(d_o), row_stats[None]], 11)
    d_attn_all = d_attn_all[0]

    g_gate = lax.dot_general(a2_all[0], d_gate, (((0,), (0,)), ((), ())), preferred_element_type=f32)
    g_up = lax.dot_general(a2_all[0], d_up, (((0,), (0,)), ((), ())), preferred_element_type=f32)
    g_gu = jnp.concatenate([g_gate, g_up], axis=1)
    gu_square = jnp.sum(g_gu * g_gu)
    g_gu = lax.all_to_all(
        g_gu.astype(bf16).reshape(devices, feats, 2 * units), AXES, split_axis=0, concat_axis=0, tiled=True
    )
    g_gu = g_gu.reshape(devices, feats, 2, units).transpose(1, 2, 0, 3).reshape(feats, 2 * FF).astype(f32)

    dq_part, g_kv_part, g_gain_kv, g_bias_kv, dx_tok = attend_back(
        n_one, tile_lo, tile_hi, q_all[:PAIRS], d_o_all, row_stats_all[0], x_tok, kv_tok, w_kv[:1], gain_attn[:1],
        freq_wide, frow_wide, flat_of, pos_of, length, rp,
    )
    padded = -(-feats // 16) * 16
    g_kv_part = g_kv_part.reshape(2, n_y, 2, n_batch, feats, 256).transpose(2, 0, 1, 3, 4, 5)
    g_kv_part = jnp.pad(g_kv_part.reshape(devices, feats, 256), ((0, 0), (0, padded - feats), (0, 0)))
    dq, g_kv = reduce([dq_part, g_kv_part.reshape(1, devices * padded, 256)], 12)
    g_kv = g_kv[0, :feats]
    dq = rotate(from_pairs(dq, 1).reshape(own_rows, QUERY_HEADS, HEAD_SIZE), cosine, sine, -1.0)
    dq = dq.reshape(own_rows, MODEL_WIDTH).astype(bf16)
    (dq_all,) = gather([dq[None]], 13)
    dq_all = dq_all[0]
    d_a1 = lax.dot_general(dq_all, w_q[0], (((1,), (1,)), ((), ())), preferred_element_type=f32)
    x_row = picked[0].astype(f32)
    scale_row = lax.rsqrt(jnp.mean(x_row * x_row, axis=-1, keepdims=True) + EPS_NORM)
    d_row, g_gain_row = norm_backward(d_a1, x_row, scale_row, gain_attn[0])
    d_row = jnp.where(owned[:, None], d_row + d_attn_all.astype(f32), 0.0).astype(bf16)
    g_gain_row = jnp.sum(jnp.where(owned[:, None], g_gain_row, 0.0), axis=0)

    embed_grad, embed_square = table_grad(
        n_one, d_logits, af_all[0], d_row, own_row.reshape(1, -1), row_of, dx_tok, block
    )

    def mine(rows, grads):
        cols = lax.dynamic_slice_in_dim(rows, lin * feats, feats, 1)
        return lax.dot_general(cols, grads, (((0,), (0,)), ((), ())), preferred_element_type=f32)

    g_out = mine(o_all[0], d_attn_all)
    g_q = mine(a1_all[0], dq_all)
    g_qkv = jnp.concatenate([g_q, g_kv], axis=1)

    small_part = jnp.concatenate(
        [
            jnp.sum(g_gain_kv, axis=0) + g_gain_row,
            jnp.sum(g_gain_mlp, axis=0),
            jnp.sum(g_gain_final, axis=0),
            jnp.sum(dq.astype(f32), axis=0),
            jnp.sum(g_bias_kv, axis=0),
        ]
    )
    square_part = (
        jnp.sum(g_qkv * g_qkv) + jnp.sum(g_out * g_out) + gu_square + jnp.sum(g_down * g_down) + jnp.sum(embed_square)
    )
    last = jnp.concatenate([small_part, jnp.full((128,), square_part, f32), jnp.zeros((128,), f32)]).reshape(1, -1, 128)
    (last_all,) = gather([last], 14)
    last_all = jnp.sum(last_all.reshape(devices, -1, 128), axis=0)
    g_small = last_all[:small_rows]
    norm = jnp.sqrt(jnp.sum(g_small * g_small) + last_all[small_rows, 0])
    g_small = lax.dynamic_slice_in_dim(g_small, lin * small_params.shape[1], small_params.shape[1], 1)

    owned_grads = (g_qkv, g_out, g_gu, g_down, embed_grad, g_small)
    clip = jnp.minimum(1.0, CLIP / (norm + 1e-06))
    new_weights, new_firsts, new_seconds, new_lows, clipped_list = ([], [], [], [], [])
    for w, g, m, v in zip(masters, owned_grads, firsts, seconds):
        g = g * clip
        m_new = MOM1 * m + (1.0 - MOM1) * g
        v_new = MOM2 * v + (1.0 - MOM2) * g * g
        update = m_new / (1.0 - MOM1**STEP) / (jnp.sqrt(v_new / (1.0 - MOM2**STEP)) + EPS_ADAM)
        w_new = w - RATE * (update + DECAY * w)
        new_weights.append(w_new)
        new_firsts.append(m_new)
        new_seconds.append(v_new)
        clipped_list.append(g)
        new_lows.append(w_new.astype(bf16))
    return (
        *new_weights[:5], clipped_list[5], *new_firsts, *new_seconds, *new_lows[:5], norm,
    )


def solution(mesh):
    rows, cols = P(AXES, None), P(None, AXES)
    six = (rows, rows, rows, rows, rows, cols)
    in_specs = (P(), P(), P(), P()) + six * 4
    out_specs = six * 3 + (rows,) * 5 + (P(),)
    return jax.shard_map(body, mesh=mesh, in_specs=in_specs, out_specs=out_specs, check_vma=False)
```

time: 5680 us -> 741 us (0.13)
  blocking collectives: 2480 us -> 0 us
  other arithmetic: 1210 us -> 100 us
  local copies, waits for them, and re-layouts: 1060 us -> 95.8 us
  Pallas kernels: 0 us -> 449 us
  waiting for transfers between devices: 439 us -> 0.02 us
  matrix products: 327 us -> 52.8 us
  starting transfers between devices: 117 us -> 11.9 us
    unnamed x2 -> x0, blocking collectives: 1350 us -> none
    all_gather x14 -> x0, blocking collectives: 1100 us -> none  [the longest x1 471 us: body(): lax.all_gather(small_params.astype(bf16), ('half', 'mp', 'batch'), axis=1...]
    unnamed x10 -> x6, other arithmetic: 828 us -> 1.96 us
    pallas_call x0 -> x18, Pallas kernels: none -> 449 us  [the longest x8 156 us: gather(): pl.pallas_call(functools.partial(gather_kernel, n), out_shape=[jax.ShapeD...]
    convert_element_type x8 -> x6, local copies, waits for them, and re-layouts: 373 us -> 3.02 us  [the longest x3 2.68 us: body(): flat_small.reshape(devices, 2, small_rows, -1).transpose(1, 2, 0, 3)]
    reduce_scatter x6 -> x0, waiting for transfers between devices: 294 us -> none  [the longest x2 251 us: body(): lax.psum_scatter(padded, ('half', 'mp', 'batch'), scatter_dimension=0, ti...]
    dot_general x44 -> x23, matrix products: 327 us -> 52.8 us  [the longest x2 16.4 us: body(): lax.dot_general(tables[i], af_all[i], (((1,), (1,)), ((), ())), preferred...]
    unnamed x328 -> x165, local copies, waits for them, and re-layouts: 246 us -> 22.9 us
  transfers between devices with their start and end apart: 31 -> 3, of which waited for: 9 -> 0; matrix products, arithmetic and copies ran while one was open for 57% -> 15% of each run, Pallas kernels for 0% -> 11%
where the time goes in v1:
time: 741 us; the launch traced here: 732 us
  Pallas kernels  449 us (61%)
  other arithmetic  100 us (13%)
  local copies, waits for them, and re-layouts  95.8 us (13%)
  matrix products  52.8 us (7%)
  between operations  22.6 us (3%)
  starting transfers between devices  11.9 us (2%)
    pallas_call x8, Pallas kernels, gather(): pl.pallas_call(functools.partial(gather_kernel, n), out_shape=[jax.ShapeD...  156 us
    pallas_call x5, Pallas kernels, reduce(): pl.pallas_call(functools.partial(reduce_kernel, n), out_shape=[jax.ShapeD...  120 us
    convert_element_type x5, other arithmetic, body(): new_lows.append(w_new.astype(bf16))  52.4 us
    pallas_call x1, Pallas kernels, lookup(): pl.pallas_call(functools.partial(lookup_kernel, block, span), grid=(steps...  42.2 us
    pallas_call x1, Pallas kernels, mix(): pl.pallas_call(mix_kernel, out_shape=[jax.ShapeDtypeStruct((planes, row,...  41.5 us
    pallas_call x1, Pallas kernels, table_grad(): pl.pallas_call(functools.partial(table_grad_kernel, block, span, kept), g...  32.5 us
    pallas_call x1, Pallas kernels, attend(): pl.pallas_call(functools.partial(attend_kernel, length, rp), grid=(2,), o...  32 us
    pallas_call x1, Pallas kernels, attend_back(): pl.pallas_call(functools.partial(attend_back_kernel, length, rp), grid=(1...  24.3 us
  transfers between devices with their start and end apart: 3, of which 0 were waited for; matrix products, arithmetic and copies ran while one was open for 15% of the time, Pallas kernels for 11%

profile of v1, /device:TPU:0, one launch (start us, length us, event | category | flops | bytes accessed | tf_op | source)
XLA Modules:
  0.0 732.4 jit_solution(4500973926573117879)
XLA Ops:
  31.8 7.6 %all-to-all-start = ((bf16[32,2,28,304]{3,1,2,0:T(2,128)(2,1)}), bf16[32,2,28,304]{3,1,2,0:T(2,128)(2,1)}, u32[]{:S(2)}, u32[]{:S(2)}) async-start(bf16[32,2,28,304]{3,1,2,0:T(2,128)(2,1)} %copy.312), calls=%async_computation | async-start | bytes 2752512 | tf_op jit(solution)/shard_map/all_to_all | solution.py:922
  51.8 42.2 %lookup.1 = (bf16[4748,896]{1,0:T(8,128)(2,1)}, bf16[2,512,896]{2,1,0:T(8,128)(2,1)}, bf16[2,8192,896]{2,1,0:T(8,128)(2,1)}) custom-call(s32[1]{0:T(128)} %bitcast.1.n_ref, f32[4748,896]{1,0:T(8,128)} %table_ref.1, bf16[4748,896]{1,0:T(8,128)(2,1)} %frozen_ref.1, s32[64,128]{1,0:T(8,128)} %get-tuple-element.290.rows_ref, ...), custom_call_target="tpu_custom_call" | custom-call | tf_op jit(solution)/shard_map/lookup/pallas_call | solution.py:345
  95.6 38.5 %reduce_1.1 = f32[2,16,896]{2,1,0:T(8,128)S(1)} custom-call(bf16[2,512,896]{2,1,0:T(8,128)(2,1)S(1)} %copy-done.2), custom_call_target="tpu_custom_call" | custom-call | tf_op jit(solution)/shard_map/reduce_1/pallas_call | solution.py:256
  165.3 9.5 %reshape.786 = bf16[896,4224]{1,0:T(8,128)(2,1)} reshape(bf16[32,28,4224]{2,1,0:T(8,128)(2,1)} %all-gather.3.cloned.1.call-done) | data formatting | bytes 15138816
  194.2 27.5 %gather_2.1 = (bf16[14,512,128]{2,1,0:T(8,128)(2,1)S(1)}, bf16[1,512,896]{2,1,0:T(8,128)(2,1)S(1)}) custom-call(bf16[14,16,128]{2,1,0:T(8,128)(2,1)S(1)} %bitcast.355, bf16[1,16,896]{2,1,0:T(8,128)(2,1)S(1)} %slice.281.refs_1_), custom_call_target="tpu_custom_call" | custom-call | tf_op jit(solution)/shard_map/gather_2/pallas_call | solution.py:155
  223.9 32.0 %attend.1 = (bf16[14,512,128]{2,1,0:T(8,128)(2,1)}, f32[2,512,128]{2,1,0:T(8,128)}, f32[2,512,128]{2,1,0:T(8,128)}, bf16[2,8192,256]{2,1,0:T(8,128)(2,1)}) custom-call(s32[1]{0:T(128)} %bitcast.1.n_ref, s32[64]{0:T(128)} %and_select_fusion.1.lo_ref, s32[64]{0:T(128)} %fusion.115.hi_ref, bf16[14,512,128]{2,1,0:T(8,128)(2,1)} %copy-done.6, ...), custom_call_target="tpu_custom_call" | custom-call | tf_op jit(solution)/shard_map/attend/pallas_call | solution.py:484
  255.9 41.5 %mix.1 = (f32[14,16,128]{2,1,0:T(8,128)}, f32[2,16,128]{2,1,0:T(8,128)}, f32[2,16,128]{2,1,0:T(8,128)}) custom-call(bf16[14,512,128]{2,1,0:T(8,128)(2,1)} %get-tuple-element.69.o_ref, f32[2,512,128]{2,1,0:T(8,128)} %get-tuple-element.70.m_ref, f32[2,512,128]{2,1,0:T(8,128)} %get-tuple-element.71.l_ref), custom_call_target="tpu_custom_call" | custom-call | tf_op jit(solution)/shard_map/mix/pallas_call | solution.py:818
  304.9 30.8 %gather_4.1 = (bf16[2,512,896]{2,1,0:T(8,128)(2,1)S(1)}, bf16[1,512,896]{2,1,0:T(8,128)(2,1)S(1)}) custom-call(bf16[2,16,896]{2,1,0:T(8,128)(2,1)S(1)} %multiply_convert_fusion.3.refs_0_, bf16[1,16,896]{2,1,0:T(8,128)(2,1)S(1)} %slice.294.refs_1_), custom_call_target="tpu_custom_call" | custom-call | tf_op jit(solution)/shard_map/gather_4/pallas_call | solution.py:155
  339.6 23.8 %reduce_5.1 = f32[2,16,896]{2,1,0:T(8,128)S(1)} custom-call(bf16[2,512,896]{2,1,0:T(8,128)(2,1)S(1)} %pad_maximum_fusion.refs_0_), custom_call_target="tpu_custom_call" | custom-call | tf_op jit(solution)/shard_map/reduce_5/pallas_call | solution.py:256
  364.1 18.1 %gather_6.1 = bf16[2,512,896]{2,1,0:T(8,128)(2,1)S(1)} custom-call(bf16[2,16,896]{2,1,0:T(8,128)(2,1)S(1)} %multiply_convert_fusion.2.refs_0_), custom_call_target="tpu_custom_call" | custom-call | tf_op jit(solution)/shard_map/gather_6/pallas_call | solution.py:155
  382.2 8.5 %fusion.165 = (f32[512]{0:T(512)S(1)}, f32[512,4748]{0,1:T(8,128)S(1)}) fusion(bf16[4748,896]{1,0:T(8,128)(2,1)} %frozen_ref.1, bf16[2,512,896]{2,1,0:T(8,128)(2,1)S(1)} %gather_6.1), kind=kOutput, calls=%fused_computation.331 | convolution fusion | flops 4358739456 | bytes 19151872 | tf_op jit(solution)/shard_map/dot_general | solution.py:1009
  390.7 7.9 %fusion.164 = (f32[512]{0:T(512)S(1)}, f32[4748,512]{1,0:T(8,128)S(1)}) fusion(bf16[4748,896]{1,0:T(8,128)(2,1)} %get-tuple-element.75, bf16[2,512,896]{2,1,0:T(8,128)(2,1)S(1)} %gather_6.1), kind=kOutput, calls=%fused_computation.330 | convolution fusion | flops 4358739456 | bytes 19151872 | tf_op jit(solution)/shard_map/dot_general | solution.py:1009
  404.3 11.4 %gather_7.1 = f32[1,256,512]{2,1,0:T(8,128)S(1)} custom-call(f32[1,8,512]{2,1,0:T(8,128)S(1)} %bitcast.356), custom_call_target="tpu_custom_call" | custom-call | tf_op jit(solution)/shard_map/gather_7/pallas_call | solution.py:155
  425.2 10.6 %fusion.29.refs_0_ = bf16[1,512,896]{2,1,0:T(8,128)(2,1)S(1)} fusion(bf16[4748,512]{1,0:T(8,128)(2,1)S(1)} %fusion.5.dl_ref, bf16[4748,896]{1,0:T(8,128)(2,1)} %get-tuple-element.75), kind=kOutput, calls=%fused_computation.58 | convolution fusion | flops 4356767744 | bytes 14287872 | tf_op jit(solution)/shard_map/dot_general | solution.py:1042
  435.8 15.6 %reduce_8.1 = f32[1,16,896]{2,1,0:T(8,128)S(1)} custom-call(bf16[1,512,896]{2,1,0:T(8,128)(2,1)S(1)} %fusion.29.refs_0_), custom_call_target="tpu_custom_call" | custom-call | tf_op jit(solution)/shard_map/reduce_8/pallas_call | solution.py:256
  452.2 12.8 %gather_9.1 = bf16[1,512,896]{2,1,0:T(8,128)(2,1)S(1)} custom-call(bf16[1,16,896]{2,1,0:T(8,128)(2,1)S(1)} %fusion.147.refs_0_), custom_call_target="tpu_custom_call" | custom-call | tf_op jit(solution)/shard_map/gather_9/pallas_call | solution.py:155
  467.0 15.3 %reduce_10.1 = f32[1,16,896]{2,1,0:T(8,128)S(1)} custom-call(bf16[1,512,896]{2,1,0:T(8,128)(2,1)S(1)} %fusion.30.refs_0_), custom_call_target="tpu_custom_call" | custom-call | tf_op jit(solution)/shard_map/reduce_10/pallas_call | solution.py:256
  492.0 21.9 %gather_11.1 = (bf16[1,512,896]{2,1,0:T(8,128)(2,1)S(1)}, bf16[7,512,128]{2,1,0:T(8,128)(2,1)S(1)}, f32[1,512,128]{2,1,0:T(8,128)S(1)}) custom-call(bf16[1,16,896]{2,1,0:T(8,128)(2,1)S(1)} %add_convert_fusion.2.refs_0_, bf16[7,16,128]{2,1,0:T(8,128)(2,1)S(1)} %bitcast_bitcast_fusion.refs_1_, f32[1,16,128]{2,1,0:T(8,128)S(1)} %maximum_bitcast_fusion.1.refs_2_), custom_call_target="tpu_custom_call" | custom-call | tf_op jit(solution)/shard_map/gather_11/pallas_call | solution.py:155
  515.5 24.3 %attend_back.1 = (bf16[7,512,128]{2,1,0:T(8,128)(2,1)}, f32[896,256]{1,0:T(8,128)}, f32[8,896]{1,0:T(8,128)}, f32[8,256]{1,0:T(8,128)}, bf16[8192,896]{1,0:T(8,128)(2,1)}) custom-call(s32[1]{0:T(128)} %bitcast.1.n_ref, s32[64]{0:T(128)} %and_select_fusion.1.lo_ref, s32[64]{0:T(128)} %fusion.115.hi_ref, bf16[7,512,128]{2,1,0:T(8,128)(2,1)} %slice.236.q_ref, ...), custom_call_target="tpu_custom_call" | custom-call | tf_op jit(solution)/shard_map/attend_back/pallas_call | solution.py:597
  544.4 26.6 %reduce_12.1 = (f32[7,16,128]{2,1,0:T(8,128)S(1)}, f32[1,32,256]{2,1,0:T(8,128)S(1)}) custom-call(bf16[7,512,128]{2,1,0:T(8,128)(2,1)S(1)} %copy-done.11, f32[1,1024,256]{2,1,0:T(8,128)S(1)} %bitcast.351), custom_call_target="tpu_custom_call" | custom-call | tf_op jit(solution)/shard_map/reduce_12/pallas_call | solution.py:256
  571.5 13.6 %gather_13.1 = bf16[1,512,896]{2,1,0:T(8,128)(2,1)S(1)} custom-call(bf16[1,16,896]{2,1,0:T(8,128)(2,1)S(1)} %convert_element_type.201.refs_0_), custom_call_target="tpu_custom_call" | custom-call | tf_op jit(solution)/shard_map/gather_13/pallas_call | solution.py:155
  595.2 32.5 %table_grad.1 = (f32[4748,896]{1,0:T(8,128)}, f32[8,896]{1,0:T(8,128)}) custom-call(s32[1]{0:T(128)} %bitcast.1.n_ref, bf16[4748,512]{1,0:T(8,128)(2,1)} %copy-done.17, bf16[512,896]{1,0:T(8,128)(2,1)} %slice_bitcast_fusion.4.af_ref, bf16[512,896]{1,0:T(8,128)(2,1)} %fusion.18.dxs_ref, s32[1,512]{1,0:T(1,128)} %and_select_fusion.srow_ref, ...), custom_call_target="tpu_custom_call" | custom-call | tf_op jit(solution)/shard_map/table_grad/pallas_call | solution.py:685
  634.0 20.4 %gather_14.1 = f32[1,1024,128]{2,1,0:T(8,128)S(1)} custom-call(f32[1,32,128]{2,1,0:T(8,128)S(1)} %bitcast.358), custom_call_target="tpu_custom_call" | custom-call | tf_op jit(solution)/shard_map/gather_14/pallas_call | solution.py:155
  665.3 44.7 %fusion.149 = (bf16[4748,896]{1,0:T(8,128)(2,1)}, f32[4748,896]{1,0:T(8,128)}, f32[4748,896]{1,0:T(8,128)}, f32[4748,896]{1,0:T(8,128)}) fusion(f32[4748,896]{1,0:T(8,128)} %table_ref.1, f32[4748,896]{1,0:T(8,128)} %get-tuple-element.90, f32[]{:T(128)S(6)} %min.3, f32[4748,896]{1,0:T(8,128)} %param.44, f32[4748,896]{1,0:T(8,128)} %param.50), kind=kLoop, calls=%fused_computation.321 | loop fusion | flops 68067328 | bytes 127626240 | tf_op jit(solution)/shard_map/convert_element_type | solution.py:1141
  (375 shorter events, 172.2 us)
Async XLA Ops:
  7.2 330.9 %copy-start = (bf16[152,896]{1,0:T(8,128)(2,1)S(1)}, bf16[152,896]{1,0:T(8,128)(2,1)}, u32[]{:S(2)}) copy-start(bf16[152,896]{1,0:T(8,128)(2,1)} %param.55) | copy-start | bytes 817156
  7.2 153.9 %all-gather.3.cloned.1.call-start = ((), (), s32[]{:S(2)}) async-start(), calls=%async_computation.2 | async-start | bytes 8921088 | tf_op jit(solution)/shard_map/all_gather | solution.py:919
  31.8 111.3 %all-to-all-start = ((bf16[32,2,28,304]{3,1,2,0:T(2,128)(2,1)}), bf16[32,2,28,304]{3,1,2,0:T(2,128)(2,1)}, u32[]{:S(2)}, u32[]{:S(2)}) async-start(bf16[32,2,28,304]{3,1,2,0:T(2,128)(2,1)} %copy.312), calls=%async_computation | async-start | bytes 2752512 | tf_op jit(solution)/shard_map/all_to_all | solution.py:922
  50.3 90.9 %copy-start.56 = (s32[512]{0:T(512)}, s32[512]{0:T(512)S(1)}, u32[]{:S(2)}) copy-start(s32[512]{0:T(512)S(1)} %reshape.757) | copy-start | bytes 6148
  50.7 90.5 %copy-start.60 = (s32[512]{0:T(512)}, s32[512]{0:T(512)S(1)}, u32[]{:S(2)}) copy-start(s32[512]{0:T(512)S(1)} %lt.146) | copy-start | bytes 6148
  95.6 42.7 %copy-start.29 = (s32[64,128]{1,0:T(8,128)S(1)}, s32[64,128]{1,0:T(8,128)}, u32[]{:S(2)}) copy-start(s32[64,128]{1,0:T(8,128)} %get-tuple-element.289.flat_ref) | copy-start | bytes 98308
  95.6 44.3 %copy-start.3 = (bf16[2,512,896]{2,1,0:T(8,128)(2,1)S(1)}, bf16[2,512,896]{2,1,0:T(8,128)(2,1)}, u32[]{:S(2)}) copy-start(bf16[2,512,896]{2,1,0:T(8,128)(2,1)} %get-tuple-element.65.refs_0_) | copy-start | bytes 5505028
  143.1 50.7 %copy-start.50 = (f32[16,32]{1,0:T(8,128)}, f32[16,32]{1,0:T(8,128)S(1)}, u32[]{:S(2)}) copy-start(f32[16,32]{1,0:T(8,128)S(1)} %get-tuple-element.300) | copy-start | bytes 6148
  301.1 35.0 %copy-start.27 = (bf16[1,896,152]{1,2,0:T(8,128)(2,1)S(1)}, bf16[1,896,152]{1,2,0:T(8,128)(2,1)}, u32[]{:S(2)}) copy-start(bf16[1,896,152]{1,2,0:T(8,128)(2,1)} %copy.315) | copy-start | bytes 817156
  544.4 41.8 %copy-start.67 = (f32[8,256]{1,0:T(8,128)S(1)}, f32[8,256]{1,0:T(8,128)}, u32[]{:S(2)}) copy-start(f32[8,256]{1,0:T(8,128)} %get-tuple-element.85) | copy-start | bytes 24580
  544.4 41.8 %copy-start.62 = (f32[896]{0:T(1024)S(1)}, f32[896]{0:T(1024)}, u32[]{:S(2)}) copy-start(f32[896]{0:T(1024)} %get-tuple-element.227) | copy-start | bytes 10756
  544.4 41.8 %copy-start.66 = (f32[512]{0:T(512)S(1)}, f32[512]{0:T(512)}, u32[]{:S(2)}) copy-start(f32[512]{0:T(512)} %add_rsqrt_fusion) | copy-start | bytes 6148
  544.4 41.8 %copy-start.71 = (pred[512]{0:T(512)(128)(4,1)S(1)}, pred[512]{0:T(512)(128)(4,1)}, u32[]{:S(2)}) copy-start(pred[512]{0:T(512)(128)(4,1)} %compare_and_fusion.2) | copy-start | bytes 1540
  595.2 35.9 %copy-start.21 = (f32[896,152]{0,1:T(8,128)S(1)}, f32[896,152]{0,1:T(8,128)}, u32[]{:S(2)}) copy-start(f32[896,152]{0,1:T(8,128)} %get-tuple-element.313) | copy-start | bytes 1634308
  595.2 35.9 %copy-start.22 = (f32[896,152]{0,1:T(8,128)S(1)}, f32[896,152]{0,1:T(8,128)}, u32[]{:S(2)}) copy-start(f32[896,152]{0,1:T(8,128)} %get-tuple-element.315) | copy-start | bytes 1634308
  658.8 54.4 %all-to-all-start.1 = ((bf16[32,28,304]{2,1,0:T(8,128)(2,1)}), bf16[32,28,304]{2,1,0:T(8,128)(2,1)S(1)}, u32[]{:S(2)}, u32[]{:S(2)}) async-start(bf16[32,28,304]{2,1,0:T(8,128)(2,1)} %pad_maximum_fusion.2), calls=%async_computation.1 | async-start | bytes 1572864 | tf_op jit(solution)/shard_map/all_to_all | solution.py:1072
  665.2 44.7 %copy-start.33 = (f32[28,896]{1,0:T(8,128)S(1)}, f32[28,896]{1,0:T(8,128)}, u32[]{:S(2)}) copy-start(f32[28,896]{1,0:T(8,128)} %param.35) | copy-start | bytes 301060
  665.2 44.7 %copy-start.34 = (f32[28,896]{1,0:T(8,128)S(1)}, f32[28,896]{1,0:T(8,128)}, u32[]{:S(2)}) copy-start(f32[28,896]{1,0:T(8,128)} %get-tuple-element.309) | copy-start | bytes 301060
  665.2 44.7 %copy-start.48 = (f32[28,896]{1,0:T(8,128)S(1)}, f32[28,896]{1,0:T(8,128)}, u32[]{:S(2)}) copy-start(f32[28,896]{1,0:T(8,128)} %param.41) | copy-start | bytes 301060
  665.2 44.7 %copy-start.49 = (f32[28,896]{1,0:T(8,128)S(1)}, f32[28,896]{1,0:T(8,128)}, u32[]{:S(2)}) copy-start(f32[28,896]{1,0:T(8,128)} %param.47) | copy-start | bytes 301060
  665.2 45.5 %copy-start.24 = (f32[152,896]{1,0:T(8,128)S(1)}, f32[152,896]{1,0:T(8,128)}, u32[]{:S(2)}) copy-start(f32[152,896]{1,0:T(8,128)} %param.37) | copy-start | bytes 1634308
  665.2 45.5 %copy-start.25 = (f32[152,896]{1,0:T(8,128)S(1)}, f32[152,896]{1,0:T(8,128)}, u32[]{:S(2)}) copy-start(f32[152,896]{1,0:T(8,128)} %get-tuple-element.311) | copy-start | bytes 1634308
  665.2 45.5 %copy-start.31 = (f32[152,896]{1,0:T(8,128)S(1)}, f32[152,896]{1,0:T(8,128)}, u32[]{:S(2)}) copy-start(f32[152,896]{1,0:T(8,128)} %param.43) | copy-start | bytes 1634308
  665.3 45.5 %copy-start.32 = (f32[152,896]{1,0:T(8,128)S(1)}, f32[152,896]{1,0:T(8,128)}, u32[]{:S(2)}) copy-start(f32[152,896]{1,0:T(8,128)} %param.49) | copy-start | bytes 1634308
  (55 other events, 500.7 us)
Sparse Core Ops, SparseCore 0:
  13.5 104.9 all-gather.2

commit v2 on v1

v2 whole, which is shorter than its diff:
```python
import functools

import jax
import jax.numpy as jnp
from jax import lax
from jax.experimental import pallas as pl
from jax.experimental.pallas import tpu as pltpu
from jax.sharding import PartitionSpec as P

MODEL_WIDTH = 896
QUERY_HEADS = 14
KEY_VALUE_HEADS = 2
HEAD_SIZE = 64
FF = 4864
QKV = 1152
TOK = 256
P_SIZE = 16
MICRO = 2
STEP = 5

EPS_NORM = 1e-06
THETA = 1000000.0
BETA = 0.05
CLIP = 0.1
RATE = 0.03
DECAY = 0.01
MOM1 = 0.5
MOM2 = 0.5
EPS_ADAM = 1e-08

MESH = pl.DeviceIdType.MESH

def places():
    n_mp, n_batch = lax.axis_size("mp"), lax.axis_size("batch")
    return 2, n_mp // 2, n_batch


def coords():
    mp = lax.axis_index("mp")
    return lax.axis_index("half"), mp // 2, lax.rem(mp, 2), lax.axis_index("batch")


def comm_index():
    _, n_y, n_batch = places()
    half, y, core, batch = coords()
    return ((core * 2 + half) * n_y + y) * n_batch + batch


def peers():
    _, n_y, n_batch = places()
    half, y, core, batch = coords()
    line = []
    for k in range(1, n_batch):
        to, frm = lax.rem(batch + k, n_batch), lax.rem(batch + n_batch - k, n_batch)
        line.append(({"half": half, "mp": y * 2 + core, "batch": to}, to, frm))
    plane = []
    n_plane = 2 * n_y
    spot = half * n_y + y
    for k in range(1, n_plane):
        to, frm = lax.rem(spot + k, n_plane), lax.rem(spot + n_plane - k, n_plane)
        plane.append(
            ({"half": to // n_y, "mp": lax.rem(to, n_y) * 2 + core, "batch": batch}, to, frm)
        )
    other = ({"half": half, "mp": y * 2 + (1 - core), "batch": batch}, 1 - core, 1 - core)
    return line, plane, other


def greet(line, plane, other):
    barrier = pltpu.get_barrier_semaphore()
    everyone = line + plane + [other]
    for who, _, _ in everyone:
        pl.semaphore_signal(barrier, inc=1, device_id=who, device_id_type=MESH)
    pl.semaphore_wait(barrier, len(everyone))


def push(src, dst, send_sem, recv_sem, who):
    copy = pltpu.make_async_remote_copy(
        src_ref=src,
        dst_ref=dst,
        send_sem=send_sem,
        recv_sem=recv_sem,
        device_id=who,
        device_id_type=MESH,
    )
    copy.start()
    return copy


def gather_kernel(n_arr, *refs):
    ins, outs = refs[:n_arr], refs[n_arr : 2 * n_arr]
    send_sems, recv_sems, own_sem = refs[2 * n_arr :]
    _, n_y, n_batch = places()
    half, y, core, batch = coords()
    n_plane = 2 * n_y
    spot = half * n_y + y
    line, plane, other = peers()
    greet(line, plane, other)
    slots = iter(range(n_arr * (n_batch - 1 + n_plane * n_batch + (n_plane - 1) * n_batch)))

    def rows(i, where, j):
        size = ins[i].shape[1]
        at = (core * n_plane + where) * n_batch + lax.rem(batch + n_batch - j, n_batch)
        return outs[i].at[:, pl.ds(pl.multiple_of(at * size, size), size), :]

    def send(src, dst, who):
        slot = next(slots)
        return push(src, dst, send_sems.at[slot], recv_sems.at[slot], who)

    local, by_line, by_plane, by_core = [], [], [], []
    for i in range(n_arr):
        by_line.append([send(ins[i], rows(i, spot, 0), who) for who, _, _ in line])
    for i in range(n_arr):
        by_plane.append([[send(ins[i], rows(i, spot, 0), who) for who, _, _ in plane]])
        by_core.append(send(ins[i], rows(i, spot, 0), other[0]))
        copy = pltpu.make_async_copy(ins[i], rows(i, spot, 0), own_sem.at[i])
        copy.start()
        local.append(copy)
    for j in range(1, n_batch):
        for i in range(n_arr):
            by_line[i][j - 1].wait_recv()
            by_plane[i].append([send(rows(i, spot, j), rows(i, spot, j), who) for who, _, _ in plane])
            by_core.append(send(rows(i, spot, j), rows(i, spot, j), other[0]))
    for j in range(n_batch):
        for i in range(n_arr):
            for k, (_, _, frm) in enumerate(plane):
                by_plane[i][j][k].wait_recv()
                by_core.append(send(rows(i, frm, j), rows(i, frm, j), other[0]))
    for copy in local:
        copy.wait()
    for copy in by_core:
        copy.wait_recv()
    for i in range(n_arr):
        for copy in by_line[i] + sum(by_plane[i], []):
            copy.wait_send()
    for copy in by_core:
        copy.wait_send()


def gather(arrays, cid, vmem=48):
    _, n_y, n_batch = places()
    n_plane = 2 * n_y
    total = 2 * n_plane * n_batch
    n = len(arrays)
    copies = n * ((n_batch - 1) + (n_plane - 1) * n_batch + n_plane * n_batch)
    return pl.pallas_call(
        functools.partial(gather_kernel, n),
        out_shape=[jax.ShapeDtypeStruct((a.shape[0], a.shape[1] * total, a.shape[2]), a.dtype) for a in arrays],
        in_specs=[pl.BlockSpec(memory_space=pltpu.VMEM)] * n,
        out_specs=[pl.BlockSpec(memory_space=pltpu.VMEM)] * n,
        scratch_shapes=[
            pltpu.SemaphoreType.DMA((copies,)),
            pltpu.SemaphoreType.DMA((copies,)),
            pltpu.SemaphoreType.DMA((n,)),
        ],
        compiler_params=pltpu.CompilerParams(
            collective_id=cid, has_side_effects=True, vmem_limit_bytes=vmem * 2**20
        ),
        name=f"gather_{cid}",
    )(*arrays)


def reduce_kernel(n_arr, *refs):
    ins, outs = refs[:n_arr], refs[n_arr : 2 * n_arr]
    scr = refs[2 * n_arr : 7 * n_arr]
    send_sems, recv_sems = refs[7 * n_arr :]
    _, n_y, n_batch = places()
    half, y, core, batch = coords()
    n_plane = 2 * n_y
    spot = half * n_y + y
    line, plane, other = peers()
    greet(line, plane, other)
    f32 = jnp.float32
    slots = iter(range(n_arr * (n_plane * n_batch + (n_plane - 1) * n_batch + n_batch - 1)))
    order = list(range(1, n_batch)) + [0]
    spots = [to for _, to, _ in plane] + [spot]

    def send(src, dst, who):
        slot = next(slots)
        return push(src, dst, send_sems.at[slot], recv_sems.at[slot], who)

    def rows(i, side, where, j):
        size = outs[i].shape[1]
        at = (side * n_plane + where) * n_batch + lax.rem(batch + j, n_batch)
        return pl.ds(pl.multiple_of(at * size, size), size)

    by_core, by_plane, by_line = {}, {}, {}
    for j in order:
        for p in range(n_plane):
            for i in range(n_arr):
                src = ins[i].at[:, rows(i, 1 - core, spots[p], j), :]
                by_core[i, p, j] = send(src, scr[5 * i].at[p, j], other[0])

    def mine(i, p, j):
        by_core[i, p, j].wait_recv()
        return ins[i][:, rows(i, core, spots[p], j), :].astype(f32) + scr[5 * i][p, j].astype(f32)

    for j in order:
        for p in range(n_plane - 1):
            for i in range(n_arr):
                out = scr[5 * i + 1]
                out[p, j] = mine(i, p, j).astype(out.dtype)
                by_plane[i, p, j] = send(out.at[p, j], scr[5 * i + 2].at[p, j], plane[p][0])
    totals = {}
    for j in order:
        for i in range(n_arr):
            total = mine(i, n_plane - 1, j)
            for p in range(n_plane - 1):
                by_plane[i, p, j].wait_recv()
                total = total + scr[5 * i + 2][p, j].astype(f32)
            if j:
                out = scr[5 * i + 3]
                out[j - 1] = total.astype(out.dtype)
                by_line[i, j] = send(out.at[j - 1], scr[5 * i + 4].at[j - 1], line[j - 1][0])
            else:
                outs[i][...] = total
    for i in range(n_arr):
        for j in range(1, n_batch):
            by_line[i, j].wait_recv()
            outs[i][...] += scr[5 * i + 4][j - 1].astype(f32)
    for group in (by_core, by_plane, by_line):
        for copy in group.values():
            copy.wait_send()


def reduce(arrays, cid, vmem=48):
    _, n_y, n_batch = places()
    n_plane = 2 * n_y
    total = 2 * n_plane * n_batch
    n = len(arrays)
    copies = n * (n_plane * n_batch + (n_plane - 1) * n_batch + n_batch - 1)
    scratch = []
    for a in arrays:
        m, rows, w = a.shape
        size = rows // total
        scratch += [
            pltpu.VMEM((n_plane, n_batch, m, size, w), a.dtype),
            pltpu.VMEM((n_plane - 1, n_batch, m, size, w), a.dtype),
            pltpu.VMEM((n_plane - 1, n_batch, m, size, w), a.dtype),
            pltpu.VMEM((n_batch - 1, m, size, w), a.dtype),
            pltpu.VMEM((n_batch - 1, m, size, w), a.dtype),
        ]
    return pl.pallas_call(
        functools.partial(reduce_kernel, n),
        out_shape=[jax.ShapeDtypeStruct((a.shape[0], a.shape[1] // total, a.shape[2]), jnp.float32) for a in arrays],
        in_specs=[pl.BlockSpec(memory_space=pltpu.VMEM)] * n,
        out_specs=[pl.BlockSpec(memory_space=pltpu.VMEM)] * n,
        scratch_shapes=scratch
        + [pltpu.SemaphoreType.DMA((copies,)), pltpu.SemaphoreType.DMA((copies,))],
        compiler_params=pltpu.CompilerParams(
            collective_id=cid, has_side_effects=True, vmem_limit_bytes=vmem * 2**20
        ),
        name=f"reduce_{cid}",
    )(*arrays)


HEAD_SLOTS = (0, 2, 4, 6, 1, 3, 5, 8, 10, 12, 7, 9, 11, 13)
COMBOS = ((0, 4, 0), (0, 3, 4), (4, 7, 7), (3, 7, 10))
PAIRS = QUERY_HEADS // 2
TILE = 128


def column(vector):
    return jnp.transpose(jnp.broadcast_to(vector.astype(jnp.float32), (128, 128)))


def last_last(a, b):
    return lax.dot_general(a, b, (((1,), (1,)), ((), ())), preferred_element_type=jnp.float32)


def first_first(a, b):
    return lax.dot_general(a, b, (((0,), (0,)), ((), ())), preferred_element_type=jnp.float32)


def straight(a, b):
    return jnp.dot(a, b, preferred_element_type=jnp.float32)


def lookup_kernel(
    block, span, n_ref, rows_ref, table_ref, frozen_ref, flat_ref, frow_ref,
    low_ref, picked_ref, x_ref, held, rough, staged, sem,
):
    step = pl.program_id(0)
    f32, bf16 = jnp.float32, jnp.bfloat16
    low = table_ref[...].astype(bf16)
    low_ref[...] = low
    at = pl.multiple_of(step * span, span)
    held[0, pl.ds(at, span), :] = low.astype(f32)
    held[1, pl.ds(at, span), :] = frozen_ref[...].astype(f32)

    @pl.when(step == pl.num_programs(0) - 1)
    def _():
        picked_ref[...] = jnp.zeros_like(picked_ref)
        n_rows = frow_ref.shape[0]

        def tile(i, _):
            def eight(k, _):
                for j in range(8):
                    place = k * 8 + j
                    row = rows_ref[i * TILE + place]
                    for model in range(2):
                        rough[model, pl.ds(place, 1), :] = held[model, pl.ds(row, 1), :]
                return 0

            lax.fori_loop(0, TILE // 8, eight, 0)
            staged[...] = rough[...].astype(bf16)
            copy = pltpu.make_async_copy(staged, x_ref.at[:, pl.ds(pl.multiple_of(i * TILE, TILE), TILE), :], sem)
            copy.start()
            match = frow_ref[...] == jnp.broadcast_to(flat_ref[pl.ds(i, 1), :], (n_rows, TILE))
            match = jnp.where(match, 1.0, 0.0).astype(bf16)
            for model in range(2):
                picked_ref[model] = picked_ref[model] + straight(match, staged[model]).astype(bf16)
            copy.wait()
            return 0

        lax.fori_loop(0, (n_ref[0] + TILE - 1) // TILE, tile, 0)


def lookup(n_local, rows, table, frozen, flat, frow):
    block, width = table.shape
    span = 512
    steps = pl.cdiv(block, span)
    cap = flat.shape[0] * TILE
    n_rows = frow.shape[0]
    bf16 = jnp.bfloat16
    whole = lambda shape: pl.BlockSpec(shape, lambda i: (0,) * len(shape))
    smem = pl.BlockSpec(memory_space=pltpu.SMEM)
    return pl.pallas_call(
        functools.partial(lookup_kernel, block, span),
        grid=(steps,),
        out_shape=[
            jax.ShapeDtypeStruct((block, width), bf16),
            jax.ShapeDtypeStruct((2, n_rows, width), bf16),
            jax.ShapeDtypeStruct((2, cap, width), bf16),
        ],
        in_specs=[
            smem,
            smem,
            pl.BlockSpec((span, width), lambda i: (i, 0)),
            pl.BlockSpec((span, width), lambda i: (i, 0)),
            whole(flat.shape),
            whole(frow.shape),
        ],
        out_specs=[
            pl.BlockSpec((span, width), lambda i: (i, 0)),
            whole((2, n_rows, width)),
            pl.BlockSpec(memory_space=pl.ANY),
        ],
        scratch_shapes=[
            pltpu.VMEM((2, steps * span, width), jnp.float32),
            pltpu.VMEM((2, TILE, width), jnp.float32),
            pltpu.VMEM((2, TILE, width), bf16),
            pltpu.SemaphoreType.DMA,
        ],
        compiler_params=pltpu.CompilerParams(vmem_limit_bytes=60 * 2**20),
        name="lookup",
    )(n_local, rows, table, frozen, flat, frow)


def head_pieces(both, lane):
    turned = pltpu.roll(both, 64, 1)
    low, high = lane < 64, lane >= 64
    bf16 = jnp.bfloat16
    zero = jnp.zeros_like(both)
    return (
        jnp.where(low, both, zero).astype(bf16),
        jnp.where(high, turned, zero).astype(bf16),
        jnp.where(low, turned, zero).astype(bf16),
        jnp.where(high, both, zero).astype(bf16),
    )


def turn(values, positions, freq, lane, sign):
    angle = positions * freq
    cosine, sine = jnp.cos(angle), jnp.sin(angle)
    first = lax.rem(lane, 64) < 32
    mixed = jnp.where(first, -sign * pltpu.roll(values, 96, 1), sign * pltpu.roll(values, 32, 1))
    return values * cosine + mixed * sine


def allowed_of(frow, flat, r, length):
    flat = jnp.broadcast_to(flat, frow.shape)
    return jnp.where((flat <= frow) & (flat >= r * length), 1.0, 0.0)


def attend_kernel(
    length, rp, n_ref, lo_ref, hi_ref, q_ref, x_ref, w_ref, gain_ref, bias_ref, freq_ref, frow_ref, flat_ref, pos_ref,
    o_ref, st_ref, kv_ref, xbuf, kvbuf, m_scr, l_scr, o_scr, sem,
):
    model = pl.program_id(0)
    f32, bf16 = jnp.float32, jnp.bfloat16
    lane = lax.broadcasted_iota(jnp.int32, (TILE, 128), 1)
    lane_r = lax.broadcasted_iota(jnp.int32, (rp, 128), 1)
    m_scr[...] = jnp.full(m_scr.shape, -1e30, f32)
    l_scr[...] = jnp.zeros_like(l_scr)
    o_scr[...] = jnp.zeros_like(o_scr)

    tiles = (n_ref[0] + TILE - 1) // TILE

    def fetch(i):
        slot = lax.rem(i, 2)
        at = pl.ds(pl.multiple_of(i * TILE, TILE), TILE)
        return pltpu.make_async_copy(x_ref.at[model, at, :], xbuf.at[slot], sem.at[slot])

    @pl.when(tiles > 0)
    def _():
        fetch(0).start()

    def tile(i, _):
        at = pl.ds(pl.multiple_of(i * TILE, TILE), TILE)

        @pl.when(i + 1 < tiles)
        def _():
            fetch(i + 1).start()

        fetch(i).wait()
        x = xbuf[lax.rem(i, 2)].astype(f32)
        scale = lax.rsqrt(jnp.mean(x * x, axis=-1, keepdims=True) + EPS_NORM)
        normed = (x * scale * gain_ref[0]).astype(bf16)
        mixed = straight(normed, w_ref[...]) + bias_ref[0]
        key = turn(mixed[:, :128], column(pos_ref[pl.ds(i, 1), :]), freq_ref[...], lane, 1.0)
        key = key.astype(bf16)
        value = mixed[:, 128:].astype(bf16)
        kvbuf[...] = jnp.concatenate([key, value], axis=1)
        out = pltpu.make_async_copy(kvbuf, kv_ref.at[model, at, :], sem.at[2])
        out.start()
        keys = head_pieces(key.astype(f32), lane)
        values = head_pieces(value.astype(f32), lane)
        one = jnp.ones((TILE, 128), bf16)
        values = tuple(jnp.where((lane < 64) == (c % 2 == 0), v, one) for c, v in enumerate(values))
        flat = flat_ref[pl.ds(i, 1), :]

        def rollout(r, _):
            rows = pl.ds(pl.multiple_of(r * rp, rp), rp)
            ok = allowed_of(frow_ref[rows, :], flat, r, length)[None]
            shift = (ok - 1.0) * 1e30
            falls, adds = {}, {}
            for c, (p0, p1, s0) in enumerate(COMBOS):
                n = p1 - p0
                query = q_ref[p0:p1, rows, :].reshape(n * rp, 128)
                score = last_last(query, keys[c]).reshape(n, rp, TILE) * HEAD_SIZE ** (-0.5)
                score = score * ok + shift
                old = m_scr[s0 : s0 + n, rows, :]
                new = jnp.maximum(old, jnp.max(score, axis=-1, keepdims=True))
                m_scr[s0 : s0 + n, rows, :] = new
                fall = old - new
                prob = jnp.exp(score - new) * ok
                add = straight(prob.astype(bf16).reshape(n * rp, TILE), values[c]).reshape(n, rp, 128)
                for k in range(n):
                    falls[p0 + k, c % 2] = fall[k]
                    adds[p0 + k, c % 2] = add[k]
            for p in range(PAIRS):
                alpha = jnp.exp(jnp.where(lane_r < 64, falls[p, 0], falls[p, 1]))
                turned = pltpu.roll(alpha, 64, 1)
                o_scr[p, rows, :] = o_scr[p, rows, :] * alpha + jnp.where(lane_r < 64, adds[p, 0], adds[p, 1])
                l_scr[p, rows, :] = l_scr[p, rows, :] * turned + jnp.where(lane_r < 64, adds[p, 1], adds[p, 0])
            return 0

        lax.fori_loop(lo_ref[i], hi_ref[i] + 1, rollout, 0)
        out.wait()
        return 0

    lax.fori_loop(0, tiles, tile, 0)

    def leave(r, _):
        rows = pl.ds(pl.multiple_of(r * rp, rp), rp)
        o_ref[:, rows, :] = o_scr[:, rows, :].astype(bf16)
        tops = jnp.full((rp, 128), -1e30, f32)
        totals = jnp.zeros((rp, 128), f32)
        for slot, head in enumerate(HEAD_SLOTS):
            tops = jnp.where(lane_r == head, m_scr[slot, rows, :], tops)
            held = l_scr[head // 2, rows, :]
            held = held[:, 64:65] if head % 2 == 0 else held[:, 0:1]
            totals = jnp.where(lane_r == head, held, totals)
        st_ref[0, rows, :] = tops
        st_ref[1, rows, :] = totals
        return 0

    lax.fori_loop(0, m_scr.shape[1] // rp, leave, 0)


def attend(n_local, lo, hi, q, x, w, gain, bias, freq, frow, flat, pos, length, rp):
    n_rows = q.shape[1]
    width = x.shape[2]
    cap = x.shape[1]
    bf16 = jnp.bfloat16
    whole = lambda shape: pl.BlockSpec(shape, lambda i: (0,) * len(shape))
    smem = pl.BlockSpec(memory_space=pltpu.SMEM)
    anyw = pl.BlockSpec(memory_space=pl.ANY)
    model = lambda shape: pl.BlockSpec(shape, lambda i: (i, 0, 0))
    return pl.pallas_call(
        functools.partial(attend_kernel, length, rp),
        grid=(2,),
        out_shape=[
            jax.ShapeDtypeStruct((2 * PAIRS, n_rows, 128), bf16),
            jax.ShapeDtypeStruct((4, n_rows, 128), jnp.float32),
            jax.ShapeDtypeStruct((2, cap, 256), bf16),
        ],
        in_specs=[
            smem, smem, smem, model((PAIRS, n_rows, 128)), anyw, pl.BlockSpec((width, 256), lambda i: (0, i)), model((1, 1, width)),
            model((1, 1, 256)), whole((1, 128)), whole(frow.shape), whole(flat.shape), whole(pos.shape),
        ],
        out_specs=[model((PAIRS, n_rows, 128)), model((2, n_rows, 128)), anyw],
        scratch_shapes=[
            pltpu.VMEM((2, TILE, width), bf16),
            pltpu.VMEM((TILE, 256), bf16),
            pltpu.VMEM((QUERY_HEADS, n_rows, 128), jnp.float32),
            pltpu.VMEM((PAIRS, n_rows, 128), jnp.float32),
            pltpu.VMEM((PAIRS, n_rows, 128), jnp.float32),
            pltpu.SemaphoreType.DMA((3,)),
        ],
        compiler_params=pltpu.CompilerParams(vmem_limit_bytes=62 * 2**20),
        name="attend",
    )(n_local, lo, hi, q, x, w, gain, bias, freq, frow, flat, pos)


def attend_back_kernel(
    length, rp, n_ref, lo_ref, hi_ref, q_ref, do_ref, st_ref, x_ref, kv_ref, w_ref, gain_ref, freq_ref, frow_ref, flat_ref,
    pos_ref, dq_ref, gkv_ref, gs_ref, gb_ref, dx_ref, xbuf, kvbuf, dxbuf, dq_scr, dk_scr, dv_scr, sem,
):
    f32, bf16 = jnp.float32, jnp.bfloat16
    lane = lax.broadcasted_iota(jnp.int32, (TILE, 128), 1)
    dq_scr[...] = jnp.zeros_like(dq_scr)
    gkv_ref[...] = jnp.zeros_like(gkv_ref)
    gs_ref[...] = jnp.zeros_like(gs_ref)
    gb_ref[...] = jnp.zeros_like(gb_ref)

    def tile(i, _):
        at = pl.ds(pl.multiple_of(i * TILE, TILE), TILE)
        one = pltpu.make_async_copy(x_ref.at[0, at, :], xbuf, sem.at[0])
        one.start()
        two = pltpu.make_async_copy(kv_ref.at[0, at, :], kvbuf, sem.at[1])
        two.start()
        one.wait()
        two.wait()
        keys = head_pieces(kvbuf[:, :128].astype(f32), lane)
        values = head_pieces(kvbuf[:, 128:].astype(f32), lane)
        flat = flat_ref[pl.ds(i, 1), :]
        dk_scr[...] = jnp.zeros_like(dk_scr)
        dv_scr[...] = jnp.zeros_like(dv_scr)

        def rollout(r, _):
            rows = pl.ds(pl.multiple_of(r * rp, rp), rp)
            ok = allowed_of(frow_ref[rows, :], flat, r, length)[None]
            shift = (ok - 1.0) * 1e30
            stats = st_ref[rows, :]
            adds = {}
            for c, (p0, p1, s0) in enumerate(COMBOS):
                n = p1 - p0
                heads = HEAD_SLOTS[s0 : s0 + n]
                query = q_ref[p0:p1, rows, :].reshape(n * rp, 128)
                back = do_ref[p0:p1, rows, :].reshape(n * rp, 128)
                lse = jnp.stack([stats[:, h : h + 1] for h in heads])
                delta = jnp.stack([stats[:, 16 + h : 17 + h] for h in heads])
                score = last_last(query, keys[c]).reshape(n, rp, TILE) * HEAD_SIZE ** (-0.5)
                prob = jnp.exp(score * ok + shift - lse)
                d_prob = last_last(back, values[c]).reshape(n, rp, TILE)
                d_score = (prob * (d_prob - delta)).astype(bf16).reshape(n * rp, TILE)
                add = straight(d_score, keys[c]).reshape(n, rp, 128)
                dk_scr[c] += first_first(d_score, query)
                dv_scr[c] += first_first(prob.astype(bf16).reshape(n * rp, TILE), back)
                for k in range(n):
                    adds[p0 + k, c % 2] = add[k]
            for p in range(PAIRS):
                dq_scr[p, rows, :] = dq_scr[p, rows, :] + adds[p, 0] + adds[p, 1]
            return 0

        lax.fori_loop(lo_ref[i], hi_ref[i] + 1, rollout, 0)

        def joined(scr):
            return jnp.where(lane < 64, scr[0] + pltpu.roll(scr[1], 64, 1), scr[3] + pltpu.roll(scr[2], 64, 1))

        d_key = turn(joined(dk_scr) * HEAD_SIZE ** (-0.5), column(pos_ref[pl.ds(i, 1), :]), freq_ref[...], lane, -1.0)
        d_mixed = jnp.concatenate([d_key, joined(dv_scr)], axis=1).astype(bf16)
        x = xbuf[...].astype(f32)
        scale = lax.rsqrt(jnp.mean(x * x, axis=-1, keepdims=True) + EPS_NORM)
        gain = gain_ref[0]
        normed = (x * scale * gain).astype(bf16)
        gkv_ref[...] += first_first(normed, d_mixed)
        gb_ref[...] += jnp.sum(d_mixed.astype(f32).reshape(TILE // 8, 8, 256), axis=0)
        d_normed = last_last(d_mixed, w_ref[...])
        gs_ref[...] += jnp.sum((d_normed * x * scale).reshape(TILE // 8, 8, x.shape[1]), axis=0)
        d_hat = d_normed * gain
        d_x = scale * (d_hat - x * scale * scale * jnp.mean(d_hat * x, axis=-1, keepdims=True))
        dxbuf[...] = d_x.astype(bf16)
        out = pltpu.make_async_copy(dxbuf, dx_ref.at[at, :], sem.at[2])
        out.start()
        out.wait()
        return 0

    lax.fori_loop(0, (n_ref[0] + TILE - 1) // TILE, tile, 0)
    dq_ref[...] = (dq_scr[...] * HEAD_SIZE ** (-0.5)).astype(bf16)


def attend_back(n_local, lo, hi, q, do, stats, x, kv, w, gain, freq, frow, flat, pos, length, rp):
    n_rows = q.shape[1]
    width = x.shape[2]
    cap = x.shape[1]
    bf16, f32 = jnp.bfloat16, jnp.float32
    whole = lambda shape: pl.BlockSpec(shape, lambda i: (0,) * len(shape))
    smem = pl.BlockSpec(memory_space=pltpu.SMEM)
    anyw = pl.BlockSpec(memory_space=pl.ANY)
    return pl.pallas_call(
        functools.partial(attend_back_kernel, length, rp),
        grid=(1,),
        out_shape=[
            jax.ShapeDtypeStruct((PAIRS, n_rows, 128), bf16),
            jax.ShapeDtypeStruct((width, 256), f32),
            jax.ShapeDtypeStruct((8, width), f32),
            jax.ShapeDtypeStruct((8, 256), f32),
            jax.ShapeDtypeStruct((cap, width), bf16),
        ],
        in_specs=[
            smem, smem, smem, whole((PAIRS, n_rows, 128)), whole((PAIRS, n_rows, 128)), whole((n_rows, 128)), anyw, anyw,
            whole((width, 256)), whole((1, 1, width)), whole((1, 128)), whole(frow.shape), whole(flat.shape),
            whole(pos.shape),
        ],
        out_specs=[
            whole((PAIRS, n_rows, 128)), whole((width, 256)), whole((8, width)), whole((8, 256)), anyw,
        ],
        scratch_shapes=[
            pltpu.VMEM((TILE, width), bf16),
            pltpu.VMEM((TILE, 256), bf16),
            pltpu.VMEM((TILE, width), bf16),
            pltpu.VMEM((PAIRS, n_rows, 128), f32),
            pltpu.VMEM((4, TILE, 128), f32),
            pltpu.VMEM((4, TILE, 128), f32),
            pltpu.SemaphoreType.DMA((3,)),
        ],
        compiler_params=pltpu.CompilerParams(vmem_limit_bytes=60 * 2**20),
        name="attend_back",
    )(n_local, lo, hi, q, do, stats, x, kv, w, gain, freq, frow, flat, pos)


def table_grad_kernel(
    block, span, n_ref, rows_ref, dl_ref, af_ref, drow_ref, frow_ref, flat_ref, dx_ref,
    g_ref, sq_ref, added, moved, rough, sem,
):
    step = pl.program_id(0)
    f32, bf16 = jnp.float32, jnp.bfloat16

    @pl.when(step == 0)
    def _():
        sq_ref[...] = jnp.zeros_like(sq_ref)
        added[...] = jnp.zeros_like(added)
        n_rows = drow_ref.shape[0]

        def tile(i, _):
            copy = pltpu.make_async_copy(dx_ref.at[pl.ds(pl.multiple_of(i * TILE, TILE), TILE), :], moved, sem)
            copy.start()
            token = column(flat_ref[pl.ds(i, 1), :])
            token = jnp.concatenate([token] * (n_rows // 128), axis=1)
            match = jnp.where(token == jnp.broadcast_to(frow_ref[...], (TILE, n_rows)), 1.0, 0.0).astype(bf16)
            own = straight(match, drow_ref[...])
            copy.wait()
            rough[...] = own + moved[...].astype(f32)

            def eight(k, _):
                for j in range(8):
                    place = k * 8 + j
                    row = pl.ds(rows_ref[i * TILE + place], 1)
                    added[row, :] = added[row, :] + rough[pl.ds(place, 1), :]
                return 0

            lax.fori_loop(0, TILE // 8, eight, 0)
            return 0

        lax.fori_loop(0, (n_ref[0] + TILE - 1) // TILE, tile, 0)

    inside = step * span + lax.broadcasted_iota(jnp.int32, (span, 1), 0) < block
    logit = jnp.where(inside, dl_ref[...].astype(f32), 0.0).astype(bf16)
    total = straight(logit, af_ref[...]) + added[pl.ds(pl.multiple_of(step * span, span), span), :]
    g_ref[...] = total.astype(bf16)
    square = total * total
    sq_ref[...] += jnp.sum(square.reshape(span // 8, 8, square.shape[1]), axis=0)


def table_grad(n_local, rows, dl, af, drow, frow, flat, dx, block):
    n_rows, width = af.shape
    span = 512
    steps = pl.cdiv(block, span)
    whole = lambda shape: pl.BlockSpec(shape, lambda i: (0,) * len(shape))
    smem = pl.BlockSpec(memory_space=pltpu.SMEM)
    return pl.pallas_call(
        functools.partial(table_grad_kernel, block, span),
        grid=(steps,),
        out_shape=[
            jax.ShapeDtypeStruct((block, width), jnp.bfloat16),
            jax.ShapeDtypeStruct((8, width), jnp.float32),
        ],
        in_specs=[
            smem, smem,
            pl.BlockSpec((span, n_rows), lambda i: (i, 0)),
            whole(af.shape), whole(drow.shape), whole(frow.shape), whole(flat.shape),
            pl.BlockSpec(memory_space=pl.ANY),
        ],
        out_specs=[pl.BlockSpec((span, width), lambda i: (i, 0)), whole((8, width))],
        scratch_shapes=[
            pltpu.VMEM((steps * span, width), jnp.float32),
            pltpu.VMEM((TILE, width), jnp.bfloat16),
            pltpu.VMEM((TILE, width), jnp.float32),
            pltpu.SemaphoreType.DMA,
        ],
        compiler_params=pltpu.CompilerParams(vmem_limit_bytes=56 * 2**20),
        name="table_grad",
    )(n_local, rows, dl, af, drow, frow, flat, dx)


def spread_kernel(own_ref, frozen_ref, out_ref):
    devices, _, _, wide = out_ref.shape
    units, rows = wide // 2, own_ref.shape[0]
    bf16 = jnp.bfloat16
    out_ref[...] = jnp.zeros_like(out_ref)
    for side in range(2):
        for d in range(devices):
            at = (side * devices + d) * units
            out_ref[d, 0, :rows, side * units : (side + 1) * units] = own_ref[:, at : at + units].astype(bf16)
            out_ref[d, 1, :rows, side * units : (side + 1) * units] = frozen_ref[:, at : at + units]


def spread(own, frozen, devices, units, rows_up):
    vm = pl.BlockSpec(memory_space=pltpu.VMEM)
    return pl.pallas_call(
        spread_kernel,
        out_shape=jax.ShapeDtypeStruct((devices, 2, rows_up, 2 * units), jnp.bfloat16),
        in_specs=[vm, vm],
        out_specs=vm,
        compiler_params=pltpu.CompilerParams(vmem_limit_bytes=48 * 2**20),
        name="spread",
    )(own, frozen)


def join_kernel(g_ref, out_ref):
    devices, _, wide = g_ref.shape
    units, rows = wide // 2, out_ref.shape[0]
    for side in range(2):
        for d in range(devices):
            at = (side * devices + d) * units
            out_ref[:, at : at + units] = g_ref[d, :rows, side * units : (side + 1) * units].astype(jnp.float32)


def join(g, rows, units):
    vm = pl.BlockSpec(memory_space=pltpu.VMEM)
    return pl.pallas_call(
        join_kernel,
        out_shape=jax.ShapeDtypeStruct((rows, 2 * units * g.shape[0]), jnp.float32),
        in_specs=[vm],
        out_specs=vm,
        compiler_params=pltpu.CompilerParams(vmem_limit_bytes=48 * 2**20),
        name="join",
    )(g)


def blend(parts, lane):
    f32 = jnp.float32
    n_models = len(parts[0][1]) // 2
    planes, stats = [], []
    for model in range(n_models):
        tops = [p[1][2 * model] for p in parts]
        top = tops[0]
        for t in tops[1:]:
            top = jnp.maximum(top, t)
        weights = [jnp.exp(t - top) for t in tops]
        stats += [top, sum(p[1][2 * model + 1] * w for p, w in zip(parts, weights))]
        for pair in range(PAIRS):
            acc = None
            for p, w in zip(parts, weights):
                each = jnp.where(lane < 64, w[:, 2 * pair : 2 * pair + 1], w[:, 2 * pair + 1 : 2 * pair + 2])
                term = p[0][model * PAIRS + pair].astype(f32) * each
                acc = term if acc is None else acc + term
            planes.append(acc)
    return planes, stats


def mix_kernel(o_ref, st_ref, oo_ref, so_ref, *rest):
    core_o, core_s, sum_o, sum_s, plane_o, plane_s, keep_o, keep_s, line_o, line_s, send_sems, recv_sems = rest
    _, n_y, n_batch = places()
    half, y, core, batch = coords()
    n_plane = 2 * n_y
    spot = half * n_y + y
    line, plane, other = peers()
    greet(line, plane, other)
    size = oo_ref.shape[1]
    lane = lax.broadcasted_iota(jnp.int32, (size, 128), 1)
    order = list(range(1, n_batch)) + [0]
    spots = [to for _, to, _ in plane] + [spot]
    slots = iter(range(2 * (n_plane * n_batch + (n_plane - 1) * n_batch + n_batch - 1)))

    def send(src, dst, who):
        slot = next(slots)
        return push(src, dst, send_sems.at[slot], recv_sems.at[slot], who)

    def rows(side, where, j):
        at = (side * n_plane + where) * n_batch + lax.rem(batch + j, n_batch)
        return pl.ds(pl.multiple_of(at * size, size), size)

    def store(o, s, merged):
        for k, value in enumerate(merged[0]):
            o[k] = value.astype(o.dtype)
        for k, value in enumerate(merged[1]):
            s[k] = value

    by_core, by_plane, by_line = {}, {}, {}
    for j in order:
        for p in range(n_plane):
            at = rows(1 - core, spots[p], j)
            by_core[p, j] = (
                send(o_ref.at[:, at, :], core_o.at[p, j], other[0]), send(st_ref.at[:, at, :], core_s.at[p, j], other[0])
            )

    def mine(p, j):
        at = rows(core, spots[p], j)
        for copy in by_core[p, j]:
            copy.wait_recv()
        return blend([(o_ref[:, at, :], st_ref[:, at, :]), (core_o[p, j], core_s[p, j])], lane)

    for j in order:
        for p in range(n_plane - 1):
            store(sum_o.at[p, j], sum_s.at[p, j], mine(p, j))
            by_plane[p, j] = (
                send(sum_o.at[p, j], plane_o.at[p, j], plane[p][0]), send(sum_s.at[p, j], plane_s.at[p, j], plane[p][0])
            )
    for j in order:
        parts = [mine(n_plane - 1, j)]
        for p in range(n_plane - 1):
            for copy in by_plane[p, j]:
                copy.wait_recv()
            parts.append((plane_o[p, j], plane_s[p, j]))
        store(keep_o.at[j], keep_s.at[j], blend(parts, lane))
        if j:
            by_line[j] = (
                send(keep_o.at[j], line_o.at[j - 1], line[j - 1][0]), send(keep_s.at[j], line_s.at[j - 1], line[j - 1][0])
            )
    parts = [(keep_o[0], keep_s[0])]
    for j in range(1, n_batch):
        for copy in by_line[j]:
            copy.wait_recv()
        parts.append((line_o[j - 1], line_s[j - 1]))
    store(oo_ref, so_ref, blend(parts, lane))
    for group in (by_core, by_plane, by_line):
        for pair in group.values():
            for copy in pair:
                copy.wait_send()


def mix(o, stats, cid):
    _, n_y, n_batch = places()
    n_plane = 2 * n_y
    planes, all_rows, _ = o.shape
    ns = stats.shape[0]
    bf16, f32 = jnp.bfloat16, jnp.float32
    copies = 2 * (n_plane * n_batch + (n_plane - 1) * n_batch + n_batch - 1)
    row = all_rows // (2 * n_plane * n_batch)
    vm = pl.BlockSpec(memory_space=pltpu.VMEM)
    scratch = []
    for lead in ((n_plane, n_batch), (n_plane - 1, n_batch), (n_plane - 1, n_batch), (n_batch,), (n_batch - 1,)):
        scratch += [pltpu.VMEM(lead + (planes, row, 128), bf16), pltpu.VMEM(lead + (ns, row, 128), f32)]
    return pl.pallas_call(
        mix_kernel,
        out_shape=[
            jax.ShapeDtypeStruct((planes, row, 128), f32),
            jax.ShapeDtypeStruct((ns, row, 128), f32),
        ],
        in_specs=[vm] * 2,
        out_specs=[vm] * 2,
        scratch_shapes=scratch + [pltpu.SemaphoreType.DMA((copies,)), pltpu.SemaphoreType.DMA((copies,))],
        compiler_params=pltpu.CompilerParams(collective_id=cid, has_side_effects=True, vmem_limit_bytes=56 * 2**20),
        name="mix",
    )(o, stats)


AXES = ("half", "mp", "batch")


def norm_forward(x, gain):
    scale = lax.rsqrt(jnp.mean(x * x, axis=-1, keepdims=True) + EPS_NORM)
    return (x * scale * gain, scale)


def norm_backward(d_out, x, scale, gain):
    d_gain = d_out * x * scale
    d_hat = d_out * gain
    d_x = scale * (d_hat - x * scale * scale * jnp.mean(d_hat * x, axis=-1, keepdims=True))
    return (d_x, d_gain)


def frequencies():
    half_size = HEAD_SIZE // 2
    return THETA ** (-(jnp.arange(half_size, dtype=jnp.float32) * 2.0) / HEAD_SIZE)


def rotate(x, cosine, sine, sign):
    half_size = HEAD_SIZE // 2
    first, second = x[..., :half_size], x[..., half_size:]
    return jnp.concatenate(
        [first * cosine - sign * second * sine, second * cosine + sign * first * sine], axis=-1
    )


def to_pairs(x):
    lead, rows = x.shape[:-2], x.shape[-2]
    x = x.reshape(lead + (rows, PAIRS, 128))
    x = jnp.moveaxis(x, -2, -3)
    return x.reshape((-1, rows, 128))


def from_pairs(x, models):
    rows = x.shape[1]
    x = x.reshape(models, PAIRS, rows, 128)
    return jnp.moveaxis(x, 1, 2).reshape(models, rows, MODEL_WIDTH)


def bmm(x, w):
    return jnp.stack([jnp.dot(x[i], w[i], preferred_element_type=jnp.float32) for i in range(2)])


def body(
    tokens, lengths, labels, scored, qkv_weight, out_weight, gu_weight, down_weight, embed_weight, small_params,
    moment_qkv, moment_out, moment_gu, moment_down, moment_embed, moment_small,
    square_qkv, square_out, square_gu, square_down, square_embed, square_small,
    ref_qkv, ref_out, ref_gu, ref_down, ref_embed, ref_small,
):
    masters = (qkv_weight, out_weight, gu_weight, down_weight, embed_weight, small_params)
    firsts = (moment_qkv, moment_out, moment_gu, moment_down, moment_embed, moment_small)
    seconds = (square_qkv, square_out, square_gu, square_down, square_embed, square_small)
    bf16, f32, i32 = jnp.bfloat16, jnp.float32, jnp.int32
    n_mp, n_batch = lax.axis_size("mp"), lax.axis_size("batch")
    devices = 2 * n_mp * n_batch
    n_y = n_mp // 2
    block = embed_weight.shape[0]
    feats = qkv_weight.shape[0]
    units = down_weight.shape[0]
    rollouts = MICRO * n_batch
    length = n_mp * TOK
    rp = n_mp * P_SIZE
    n_rows = rollouts * rp
    own_rows = n_rows // devices
    lin = lax.axis_index(AXES)
    com = comm_index()
    base = lin * block

    feats_up = -(-feats // 16) * 16

    def to_up(x):
        return jnp.pad(x, ((0, feats_up - feats), (0, 0)))

    feat = jnp.arange(MODEL_WIDTH, dtype=i32)
    padded = jnp.arange(devices * feats_up, dtype=i32)
    to_order = (padded[None, :] == (feat // feats * feats_up + feat % feats)[:, None]).astype(bf16)
    from_order = (padded[:, None] == (feat // feats * feats_up + feat % feats)[None, :]).astype(bf16)

    def pad_feats(x):
        return jnp.dot(x, to_order, preferred_element_type=f32).astype(bf16)

    def cut_feats(x):
        high = x.astype(bf16)
        both = jnp.concatenate([high, (x - high.astype(f32)).astype(bf16)], axis=0)
        both = jnp.dot(both, from_order, preferred_element_type=f32)
        return both[: x.shape[0]] + both[x.shape[0] :]

    def placed(x):
        x = jnp.pad(x.astype(bf16), ((0, 0), (0, 128 - x.shape[1])))
        x = jnp.roll(x, lin * small_params.shape[1], axis=1)
        return jnp.pad(x, ((0, -x.shape[0] % feats_up), (0, 0)))

    qkv_low = qkv_weight.astype(bf16)
    early = to_up(
        jnp.concatenate(
            [qkv_low[:, :MODEL_WIDTH], ref_qkv[:, :MODEL_WIDTH], qkv_low[:, MODEL_WIDTH:], ref_qkv[:, MODEL_WIDTH:]], axis=1
        )
    )
    smalls = [placed(small_params), placed(ref_small)]
    tall = smalls[0].shape[0] // feats_up
    smalls = [x.reshape(tall, feats_up, 128)[k] for x in smalls for k in range(tall)]
    early = lax.all_gather(jnp.concatenate([early] + smalls, axis=1), AXES, axis=0, tiled=True)
    at_small = 2 * QKV
    w_q = (early[:, :MODEL_WIDTH], early[:, MODEL_WIDTH : 2 * MODEL_WIDTH])
    down_low = jnp.stack([down_weight.astype(bf16), ref_down])

    ids = tokens.transpose(0, 2, 1, 3).reshape(rollouts, length)
    lens = lengths.reshape(rollouts)
    spots = jnp.arange(length, dtype=i32)
    flat_ids = jnp.arange(rollouts * length, dtype=i32).reshape(rollouts, length)
    bits = max(1, (block - 1).bit_length())
    local = (ids >= base) & (ids < base + block) & (spots[None, :] < lens[:, None])
    key = jnp.where(local, (flat_ids << bits) + (ids - base), jnp.int32(2**31 - 1)).reshape(-1)
    key = lax.sort(key)
    n_local = jnp.sum(local.astype(i32))
    live = jnp.arange(rollouts * length, dtype=i32) < n_local
    row_of = jnp.where(live, key & ((1 << bits) - 1), 0)
    flat_of = jnp.where(live, key >> bits, 1 << 22).reshape(-1, TILE)
    pos_of = jnp.where(live, (key >> bits) % length, 0).reshape(-1, TILE).astype(f32)
    tile_lo = flat_of[:, 0] // length
    tile_hi = jnp.max(jnp.where(live, (key >> bits) // length, -1).reshape(-1, TILE), axis=1)
    n_one = n_local.reshape(1)

    picks = scored.transpose(0, 2, 1, 3) + (jnp.arange(n_mp, dtype=i32) * TOK)[None, None, :, None]
    picks = picks.reshape(rollouts, rp)
    valid = (picks + 1 < lens[:, None]).astype(f32)
    count = jnp.sum(valid)
    after = picks[:, :, None] + 1 == spots[None, None, :]
    targets = jnp.sum(jnp.where(after, ids[:, None, :], 0), axis=2).reshape(-1)
    frow = (picks + (jnp.arange(rollouts, dtype=i32) * length)[:, None]).reshape(-1)
    frow_wide = jnp.broadcast_to(frow[:, None], (n_rows, 128))

    low_table, picked, x_tok = lookup(n_one, row_of, embed_weight, ref_embed, flat_of, frow_wide)
    out_both = to_up(jnp.concatenate([out_weight.astype(bf16), ref_out], axis=1))
    picked, out_both = lax.optimization_barrier((picked, out_both))
    late = lax.all_gather(out_both, AXES, axis=0, tiled=True)
    w_out = (late[:, :MODEL_WIDTH], late[:, MODEL_WIDTH:])
    (x0,) = reduce([picked], 1)

    w_kv = jnp.dot(to_order, early[:, 2 * MODEL_WIDTH : at_small], preferred_element_type=f32).astype(bf16)
    small_rows = small_params.shape[0]
    flat_small = jnp.sum(early[:, at_small:].astype(f32).reshape(devices, feats_up, -1), axis=0)
    flat_small = flat_small.reshape(feats_up, 2, tall, 128).transpose(1, 2, 0, 3).reshape(2, tall * feats_up, 128)
    flat_small = flat_small[:, :small_rows].reshape(2, -1)
    gain_attn = flat_small[:, None, :MODEL_WIDTH]
    gain_mlp = flat_small[:, None, MODEL_WIDTH : 2 * MODEL_WIDTH]
    gain_final = flat_small[:, None, 2 * MODEL_WIDTH : 3 * MODEL_WIDTH]
    bias = flat_small[:, None, 3 * MODEL_WIDTH :]

    freq = frequencies()
    my_pos = lax.dynamic_slice_in_dim(picks.reshape(-1), com * own_rows, own_rows)
    angle = my_pos.astype(f32)[:, None] * freq[None, :]
    cosine, sine = jnp.cos(angle)[:, None, :], jnp.sin(angle)[:, None, :]
    a1, scale_one = norm_forward(x0, gain_attn)
    a1 = a1.astype(bf16)
    mixed = bmm(pad_feats(a1), w_q) + bias[:, :, :MODEL_WIDTH]
    q = rotate(mixed.reshape(2, own_rows, QUERY_HEADS, HEAD_SIZE), cosine, sine, 1.0)
    q = to_pairs(q.reshape(2, own_rows, MODEL_WIDTH).astype(bf16))
    q_all, a1_all = gather([q, a1[:1]], 2)
    q_all, gu_sent = lax.optimization_barrier((q_all, spread(gu_weight, ref_gu, devices, units, feats_up)))
    gu_cols = lax.all_to_all(gu_sent, AXES, split_axis=0, concat_axis=0, tiled=True)
    w_gu = tuple(gu_cols[:, model].reshape(devices * feats_up, 2 * units) for model in range(2))

    freq_wide = jnp.tile(freq, 4).reshape(1, 128)
    o_part, st_part, kv_tok = attend(
        n_one, tile_lo, tile_hi, q_all, x_tok, w_kv, gain_attn, bias[:, :, MODEL_WIDTH:], freq_wide, frow_wide, flat_of,
        pos_of, length, rp,
    )
    o_sum, st_sum = mix(o_part, st_part, 3)
    lse = st_sum[0] + jnp.log(st_sum[1])
    share = (1.0 / st_sum[1::2])[:, :, :QUERY_HEADS]
    o = from_pairs(o_sum, 2).reshape(2, own_rows, QUERY_HEADS, HEAD_SIZE) * share[..., None]
    o = o.reshape(2, own_rows, MODEL_WIDTH).astype(bf16)
    x1 = x0 + bmm(pad_feats(o), w_out)
    a2, scale_two = norm_forward(x1, gain_mlp)
    a2_all, o_all = gather([pad_feats(a2.astype(bf16)), o[:1]], 4)
    gate_up = bmm(a2_all, w_gu)
    gate, up = gate_up[:, :, :units], gate_up[:, :, units:]
    hidden = (jax.nn.silu(gate) * up).astype(bf16)
    (branch,) = reduce([bmm(hidden, down_low).astype(bf16)], 5)
    x2 = x1 + branch
    af, scale_final = norm_forward(x2, gain_final)
    (af_all,) = gather([af.astype(bf16)], 6)

    vocab = base + jnp.arange(block, dtype=i32)
    hit = vocab[:, None] == targets[None, :]
    tables = (low_table, ref_embed)
    logits = [
        lax.dot_general(tables[i], af_all[i], (((1,), (1,)), ((), ())), preferred_element_type=f32) for i in range(2)
    ]
    stats = []
    for i in range(2):
        peak = jnp.max(logits[i], axis=0)
        stats.append(
            jnp.stack(
                [
                    peak,
                    jnp.sum(jnp.exp(logits[i] - peak[None, :]), axis=0),
                    jnp.sum(jnp.where(hit, logits[i], 0.0), axis=0),
                ]
            )
        )
    stats = jnp.concatenate(stats, axis=0)
    stats = jnp.concatenate([stats, jnp.zeros((2, n_rows), f32)], axis=0)
    (stats_all,) = gather([stats[None]], 7)
    stats_all = stats_all.reshape(devices, 8, n_rows)
    lps, lses = [], []
    for i in range(2):
        peaks = stats_all[:, 3 * i]
        peak = jnp.max(peaks, axis=0)
        sums = jnp.sum(stats_all[:, 3 * i + 1] * jnp.exp(peaks - peak[None]), axis=0)
        lses.append(peak + jnp.log(sums))
        lps.append(jnp.sum(stats_all[:, 3 * i + 2], axis=0) - lses[i])
    ratio = (lps[0] - lps[1]).reshape(rollouts, rp)
    factor = BETA * n_rows / count
    reward = factor * jnp.sum(valid * ratio, axis=1)
    d_reward = (jax.nn.sigmoid(reward) - labels.reshape(rollouts).astype(f32)) / rollouts
    d_lp = (valid * (d_reward * factor)[:, None]).reshape(-1)

    probs = jnp.exp(logits[0] - lses[0][None, :])
    d_logits = (d_lp[None, :] * (hit.astype(f32) - probs)).astype(bf16)
    d_af = lax.dot_general(d_logits, low_table, (((0,), (0,)), ((), ())), preferred_element_type=f32)
    (d_final,) = reduce([d_af.astype(bf16)[None]], 8)
    d_out, g_gain_final = norm_backward(d_final[0], x2[0], scale_final[0], gain_final[0])
    (d_branch,) = gather([d_out.astype(bf16)[None]], 9)
    d_branch = d_branch[0]
    g_down = lax.dot_general(hidden[0], d_branch, (((0,), (0,)), ((), ())), preferred_element_type=f32)
    d_hidden = lax.dot_general(d_branch, down_low[0], (((1,), (1,)), ((), ())), preferred_element_type=f32)
    sigma = jax.nn.sigmoid(gate[0])
    d_gate = d_hidden * up[0] * sigma * (1.0 + gate[0] * (1.0 - sigma))
    d_up = d_hidden * gate[0] * sigma
    d_gate_up = jnp.concatenate([d_gate, d_up], axis=1).astype(bf16)
    d_a2 = lax.dot_general(d_gate_up, w_gu[0], (((1,), (1,)), ((), ())), preferred_element_type=f32)
    (d_normed,) = reduce([d_a2.astype(bf16)[None]], 10)
    d_mid, g_gain_mlp = norm_backward(cut_feats(d_normed[0]), x1[0], scale_two[0], gain_mlp[0])
    d_mid = d_mid + d_out
    d_attn = d_mid.astype(bf16)
    d_o = lax.dot_general(d_attn, w_out[0], (((1,), (1,)), ((), ())), preferred_element_type=f32)
    d_o = cut_feats(d_o).astype(bf16)
    delta = jnp.sum(
        (d_o.astype(f32) * o[0].astype(f32)).reshape(own_rows, QUERY_HEADS, HEAD_SIZE), axis=-1
    )
    row_stats = jnp.concatenate(
        [lse[:, :16], delta, jnp.zeros((own_rows, 128 - 16 - QUERY_HEADS), f32)], axis=1
    )
    d_attn_all, d_o_all, row_stats_all = gather([d_attn[None], to_pairs(d_o), row_stats[None]], 11)
    d_attn_all = d_attn_all[0]

    g_gu = lax.dot_general(a2_all[0], d_gate_up, (((0,), (0,)), ((), ())), preferred_element_type=f32)
    gu_square = jnp.sum(g_gu * g_gu)
    g_gu = g_gu.astype(bf16).reshape(devices, feats_up, 2 * units)
    g_gu, d_o_all = lax.optimization_barrier((g_gu, d_o_all))
    g_gu = lax.all_to_all(g_gu, AXES, split_axis=0, concat_axis=0, tiled=True)
    dq_part, g_kv_part, g_gain_kv, g_bias_kv, dx_tok = attend_back(
        n_one, tile_lo, tile_hi, q_all[:PAIRS], d_o_all, row_stats_all[0], x_tok, kv_tok, w_kv, gain_attn[:1],
        freq_wide, frow_wide, flat_of, pos_of, length, rp,
    )
    dq_part, g_gu = lax.optimization_barrier((dq_part, g_gu))
    g_kv_part = g_kv_part.reshape(2, n_y, 2, n_batch, feats, 256).transpose(2, 0, 1, 3, 4, 5)
    g_kv_part = jnp.pad(g_kv_part.reshape(devices, feats, 256), ((0, 0), (0, feats_up - feats), (0, 0)))
    dq, g_kv = reduce([dq_part, g_kv_part.reshape(1, devices * feats_up, 256)], 12)
    g_kv = g_kv[0, :feats]
    dq = rotate(from_pairs(dq, 1).reshape(own_rows, QUERY_HEADS, HEAD_SIZE), cosine, sine, -1.0)
    dq = dq.reshape(own_rows, MODEL_WIDTH).astype(bf16)
    d_a1 = cut_feats(lax.dot_general(dq, w_q[0], (((1,), (1,)), ((), ())), preferred_element_type=f32))
    d_row, g_gain_row = norm_backward(d_a1, x0[0], scale_one[0], gain_attn[0])
    dq_all, d_row_all = gather([dq[None], (d_row + d_mid).astype(bf16)[None]], 13)
    dq_all = dq_all[0]

    embed_grad, embed_square = table_grad(
        n_one, row_of, d_logits, af_all[0], d_row_all[0], frow.reshape(1, -1).astype(f32), flat_of, dx_tok, block
    )

    def mine(rows, grads):
        cols = lax.dynamic_slice_in_dim(rows, lin * feats, feats, 1)
        return lax.dot_general(cols, grads, (((0,), (0,)), ((), ())), preferred_element_type=f32)

    g_out = mine(o_all[0], d_attn_all)
    g_q = mine(a1_all[0], dq_all)
    g_qkv = jnp.concatenate([g_q, g_kv], axis=1)

    small_part = jnp.concatenate(
        [
            jnp.sum(g_gain_kv, axis=0) + jnp.sum(g_gain_row, axis=0),
            jnp.sum(g_gain_mlp, axis=0),
            jnp.sum(g_gain_final, axis=0),
            jnp.sum(dq.astype(f32), axis=0),
            jnp.sum(g_bias_kv, axis=0),
        ]
    )
    square_part = (
        jnp.sum(g_qkv * g_qkv) + jnp.sum(g_out * g_out) + gu_square + jnp.sum(g_down * g_down) + jnp.sum(embed_square)
    )
    last = jnp.concatenate([small_part, jnp.full((128,), square_part, f32), jnp.zeros((128,), f32)]).reshape(1, -1, 128)
    (last_all,) = gather([last], 14)
    last_all = jnp.sum(last_all.reshape(devices, -1, 128), axis=0)
    g_small = last_all[:small_rows]
    norm = jnp.sqrt(jnp.sum(g_small * g_small) + last_all[small_rows, 0])
    g_small = lax.dynamic_slice_in_dim(g_small, lin * small_params.shape[1], small_params.shape[1], 1)

    g_gu = join(g_gu, feats, units)
    owned_grads = (g_qkv, g_out, g_gu, g_down, embed_grad, g_small)
    clip = jnp.minimum(1.0, CLIP / (norm + 1e-06))
    new_weights, new_firsts, new_seconds, new_lows, clipped_list = ([], [], [], [], [])
    for w, g, m, v in zip(masters, owned_grads, firsts, seconds):
        g = g.astype(f32) * clip
        m_new = MOM1 * m + (1.0 - MOM1) * g
        v_new = MOM2 * v + (1.0 - MOM2) * g * g
        update = m_new / (1.0 - MOM1**STEP) / (jnp.sqrt(v_new / (1.0 - MOM2**STEP)) + EPS_ADAM)
        w_new = w - RATE * (update + DECAY * w)
        new_weights.append(w_new)
        new_firsts.append(m_new)
        new_seconds.append(v_new)
        clipped_list.append(g)
        new_lows.append(w_new.astype(bf16))
    return (
        *new_weights[:5], clipped_list[5], *new_firsts, *new_seconds, *new_lows[:5], norm,
    )


def solution(mesh):
    rows, cols = P(AXES, None), P(None, AXES)
    six = (rows, rows, rows, rows, rows, cols)
    in_specs = (P(), P(), P(), P()) + six * 4
    out_specs = six * 3 + (rows,) * 5 + (P(),)
    return jax.shard_map(body, mesh=mesh, in_specs=in_specs, out_specs=out_specs, check_vma=False)
```

time: 741 us -> 590 us (0.80)
  Pallas kernels: 449 us -> 352 us
  local copies, waits for them, and re-layouts: 95.8 us -> 49.7 us
  other arithmetic: 100 us -> 89.2 us
    pallas_call x5, Pallas kernels: 120 us -> 93.2 us  [reduce(): pl.pallas_call(functools.partial(reduce_kernel, n), out_shape=[jax.ShapeD...]
    pallas_call x1, Pallas kernels: 42.2 us -> 20.2 us  [lookup(): pl.pallas_call(functools.partial(lookup_kernel, block, span), grid=(steps...]
    slice x10 -> x11, local copies, waits for them, and re-layouts: 20.7 us -> 4.05 us  [the longest x1 1.7 us: body(): gu_cols[:, model].reshape(devices * feats_up, 2 * units)]
    another operation x11 -> x1, local copies, waits for them, and re-layouts: 14.3 us -> 0.01 us  [the longest x4 11 us: body(): jnp.stack([gu_weight.astype(bf16), ref_gu])]
    pallas_call x8, Pallas kernels: 156 us -> 142 us  [gather(): pl.pallas_call(functools.partial(gather_kernel, n), out_shape=[jax.ShapeD...]
    pallas_call x1, Pallas kernels: 41.5 us -> 29.9 us  [mix(): pl.pallas_call(mix_kernel, out_shape=[jax.ShapeDtypeStruct((planes, row,...]
    pallas_call x1 -> x3, Pallas kernels: 32.5 us -> 22 us  [the longest x1 18.6 us: table_grad(): pl.pallas_call(functools.partial(table_grad_kernel, block, span), grid=(s...]
    unnamed x165 -> x171, local copies, waits for them, and re-layouts: 22.9 us -> 13.2 us
  transfers between devices with their start and end apart: 3 -> 4, of which waited for: 0 -> 0; matrix products, arithmetic and copies ran while one was open for 15% -> 12% of each run, Pallas kernels for 11% -> 30%
where the time goes in v2:
time: 590 us; the launch traced here: 579 us
  Pallas kernels  352 us (60%)
  other arithmetic  89.2 us (15%)
  matrix products  58.1 us (10%)
  local copies, waits for them, and re-layouts  49.7 us (8%)
  between operations  22.6 us (4%)
  starting transfers between devices  7.06 us (1%)
    pallas_call x8, Pallas kernels, gather(): pl.pallas_call(functools.partial(gather_kernel, n), out_shape=[jax.ShapeD...  142 us
    pallas_call x5, Pallas kernels, reduce(): pl.pallas_call(functools.partial(reduce_kernel, n), out_shape=[jax.ShapeD...  93.2 us
    convert_element_type x5, other arithmetic, body(): new_lows.append(w_new.astype(bf16))  51.1 us
    pallas_call x1, Pallas kernels, mix(): pl.pallas_call(mix_kernel, out_shape=[jax.ShapeDtypeStruct((planes, row,...  29.9 us
    pallas_call x1, Pallas kernels, attend(): pl.pallas_call(functools.partial(attend_kernel, length, rp), grid=(2,), o...  24 us
    pallas_call x1, Pallas kernels, attend_back(): pl.pallas_call(functools.partial(attend_back_kernel, length, rp), grid=(1...  20.4 us
    pallas_call x1, Pallas kernels, lookup(): pl.pallas_call(functools.partial(lookup_kernel, block, span), grid=(steps...  20.2 us
    pallas_call x1, Pallas kernels, table_grad(): pl.pallas_call(functools.partial(table_grad_kernel, block, span), grid=(s...  18.6 us
  transfers between devices with their start and end apart: 4, of which 0 were waited for; matrix products, arithmetic and copies ran while one was open for 12% of the time, Pallas kernels for 30%

profile of v2, /device:TPU:0, one launch (start us, length us, event | category | flops | bytes accessed | tf_op | source)
XLA Modules:
  0.0 578.9 jit_solution(15999467807707389319)
XLA Ops:
  17.4 6.8 %sort.14 = (s32[8192]{0:T(1024)S(1)}, s32[8192]{0:T(1024)}) sort(s32[8192]{0:T(1024)S(1)} %fusion.149, s32[8192]{0:T(1024)S(1)} %iota.84), dimensions={0}, to_apply=%region_1.2 | sort | flops 106496 | bytes 131072 | tf_op jit(solution)/shard_map/sort | solution.py:986
  26.3 20.2 %lookup.1 = (bf16[4748,896]{1,0:T(8,128)(2,1)}, bf16[2,512,896]{2,1,0:T(8,128)(2,1)}, bf16[2,8192,896]{2,1,0:T(8,128)(2,1)}) custom-call(s32[1]{0:T(128)} %bitcast.1.n_ref, s32[8192]{0:T(1024)} %get-tuple-element.279.rows_ref, f32[4748,896]{1,0:T(8,128)} %table_ref.1, bf16[4748,896]{1,0:T(8,128)(2,1)} %frozen_ref.2, s32[64,128]{1,0:T(8,128)} %get-tuple-element.278.flat_ref, ...), custom_call_target="tpu_custom_call" | custom-call | tf_op jit(solution)/shard_map/lookup/pallas_call | solution.py:327
  50.1 28.7 %reduce_1.1 = f32[2,16,896]{2,1,0:T(8,128)S(1)} custom-call(bf16[2,512,896]{2,1,0:T(8,128)(2,1)S(1)} %copy-done.13), custom_call_target="tpu_custom_call" | custom-call | tf_op jit(solution)/shard_map/reduce_1/pallas_call | solution.py:242
  107.0 26.1 %gather_2.1 = (bf16[14,512,128]{2,1,0:T(8,128)(2,1)S(1)}, bf16[1,512,896]{2,1,0:T(8,128)(2,1)S(1)}) custom-call(bf16[14,16,128]{2,1,0:T(8,128)(2,1)S(1)} %bitcast.335, bf16[1,16,896]{2,1,0:T(8,128)(2,1)S(1)} %slice.316.refs_1_), custom_call_target="tpu_custom_call" | custom-call | tf_op jit(solution)/shard_map/gather_2/pallas_call | solution.py:145
  143.5 24.0 %attend.1 = (bf16[14,512,128]{2,1,0:T(8,128)(2,1)}, f32[4,512,128]{2,1,0:T(8,128)}, bf16[2,8192,256]{2,1,0:T(8,128)(2,1)}) custom-call(s32[1]{0:T(128)} %bitcast.1.n_ref, s32[64]{0:T(128)} %and_select_fusion.1.lo_ref, s32[64]{0:T(128)} %fusion.145.hi_ref, bf16[14,512,128]{2,1,0:T(8,128)(2,1)} %copy-done.4, bf16[2,8192,896]{2,1,0:T(8,128)(2,1)} %get-tuple-element.67.x_ref, ...), custom_call_target="tpu_custom_call" | custom-call | tf_op jit(solution)/shard_map/attend/pallas_call | solution.py:490
  167.5 29.9 %mix.1 = (f32[14,16,128]{2,1,0:T(8,128)}, f32[4,16,128]{2,1,0:T(8,128)}) custom-call(bf16[14,512,128]{2,1,0:T(8,128)(2,1)} %get-tuple-element.68.o_ref, f32[4,512,128]{2,1,0:T(8,128)} %get-tuple-element.69.st_ref), custom_call_target="tpu_custom_call" | custom-call | tf_op jit(solution)/shard_map/mix/pallas_call | solution.py:857
  205.0 24.9 %gather_4.1 = (bf16[2,512,1024]{2,1,0:T(8,128)(2,1)S(1)}, bf16[1,512,896]{2,1,0:T(8,128)(2,1)S(1)}) custom-call(bf16[2,16,1024]{2,1,0:T(8,128)(2,1)S(1)} %fusion.46.refs_0_, bf16[1,16,896]{2,1,0:T(8,128)(2,1)S(1)} %slice.326.refs_1_), custom_call_target="tpu_custom_call" | custom-call | tf_op jit(solution)/shard_map/gather_4/pallas_call | solution.py:145
  239.5 15.8 %reduce_5.1 = f32[2,16,896]{2,1,0:T(8,128)S(1)} custom-call(bf16[2,512,896]{2,1,0:T(8,128)(2,1)S(1)} %pad_maximum_fusion.refs_0_), custom_call_target="tpu_custom_call" | custom-call | tf_op jit(solution)/shard_map/reduce_5/pallas_call | solution.py:242
  255.6 16.8 %gather_6.1 = bf16[2,512,896]{2,1,0:T(8,128)(2,1)S(1)} custom-call(bf16[2,16,896]{2,1,0:T(8,128)(2,1)S(1)} %multiply_convert_fusion.1.refs_0_), custom_call_target="tpu_custom_call" | custom-call | tf_op jit(solution)/shard_map/gather_6/pallas_call | solution.py:145
  277.9 7.8 %fusion.195 = (f32[512]{0:T(512)S(1)}, f32[4748,512]{1,0:T(8,128)S(1)}) fusion(bf16[4748,896]{1,0:T(8,128)(2,1)} %get-tuple-element.75, bf16[2,512,896]{2,1,0:T(8,128)(2,1)S(1)} %gather_6.1), kind=kOutput, calls=%fused_computation.361 | convolution fusion | flops 4358739456 | bytes 19151872 | tf_op jit(solution)/shard_map/dot_general | solution.py:1061
  285.8 5.7 fusion.2
  291.5 10.7 %gather_7.1 = f32[1,256,512]{2,1,0:T(8,128)S(1)} custom-call(f32[1,8,512]{2,1,0:T(8,128)S(1)} %bitcast.336), custom_call_target="tpu_custom_call" | custom-call | tf_op jit(solution)/shard_map/gather_7/pallas_call | solution.py:145
  304.4 5.8 fusion.5.dl_ref
  310.2 10.6 %fusion.36.refs_0_ = bf16[1,512,896]{2,1,0:T(8,128)(2,1)S(1)} fusion(bf16[4748,512]{1,0:T(8,128)(2,1)S(1)} %fusion.5.dl_ref, bf16[4748,896]{1,0:T(8,128)(2,1)} %get-tuple-element.75), kind=kOutput, calls=%fused_computation.55 | convolution fusion | flops 4356767744 | bytes 14287872 | tf_op jit(solution)/shard_map/dot_general | solution.py:1094
  320.8 12.4 %reduce_8.1 = f32[1,16,896]{2,1,0:T(8,128)S(1)} custom-call(bf16[1,512,896]{2,1,0:T(8,128)(2,1)S(1)} %fusion.36.refs_0_), custom_call_target="tpu_custom_call" | custom-call | tf_op jit(solution)/shard_map/reduce_8/pallas_call | solution.py:242
  333.4 12.6 %gather_9.1 = bf16[1,512,896]{2,1,0:T(8,128)(2,1)S(1)} custom-call(bf16[1,16,896]{2,1,0:T(8,128)(2,1)S(1)} %multiply_convert_fusion.6.refs_0_), custom_call_target="tpu_custom_call" | custom-call | tf_op jit(solution)/shard_map/gather_9/pallas_call | solution.py:145
  351.6 13.0 %reduce_10.1 = f32[1,16,1024]{2,1,0:T(8,128)S(1)} custom-call(bf16[1,512,1024]{2,1,0:T(8,128)(2,1)S(1)} %fusion.35.refs_0_), custom_call_target="tpu_custom_call" | custom-call | tf_op jit(solution)/shard_map/reduce_10/pallas_call | solution.py:242
  369.8 19.2 %gather_11.1 = (bf16[1,512,896]{2,1,0:T(8,128)(2,1)S(1)}, bf16[7,512,128]{2,1,0:T(8,128)(2,1)S(1)}, f32[1,512,128]{2,1,0:T(8,128)S(1)}) custom-call(bf16[1,16,896]{2,1,0:T(8,128)(2,1)S(1)} %get-tuple-element.243.refs_0_, bf16[7,16,128]{2,1,0:T(8,128)(2,1)S(1)} %bitcast_bitcast_fusion.refs_1_, f32[1,16,128]{2,1,0:T(8,128)S(1)} %maximum_bitcast_fusion.refs_2_), custom_call_target="tpu_custom_call" | custom-call | tf_op jit(solution)/shard_map/gather_11/pallas_call | solution.py:145
  395.8 20.4 %attend_back.1 = (bf16[7,512,128]{2,1,0:T(8,128)(2,1)}, f32[896,256]{1,0:T(8,128)}, f32[8,896]{1,0:T(8,128)}, f32[8,256]{1,0:T(8,128)}, bf16[8192,896]{1,0:T(8,128)(2,1)}) custom-call(s32[1]{0:T(128)} %bitcast.1.n_ref, s32[64]{0:T(128)} %and_select_fusion.1.lo_ref, s32[64]{0:T(128)} %fusion.145.hi_ref, bf16[7,512,128]{2,1,0:T(8,128)(2,1)} %slice.249.q_ref, ...), custom_call_target="tpu_custom_call" | custom-call | tf_op jit(solution)/shard_map/attend_back/pallas_call | solution.py:602
  427.6 23.4 %reduce_12.1 = (f32[7,16,128]{2,1,0:T(8,128)S(1)}, f32[1,32,256]{2,1,0:T(8,128)S(1)}) custom-call(bf16[7,512,128]{2,1,0:T(8,128)(2,1)S(1)} %copy-done.15, f32[1,1024,256]{2,1,0:T(8,128)S(1)} %bitcast.330), custom_call_target="tpu_custom_call" | custom-call | tf_op jit(solution)/shard_map/reduce_12/pallas_call | solution.py:242
  454.8 20.3 %gather_13.1 = (bf16[1,512,896]{2,1,0:T(8,128)(2,1)S(1)}, bf16[1,512,896]{2,1,0:T(8,128)(2,1)S(1)}) custom-call(bf16[1,16,896]{2,1,0:T(8,128)(2,1)S(1)} %convert_element_type.232.refs_0_, bf16[1,16,896]{2,1,0:T(8,128)(2,1)S(1)} %fusion.152.refs_1_), custom_call_target="tpu_custom_call" | custom-call | tf_op jit(solution)/shard_map/gather_13/pallas_call | solution.py:145
  476.0 18.6 %table_grad.1 = (bf16[4748,896]{1,0:T(8,128)(2,1)}, f32[8,896]{1,0:T(8,128)}) custom-call(s32[1]{0:T(128)} %bitcast.1.n_ref, s32[8192]{0:T(1024)} %get-tuple-element.279.rows_ref, bf16[4748,512]{1,0:T(8,128)(2,1)} %copy-done.23, bf16[512,896]{1,0:T(8,128)(2,1)} %slice_bitcast_fusion.2.af_ref, bf16[512,896]{1,0:T(8,128)(2,1)} %bitcast.333, ...), custom_call_target="tpu_custom_call" | custom-call | tf_op jit(solution)/shard_map/table_grad/pallas_call | solution.py:683
  501.5 11.7 %gather_14.1 = f32[1,1024,128]{2,1,0:T(8,128)S(1)} custom-call(f32[1,32,128]{2,1,0:T(8,128)S(1)} %bitcast.338), custom_call_target="tpu_custom_call" | custom-call | tf_op jit(solution)/shard_map/gather_14/pallas_call | solution.py:145
  528.2 42.3 %fusion.178 = (bf16[4748,896]{1,0:T(8,128)(2,1)}, f32[4748,896]{1,0:T(8,128)}, f32[4748,896]{1,0:T(8,128)}, f32[4748,896]{1,0:T(8,128)}) fusion(f32[4748,896]{1,0:T(8,128)} %table_ref.1, f32[]{:T(128)S(6)} %min.3, bf16[4748,896]{1,0:T(8,128)(2,1)} %get-tuple-element.95, f32[4748,896]{1,0:T(8,128)} %param.44, f32[4748,896]{1,0:T(8,128)} %param.50), kind=kLoop, calls=%fused_computation.352 | loop fusion | flops 72321536 | bytes 119117824 | tf_op jit(solution)/shard_map/convert_element_type | solution.py:1187
  (369 shorter events, 128.6 us)
Async XLA Ops:
  7.2 231.1 %copy-start = (bf16[152,896]{1,0:T(8,128)(2,1)S(1)}, bf16[152,896]{1,0:T(8,128)(2,1)}, u32[]{:S(2)}) copy-start(bf16[152,896]{1,0:T(8,128)(2,1)} %param.55) | copy-start | bytes 817156
  7.2 81.1 %all-gather.3.cloned.1.call-start = ((), (), s32[]{:S(2)}) async-start(), calls=%async_computation.2 | async-start | bytes 5406720 | tf_op jit(solution)/shard_map/all_gather | solution.py:974
  12.3 188.0 %all-gather.5.cloned.1.call-start = ((), (), s32[]{:S(2)}) async-start(), calls=%async_computation.3 | async-start | bytes 3784704 | tf_op jit(solution)/shard_map/all_gather | solution.py:1008
  16.2 69.2 %copy-start.56 = (s32[512]{0:T(512)}, s32[512]{0:T(512)S(1)}, u32[]{:S(2)}) copy-start(s32[512]{0:T(512)S(1)} %reshape.622) | copy-start | bytes 6148
  26.3 53.2 %copy-start.44 = (s32[2,4,4,256]{3,2,1,0:T(4,128)S(1)}, s32[2,4,4,256]{3,2,1,0:T(4,128)}, u32[]{:S(2)}) copy-start(s32[2,4,4,256]{3,2,1,0:T(4,128)} %param.30) | copy-start | bytes 98308
  26.3 55.2 %copy-start.72 = (f32[30,4]{0,1:T(4,128)S(1)}, f32[30,4]{0,1:T(4,128)}, u32[]{:S(2)}) copy-start(f32[30,4]{0,1:T(4,128)} %param.51) | copy-start | bytes 1444
  26.3 55.9 %copy-start.73 = (f32[30,4]{0,1:T(4,128)S(1)}, f32[30,4]{0,1:T(4,128)}, u32[]{:S(2)}) copy-start(f32[30,4]{0,1:T(4,128)} %param.45) | copy-start | bytes 1444
  26.3 56.6 %copy-start.2 = (f32[28,9728]{1,0:T(8,128)S(1)}, f32[28,9728]{1,0:T(8,128)}, u32[]{:S(2)}) copy-start(f32[28,9728]{1,0:T(8,128)} %own_ref.1) | copy-start | bytes 3268612
  26.3 56.6 %copy-start.18 = (bf16[28,9728]{1,0:T(8,128)(2,1)S(1)}, bf16[28,9728]{1,0:T(8,128)(2,1)}, u32[]{:S(2)}) copy-start(bf16[28,9728]{1,0:T(8,128)(2,1)} %frozen_ref.3) | copy-start | bytes 1634308
  46.5 39.0 %copy-start.31 = (s32[64,128]{1,0:T(8,128)S(1)}, s32[64,128]{1,0:T(8,128)}, u32[]{:S(2)}) copy-start(s32[64,128]{1,0:T(8,128)} %get-tuple-element.278.flat_ref) | copy-start | bytes 98308
  78.8 125.2 %copy-start.8 = (f32[2,16,896]{2,1,0:T(8,128)}, f32[2,16,896]{2,1,0:T(8,128)S(1)}, u32[]{:S(2)}) copy-start(f32[2,16,896]{2,1,0:T(8,128)S(1)} %reduce_1.1) | copy-start | bytes 344068
  85.5 53.5 %copy-start.68 = (s32[896]{0:T(1024)}, s32[896]{0:T(1024)S(1)}, u32[]{:S(2)}) copy-start(s32[896]{0:T(1024)S(1)} %fusion.166) | copy-start | bytes 10756
  135.3 98.5 %all-to-all-start = ((bf16[32,2,32,304]{3,2,1,0:T(8,128)(2,1)}), bf16[32,2,32,304]{3,2,1,0:T(8,128)(2,1)}, u32[]{:S(2)}, u32[]{:S(2)}) async-start(bf16[32,2,32,304]{3,2,1,0:T(8,128)(2,1)} %spread.1), calls=%async_computation | async-start | bytes 3145728 | tf_op jit(solution)/shard_map/all_to_all | solution.py:1033
  199.2 34.6 %copy-start.53 = (f32[4,16,128]{2,1,0:T(8,128)S(1)}, f32[4,16,128]{2,1,0:T(8,128)}, u32[]{:S(2)}) copy-start(f32[4,16,128]{2,1,0:T(8,128)} %get-tuple-element.71) | copy-start | bytes 98308
  199.4 34.5 %copy-start.40 = (bf16[2,16,896]{2,1,0:T(8,128)(2,1)}, bf16[2,16,896]{2,1,0:T(8,128)(2,1)S(1)}, u32[]{:S(2)}) copy-start(bf16[2,16,896]{2,1,0:T(8,128)(2,1)S(1)} %multiply_convert_fusion.3) | copy-start | bytes 172036
  202.1 70.3 %slice-start = ((s8[8515584]{0:T(1024)(128)(4,1)}), s8[126976]{0:T(1024)(128)(4,1)S(1)}, s32[]{:S(2)}) async-start(s8[8515584]{0:T(1024)(128)(4,1)} %bitcast.339), calls=%async_computation.4 | async-start | bytes 253952
  204.1 161.3 %copy-start.32 = (f32[2,16,896]{2,1,0:T(8,128)}, f32[2,16,896]{2,1,0:T(8,128)S(1)}, u32[]{:S(2)}) copy-start(f32[2,16,896]{2,1,0:T(8,128)S(1)} %get-tuple-element.254) | copy-start | bytes 344068
  235.6 36.8 %slice-start.1 = ((s8[8515584]{0:T(1024)(128)(4,1)}), s8[4194304]{0:T(1024)(128)(4,1)S(1)}, s32[]{:S(2)}) async-start(s8[8515584]{0:T(1024)(128)(4,1)} %bitcast.339), calls=%async_computation.5 | async-start | bytes 8388608
  238.8 33.6 %slice-start.2 = ((s8[8515584]{0:T(1024)(128)(4,1)}), s8[4194304]{0:T(1024)(128)(4,1)S(1)}, s32[]{:S(2)}) async-start(s8[8515584]{0:T(1024)(128)(4,1)} %bitcast.339), calls=%async_computation.6 | async-start | bytes 8388608
  255.5 77.8 %copy-start.64 = (f32[16]{0:T(128)}, f32[16]{0:T(128)S(1)}, u32[]{:S(2)}) copy-start(f32[16]{0:T(128)S(1)} %slice_bitcast_fusion.24) | copy-start | bytes 196
  310.2 35.9 %copy-start.25 = (f32[1,512,304]{1,2,0:T(8,128)S(1)}, f32[1,512,304]{1,2,0:T(8,128)}, u32[]{:S(2)}) copy-start(f32[1,512,304]{1,2,0:T(8,128)} %copy-done.24) | copy-start | bytes 1867780
  310.2 35.9 %copy-start.27 = (f32[152,896]{1,0:T(8,128)S(1)}, f32[152,896]{1,0:T(8,128)}, u32[]{:S(2)}) copy-start(f32[152,896]{1,0:T(8,128)} %param.37) | copy-start | bytes 1634308
  390.9 35.5 %all-to-all-start.1 = ((bf16[32,32,304]{2,1,0:T(8,128)(2,1)}), bf16[32,32,304]{2,1,0:T(8,128)(2,1)}, u32[]{:S(2)}, u32[]{:S(2)}) async-start(bf16[32,32,304]{2,1,0:T(8,128)(2,1)} %bitcast.348), calls=%async_computation.1 | async-start | bytes 1572864 | tf_op jit(solution)/shard_map/all_to_all | solution.py:1125
  528.2 42.3 %copy-start.1 = (bf16[152,896]{1,0:T(8,128)(2,1)S(1)}, bf16[152,896]{1,0:T(8,128)(2,1)}, u32[]{:S(2)}) copy-start(bf16[152,896]{1,0:T(8,128)(2,1)} %param.55) | copy-start | bytes 817156
  (60 other events, 870.9 us)
Sparse Core Ops, SparseCore 0:
  12.4 75.1 all-gather.2
  91.0 75.4 all-gather.4

commit v3 on v2

--- a/solution.py
+++ b/solution.py
@@ -86,15 +86,12 @@
     return copy
 
 
-def gather_kernel(n_arr, *refs):
-    ins, outs = refs[:n_arr], refs[n_arr : 2 * n_arr]
-    send_sems, recv_sems, own_sem = refs[2 * n_arr :]
+def gather_phase(ins, outs, send_sems, recv_sems, own_sem, line, plane, other):
+    n_arr = len(ins)
     _, n_y, n_batch = places()
     half, y, core, batch = coords()
     n_plane = 2 * n_y
     spot = half * n_y + y
-    line, plane, other = peers()
-    greet(line, plane, other)
     slots = iter(range(n_arr * (n_batch - 1 + n_plane * n_batch + (n_plane - 1) * n_batch)))
 
     def rows(i, where, j):
@@ -136,6 +133,13 @@
         copy.wait_send()
 
 
+def gather_kernel(n_arr, *refs):
+    ins, outs = refs[:n_arr], refs[n_arr : 2 * n_arr]
+    line, plane, other = peers()
+    greet(line, plane, other)
+    gather_phase(ins, outs, *refs[2 * n_arr :], line, plane, other)
+
+
 def gather(arrays, cid, vmem=48):
     _, n_y, n_batch = places()
     n_plane = 2 * n_y
@@ -159,16 +163,12 @@
     )(*arrays)
 
 
-def reduce_kernel(n_arr, *refs):
-    ins, outs = refs[:n_arr], refs[n_arr : 2 * n_arr]
-    scr = refs[2 * n_arr : 7 * n_arr]
-    send_sems, recv_sems = refs[7 * n_arr :]
+def reduce_phase(ins, outs, scr, send_sems, recv_sems, line, plane, other):
+    n_arr = len(ins)
     _, n_y, n_batch = places()
     half, y, core, batch = coords()
     n_plane = 2 * n_y
     spot = half * n_y + y
-    line, plane, other = peers()
-    greet(line, plane, other)
     f32 = jnp.float32
     slots = iter(range(n_arr * (n_plane * n_batch + (n_plane - 1) * n_batch + n_batch - 1)))
     order = list(range(1, n_batch)) + [0]
@@ -222,35 +222,85 @@
             copy.wait_send()
 
 
-def reduce(arrays, cid, vmem=48):
+def reduce_scratch(arrays):
+    _, n_y, n_batch = places()
+    n_plane = 2 * n_y
+    scratch = []
+    for a in arrays:
+        m, rows, w = a.shape
+        size = rows // (2 * n_plane * n_batch)
+        for lead in ((n_plane, n_batch), (n_plane - 1, n_batch), (n_plane - 1, n_batch), (n_batch - 1,), (n_batch - 1,)):
+            scratch.append(pltpu.VMEM(lead + (m, size, w), a.dtype))
+    return scratch
+
+
+def exchange_kernel(n_in, columns, n_const, n_out, n_extra, reducer, compute, *refs):
+    refs = list(refs)
+
+    def take(n):
+        part = refs[:n]
+        del refs[:n]
+        return part
+
+    n_fetch = len(columns)
+    ins, sources, consts, outs, extras = take(n_in), take(n_fetch), take(n_const), take(n_out), take(n_extra)
+    totals, staged, fetched = take(n_in), take(n_out), take(n_fetch)
+    send_one, recv_one, send_two, recv_two, own_sem, fetch_sem = refs[-6:]
+    line, plane, other = peers()
+    copies = []
+    for k, (first, width) in enumerate(columns):
+        copy = pltpu.make_async_copy(sources[k].at[:, pl.ds(first, width)], fetched[k], fetch_sem.at[k])
+        copy.start()
+        copies.append(copy)
+    greet(line, plane, other)
+    if ins:
+        reducer(ins, totals, refs[:-6], send_one, recv_one, line, plane, other)
+    for copy in copies:
+        copy.wait()
+    compute(totals, fetched + consts, staged, extras)
+    if outs:
+        gather_phase(staged, outs, send_two, recv_two, own_sem, line, plane, other)
+
+
+def exchange(name, cid, arrays, fetches, consts, compute, gathered, extras, reducer=reduce_phase):
     _, n_y, n_batch = places()
     n_plane = 2 * n_y
     total = 2 * n_plane * n_batch
-    n = len(arrays)
-    copies = n * (n_plane * n_batch + (n_plane - 1) * n_batch + n_batch - 1)
-    scratch = []
-    for a in arrays:
-        m, rows, w = a.shape
-        size = rows // total
-        scratch += [
-            pltpu.VMEM((n_plane, n_batch, m, size, w), a.dtype),
-            pltpu.VMEM((n_plane - 1, n_batch, m, size, w), a.dtype),
-            pltpu.VMEM((n_plane - 1, n_batch, m, size, w), a.dtype),
-            pltpu.VMEM((n_batch - 1, m, size, w), a.dtype),
-            pltpu.VMEM((n_batch - 1, m, size, w), a.dtype),
-        ]
+    f32 = jnp.float32
+    n_in, n_out = len(arrays), len(gathered)
+    one = max(1, n_in) * (n_plane * n_batch + (n_plane - 1) * n_batch + n_batch - 1)
+    two = max(1, n_out) * (n_batch - 1 + (n_plane - 1) * n_batch + n_plane * n_batch)
+    vm = pl.BlockSpec(memory_space=pltpu.VMEM)
+    dma = pltpu.SemaphoreType.DMA
+    columns = tuple((first, width) for _, first, width in fetches)
     return pl.pallas_call(
-        functools.partial(reduce_kernel, n),
-        out_shape=[jax.ShapeDtypeStruct((a.shape[0], a.shape[1] // total, a.shape[2]), jnp.float32) for a in arrays],
-        in_specs=[pl.BlockSpec(memory_space=pltpu.VMEM)] * n,
-        out_specs=[pl.BlockSpec(memory_space=pltpu.VMEM)] * n,
-        scratch_shapes=scratch
-        + [pltpu.SemaphoreType.DMA((copies,)), pltpu.SemaphoreType.DMA((copies,))],
-        compiler_params=pltpu.CompilerParams(
-            collective_id=cid, has_side_effects=True, vmem_limit_bytes=vmem * 2**20
+        functools.partial(
+            exchange_kernel, n_in, columns, len(consts), n_out, len(extras), reducer, compute
         ),
-        name=f"reduce_{cid}",
-    )(*arrays)
+        out_shape=[jax.ShapeDtypeStruct((m, rows * total, w), t) for m, rows, w, t in gathered]
+        + [jax.ShapeDtypeStruct(shape, t) for shape, t in extras],
+        in_specs=[vm] * n_in + [pl.BlockSpec(memory_space=pl.ANY)] * len(fetches) + [vm] * len(consts),
+        out_specs=[vm] * (n_out + len(extras)),
+        scratch_shapes=[pltpu.VMEM((a.shape[0], a.shape[1] // total, a.shape[2]), f32) for a in arrays]
+        + [pltpu.VMEM((m, rows, w), t) for m, rows, w, t in gathered]
+        + [pltpu.VMEM((a.shape[0], width), a.dtype) for a, _, width in fetches]
+        + reduce_scratch(arrays)
+        + [dma((one,)), dma((one,)), dma((two,)), dma((two,)), dma((max(1, n_out),)), dma((max(1, len(fetches)),))],
+        compiler_params=pltpu.CompilerParams(collective_id=cid, has_side_effects=True, vmem_limit_bytes=60 * 2**20),
+        name=name,
+    )(*arrays, *[a for a, _, _ in fetches], *consts)
+
+
+def norm_forward(x, gain):
+    scale = lax.rsqrt(jnp.mean(x * x, axis=-1, keepdims=True) + EPS_NORM)
+    return (x * scale * gain, scale)
+
+
+def norm_backward(d_out, x, scale, gain):
+    d_gain = d_out * x * scale
+    d_hat = d_out * gain
+    d_x = scale * (d_hat - x * scale * scale * jnp.mean(d_hat * x, axis=-1, keepdims=True))
+    return (d_x, d_gain)
 
 
 HEAD_SLOTS = (0, 2, 4, 6, 1, 3, 5, 8, 10, 12, 7, 9, 11, 13)
@@ -302,17 +352,30 @@
                 return 0
 
             lax.fori_loop(0, TILE // 8, eight, 0)
-            staged[...] = rough[...].astype(bf16)
-            copy = pltpu.make_async_copy(staged, x_ref.at[:, pl.ds(pl.multiple_of(i * TILE, TILE), TILE), :], sem)
+            slot = lax.rem(i, 2)
+            where = pl.ds(pl.multiple_of(i * TILE, TILE), TILE)
+            copy = pltpu.make_async_copy(staged.at[slot], x_ref.at[:, where, :], sem.at[slot])
+
+            @pl.when(i >= 2)
+            def _():
+                copy.wait()
+
+            staged[slot] = rough[...].astype(bf16)
             copy.start()
             match = frow_ref[...] == jnp.broadcast_to(flat_ref[pl.ds(i, 1), :], (n_rows, TILE))
             match = jnp.where(match, 1.0, 0.0).astype(bf16)
             for model in range(2):
-                picked_ref[model] = picked_ref[model] + straight(match, staged[model]).astype(bf16)
-            copy.wait()
+                picked_ref[model] = picked_ref[model] + straight(match, staged[slot, model]).astype(bf16)
             return 0
 
-        lax.fori_loop(0, (n_ref[0] + TILE - 1) // TILE, tile, 0)
+        tiles = (n_ref[0] + TILE - 1) // TILE
+        lax.fori_loop(0, tiles, tile, 0)
+        for k in range(2):
+
+            @pl.when(tiles > k)
+            def _():
+                where = pl.ds(0, TILE)
+                pltpu.make_async_copy(staged.at[k], x_ref.at[:, where, :], sem.at[k]).wait()
 
 
 def lookup(n_local, rows, table, frozen, flat, frow):
@@ -348,8 +411,8 @@
         scratch_shapes=[
             pltpu.VMEM((2, steps * span, width), jnp.float32),
             pltpu.VMEM((2, TILE, width), jnp.float32),
-            pltpu.VMEM((2, TILE, width), bf16),
-            pltpu.SemaphoreType.DMA,
+            pltpu.VMEM((2, 2, TILE, width), bf16),
+            pltpu.SemaphoreType.DMA((2,)),
         ],
         compiler_params=pltpu.CompilerParams(vmem_limit_bytes=60 * 2**20),
         name="lookup",
@@ -524,16 +587,38 @@
     gs_ref[...] = jnp.zeros_like(gs_ref)
     gb_ref[...] = jnp.zeros_like(gb_ref)
 
+    tiles = (n_ref[0] + TILE - 1) // TILE
+
+    def fetch(i):
+        slot = lax.rem(i, 2)
+        at = pl.ds(pl.multiple_of(i * TILE, TILE), TILE)
+        return (
+            pltpu.make_async_copy(x_ref.at[0, at, :], xbuf.at[slot], sem.at[slot]),
+            pltpu.make_async_copy(kv_ref.at[0, at, :], kvbuf.at[slot], sem.at[2 + slot]),
+        )
+
+    def leave(i):
+        slot = lax.rem(i, 2)
+        at = pl.ds(pl.multiple_of(i * TILE, TILE), TILE)
+        return pltpu.make_async_copy(dxbuf.at[slot], dx_ref.at[at, :], sem.at[4 + slot])
+
+    @pl.when(tiles > 0)
+    def _():
+        for copy in fetch(0):
+            copy.start()
+
     def tile(i, _):
-        at = pl.ds(pl.multiple_of(i * TILE, TILE), TILE)
-        one = pltpu.make_async_copy(x_ref.at[0, at, :], xbuf, sem.at[0])
-        one.start()
-        two = pltpu.make_async_copy(kv_ref.at[0, at, :], kvbuf, sem.at[1])
-        two.start()
-        one.wait()
-        two.wait()
-        keys = head_pieces(kvbuf[:, :128].astype(f32), lane)
-        values = head_pieces(kvbuf[:, 128:].astype(f32), lane)
+        slot = lax.rem(i, 2)
+
+        @pl.when(i + 1 < tiles)
+        def _():
+            for copy in fetch(i + 1):
+                copy.start()
+
+        for copy in fetch(i):
+            copy.wait()
+        keys = head_pieces(kvbuf[slot, :, :128].astype(f32), lane)
+        values = head_pieces(kvbuf[slot, :, 128:].astype(f32), lane)
         flat = flat_ref[pl.ds(i, 1), :]
         dk_scr[...] = jnp.zeros_like(dk_scr)
         dv_scr[...] = jnp.zeros_like(dv_scr)
@@ -571,7 +656,7 @@
 
         d_key = turn(joined(dk_scr) * HEAD_SIZE ** (-0.5), column(pos_ref[pl.ds(i, 1), :]), freq_ref[...], lane, -1.0)
         d_mixed = jnp.concatenate([d_key, joined(dv_scr)], axis=1).astype(bf16)
-        x = xbuf[...].astype(f32)
+        x = xbuf[slot].astype(f32)
         scale = lax.rsqrt(jnp.mean(x * x, axis=-1, keepdims=True) + EPS_NORM)
         gain = gain_ref[0]
         normed = (x * scale * gain).astype(bf16)
@@ -581,13 +666,22 @@
         gs_ref[...] += jnp.sum((d_normed * x * scale).reshape(TILE // 8, 8, x.shape[1]), axis=0)
         d_hat = d_normed * gain
         d_x = scale * (d_hat - x * scale * scale * jnp.mean(d_hat * x, axis=-1, keepdims=True))
-        dxbuf[...] = d_x.astype(bf16)
-        out = pltpu.make_async_copy(dxbuf, dx_ref.at[at, :], sem.at[2])
-        out.start()
-        out.wait()
+
+        @pl.when(i >= 2)
+        def _():
+            leave(i - 2).wait()
+
+        dxbuf[slot] = d_x.astype(bf16)
+        leave(i).start()
         return 0
 
-    lax.fori_loop(0, (n_ref[0] + TILE - 1) // TILE, tile, 0)
+    lax.fori_loop(0, tiles, tile, 0)
+    for k in range(2):
+
+        @pl.when(tiles > k)
+        def _():
+            leave(tiles - 1 - k).wait()
+
     dq_ref[...] = (dq_scr[...] * HEAD_SIZE ** (-0.5)).astype(bf16)
 
 
@@ -618,13 +712,13 @@
             whole((PAIRS, n_rows, 128)), whole((width, 256)), whole((8, width)), whole((8, 256)), anyw,
         ],
         scratch_shapes=[
-            pltpu.VMEM((TILE, width), bf16),
-            pltpu.VMEM((TILE, 256), bf16),
-            pltpu.VMEM((TILE, width), bf16),
+            pltpu.VMEM((2, TILE, width), bf16),
+            pltpu.VMEM((2, TILE, 256), bf16),
+            pltpu.VMEM((2, TILE, width), bf16),
             pltpu.VMEM((PAIRS, n_rows, 128), f32),
             pltpu.VMEM((4, TILE, 128), f32),
             pltpu.VMEM((4, TILE, 128), f32),
-            pltpu.SemaphoreType.DMA((3,)),
+            pltpu.SemaphoreType.DMA((6,)),
         ],
         compiler_params=pltpu.CompilerParams(vmem_limit_bytes=60 * 2**20),
         name="attend_back",
@@ -644,15 +738,28 @@
         added[...] = jnp.zeros_like(added)
         n_rows = drow_ref.shape[0]
 
+        tiles = (n_ref[0] + TILE - 1) // TILE
+
+        def fetch(i):
+            slot = lax.rem(i, 2)
+            at = pl.ds(pl.multiple_of(i * TILE, TILE), TILE)
+            return pltpu.make_async_copy(dx_ref.at[at, :], moved.at[slot], sem.at[slot])
+
+        @pl.when(tiles > 0)
+        def _():
+            fetch(0).start()
+
         def tile(i, _):
-            copy = pltpu.make_async_copy(dx_ref.at[pl.ds(pl.multiple_of(i * TILE, TILE), TILE), :], moved, sem)
-            copy.start()
+            @pl.when(i + 1 < tiles)
+            def _():
+                fetch(i + 1).start()
+
             token = column(flat_ref[pl.ds(i, 1), :])
             token = jnp.concatenate([token] * (n_rows // 128), axis=1)
             match = jnp.where(token == jnp.broadcast_to(frow_ref[...], (TILE, n_rows)), 1.0, 0.0).astype(bf16)
             own = straight(match, drow_ref[...])
-            copy.wait()
-            rough[...] = own + moved[...].astype(f32)
+            fetch(i).wait()
+            rough[...] = own + moved[lax.rem(i, 2)].astype(f32)
 
             def eight(k, _):
                 for j in range(8):
@@ -664,7 +771,7 @@
             lax.fori_loop(0, TILE // 8, eight, 0)
             return 0
 
-        lax.fori_loop(0, (n_ref[0] + TILE - 1) // TILE, tile, 0)
+        lax.fori_loop(0, tiles, tile, 0)
 
     inside = step * span + lax.broadcasted_iota(jnp.int32, (span, 1), 0) < block
     logit = jnp.where(inside, dl_ref[...].astype(f32), 0.0).astype(bf16)
@@ -696,9 +803,9 @@
         out_specs=[pl.BlockSpec((span, width), lambda i: (i, 0)), whole((8, width))],
         scratch_shapes=[
             pltpu.VMEM((steps * span, width), jnp.float32),
-            pltpu.VMEM((TILE, width), jnp.bfloat16),
+            pltpu.VMEM((2, TILE, width), jnp.bfloat16),
             pltpu.VMEM((TILE, width), jnp.float32),
-            pltpu.SemaphoreType.DMA,
+            pltpu.SemaphoreType.DMA((2,)),
         ],
         compiler_params=pltpu.CompilerParams(vmem_limit_bytes=56 * 2**20),
         name="table_grad",
@@ -748,6 +855,95 @@
         compiler_params=pltpu.CompilerParams(vmem_limit_bytes=48 * 2**20),
         name="join",
     )(g)
+
+
+def head_kernel(block, span, own_ref, frozen_ref, af_ref, aim_ref, st_ref, logit_ref):
+    step = pl.program_id(0)
+    f32 = jnp.float32
+    n_rows = af_ref.shape[1]
+
+    @pl.when(step == 0)
+    def _():
+        st_ref[...] = jnp.zeros_like(st_ref)
+        for model in range(2):
+            st_ref[3 * model : 3 * model + 1, :] = jnp.full((1, n_rows), -1e30, f32)
+
+    row = step * span + lax.broadcasted_iota(jnp.int32, (span, n_rows), 0)
+    hit = (row == aim_ref[...]) & (row < block)
+    for model, ref in enumerate((own_ref, frozen_ref)):
+        logit = jnp.where(row < block, last_last(ref[...], af_ref[model]), -1e30)
+        if model == 0:
+            logit_ref[...] = logit
+        top, total, found = (pl.ds(3 * model + k, 1) for k in range(3))
+        new = jnp.maximum(st_ref[top, :], jnp.max(logit, axis=0, keepdims=True))
+        fall = jnp.exp(st_ref[top, :] - new)
+        st_ref[total, :] = st_ref[total, :] * fall + jnp.sum(jnp.exp(logit - new), axis=0, keepdims=True)
+        st_ref[top, :] = new
+        st_ref[found, :] += jnp.sum(jnp.where(hit, logit, 0.0), axis=0, keepdims=True)
+
+
+def head(own, frozen, af, aim):
+    block, width = own.shape
+    n_rows = af.shape[1]
+    span = 512
+    whole = lambda shape: pl.BlockSpec(shape, lambda i: (0,) * len(shape))
+    return pl.pallas_call(
+        functools.partial(head_kernel, block, span),
+        grid=(pl.cdiv(block, span),),
+        out_shape=[jax.ShapeDtypeStruct((8, n_rows), jnp.float32), jax.ShapeDtypeStruct((block, n_rows), jnp.float32)],
+        in_specs=[
+            pl.BlockSpec((span, width), lambda i: (i, 0)), pl.BlockSpec((span, width), lambda i: (i, 0)),
+            whole(af.shape), whole(aim.shape),
+        ],
+        out_specs=[whole((8, n_rows)), pl.BlockSpec((span, n_rows), lambda i: (i, 0))],
+        compiler_params=pltpu.CompilerParams(vmem_limit_bytes=56 * 2**20),
+        name="head",
+    )(own, frozen, af, aim)
+
+
+def head_back_kernel(block, span, logit_ref, own_ref, lse_ref, dlp_ref, aim_ref, dl_ref, d_af_ref, acc):
+    step = pl.program_id(0)
+    f32, bf16 = jnp.float32, jnp.bfloat16
+
+    @pl.when(step == 0)
+    def _():
+        acc[...] = jnp.zeros_like(acc)
+
+    row = step * span + lax.broadcasted_iota(jnp.int32, logit_ref.shape, 0)
+    hot = jnp.where(row == aim_ref[...], 1.0, 0.0)
+    d_logit = dlp_ref[...] * (hot - jnp.exp(logit_ref[...] - lse_ref[...]))
+    d_logit = jnp.where(row < block, d_logit, 0.0).astype(bf16)
+    dl_ref[...] = d_logit
+    inside = step * span + lax.broadcasted_iota(jnp.int32, (span, 1), 0) < block
+    table = jnp.where(inside, own_ref[...].astype(f32), 0.0).astype(bf16)
+    acc[...] += first_first(d_logit, table)
+
+    @pl.when(step == pl.num_programs(0) - 1)
+    def _():
+        d_af_ref[0] = acc[...].astype(bf16)
+
+
+def head_back(logits, own, lse, dlp, aim):
+    block, width = own.shape
+    n_rows = logits.shape[1]
+    span = 512
+    whole = lambda shape: pl.BlockSpec(shape, lambda i: (0,) * len(shape))
+    return pl.pallas_call(
+        functools.partial(head_back_kernel, block, span),
+        grid=(pl.cdiv(block, span),),
+        out_shape=[
+            jax.ShapeDtypeStruct((block, n_rows), jnp.bfloat16),
+            jax.ShapeDtypeStruct((1, n_rows, width), jnp.bfloat16),
+        ],
+        in_specs=[
+            pl.BlockSpec((span, n_rows), lambda i: (i, 0)), pl.BlockSpec((span, width), lambda i: (i, 0)),
+            whole(lse.shape), whole(dlp.shape), whole(aim.shape),
+        ],
+        out_specs=[pl.BlockSpec((span, n_rows), lambda i: (i, 0)), whole((1, n_rows, width))],
+        scratch_shapes=[pltpu.VMEM((n_rows, width), jnp.float32)],
+        compiler_params=pltpu.CompilerParams(vmem_limit_bytes=56 * 2**20),
+        name="head_back",
+    )(logits, own, lse, dlp, aim)
 
 
 def blend(parts, lane):
@@ -771,14 +967,13 @@
     return planes, stats
 
 
-def mix_kernel(o_ref, st_ref, oo_ref, so_ref, *rest):
-    core_o, core_s, sum_o, sum_s, plane_o, plane_s, keep_o, keep_s, line_o, line_s, send_sems, recv_sems = rest
+def mix_phase(ins, outs, scr, send_sems, recv_sems, line, plane, other):
+    (o_ref, st_ref), (oo_ref, so_ref) = ins, outs
+    core_o, sum_o, plane_o, keep_o, line_o, core_s, sum_s, plane_s, keep_s, line_s = scr
     _, n_y, n_batch = places()
     half, y, core, batch = coords()
     n_plane = 2 * n_y
     spot = half * n_y + y
-    line, plane, other = peers()
-    greet(line, plane, other)
     size = oo_ref.shape[1]
     lane = lax.broadcasted_iota(jnp.int32, (size, 128), 1)
     order = list(range(1, n_batch)) + [0]
@@ -825,12 +1020,14 @@
             for copy in by_plane[p, j]:
                 copy.wait_recv()
             parts.append((plane_o[p, j], plane_s[p, j]))
-        store(keep_o.at[j], keep_s.at[j], blend(parts, lane))
+        merged = blend(parts, lane)
         if j:
+            store(keep_o.at[j - 1], keep_s.at[j - 1], merged)
             by_line[j] = (
-                send(keep_o.at[j], line_o.at[j - 1], line[j - 1][0]), send(keep_s.at[j], line_s.at[j - 1], line[j - 1][0])
+                send(keep_o.at[j - 1], line_o.at[j - 1], line[j - 1][0]),
+                send(keep_s.at[j - 1], line_s.at[j - 1], line[j - 1][0]),
             )
-    parts = [(keep_o[0], keep_s[0])]
+    parts = [merged]
     for j in range(1, n_batch):
         for copy in by_line[j]:
             copy.wait_recv()
@@ -842,71 +1039,133 @@
                 copy.wait_send()
 
 
-def mix(o, stats, cid):
-    _, n_y, n_batch = places()
-    n_plane = 2 * n_y
-    planes, all_rows, _ = o.shape
-    ns = stats.shape[0]
-    bf16, f32 = jnp.bfloat16, jnp.float32
-    copies = 2 * (n_plane * n_batch + (n_plane - 1) * n_batch + n_batch - 1)
-    row = all_rows // (2 * n_plane * n_batch)
-    vm = pl.BlockSpec(memory_space=pltpu.VMEM)
-    scratch = []
-    for lead in ((n_plane, n_batch), (n_plane - 1, n_batch), (n_plane - 1, n_batch), (n_batch,), (n_batch - 1,)):
-        scratch += [pltpu.VMEM(lead + (planes, row, 128), bf16), pltpu.VMEM(lead + (ns, row, 128), f32)]
-    return pl.pallas_call(
-        mix_kernel,
-        out_shape=[
-            jax.ShapeDtypeStruct((planes, row, 128), f32),
-            jax.ShapeDtypeStruct((ns, row, 128), f32),
-        ],
-        in_specs=[vm] * 2,
-        out_specs=[vm] * 2,
-        scratch_shapes=scratch + [pltpu.SemaphoreType.DMA((copies,)), pltpu.SemaphoreType.DMA((copies,))],
-        compiler_params=pltpu.CompilerParams(collective_id=cid, has_side_effects=True, vmem_limit_bytes=56 * 2**20),
-        name="mix",
-    )(o, stats)
+def low(x):
+    return x.astype(jnp.bfloat16)
+
+
+def split_dot(x, w):
+    high = low(x)
+    return straight(high, w) + straight(low(x - high.astype(jnp.float32)), w)
+
+
+def turn_rows(x, cosine, sine, sign):
+    lane = lax.broadcasted_iota(jnp.int32, x.shape, 1)
+    mixed = jnp.where(lax.rem(lane, 64) < 32, -sign * pltpu.roll(x, 96, 1), sign * pltpu.roll(x, 32, 1))
+    return x * cosine + mixed * sine
+
+
+def queries(totals, consts, staged, extras):
+    w_one, w_two, places_ref, gain_ref, bias_ref, cosine_ref, sine_ref, x_ref = consts
+    q_ref, a1_ref = staged
+    for model, w_ref in enumerate((w_one, w_two)):
+        normed, _ = norm_forward(x_ref[model], gain_ref[model])
+        normed = low(normed)
+        if model == 0:
+            a1_ref[0] = normed
+        mixed = straight(low(straight(normed, places_ref[...])), w_ref[...]) + bias_ref[model]
+        for p in range(PAIRS):
+            part = turn_rows(mixed[:, 128 * p : 128 * p + 128], cosine_ref[...], sine_ref[...], 1.0)
+            q_ref[model * PAIRS + p] = low(part)
+
+
+def attended(totals, consts, staged, extras):
+    w_one, w_two, places_ref, gain_ref, x_ref = consts
+    a2_ref, o_ref = staged
+    x1_ref, own_ref, lse_ref = extras
+    lane = lax.broadcasted_iota(jnp.int32, (own_ref.shape[0], 128), 1)
+    for model, w_ref in enumerate((w_one, w_two)):
+        total = totals[1][2 * model + 1]
+        total = jnp.where(lane < QUERY_HEADS, total, 1.0)
+        if model == 0:
+            lse_ref[...] = totals[1][0] + jnp.log(total)
+        share = 1.0 / total
+        parts = []
+        for p in range(PAIRS):
+            each = jnp.where(lane < 64, share[:, 2 * p : 2 * p + 1], share[:, 2 * p + 1 : 2 * p + 2])
+            parts.append(low(totals[0][model * PAIRS + p] * each))
+        o = jnp.concatenate(parts, axis=1)
+        if model == 0:
+            o_ref[0] = o
+            own_ref[...] = o
+        x1 = x_ref[model] + straight(low(straight(o, places_ref[...])), w_ref[...])
+        x1_ref[model] = x1
+        a2, _ = norm_forward(x1, gain_ref[model])
+        a2_ref[model] = low(straight(low(a2), places_ref[...]))
+
+
+def finals(totals, consts, staged, extras):
+    gain_ref, x1_ref = consts
+    for model in range(2):
+        x2 = x1_ref[model] + totals[0][model]
+        extras[0][model] = x2
+        af, _ = norm_forward(x2, gain_ref[model])
+        staged[0][model] = low(af)
+
+
+def scale_of(x):
+    return lax.rsqrt(jnp.mean(x * x, axis=-1, keepdims=True) + EPS_NORM)
+
+
+def finals_back(totals, consts, staged, extras):
+    gain_ref, x2_ref = consts
+    x2 = x2_ref[0]
+    d_out, d_gain = norm_backward(totals[0][0], x2, scale_of(x2), gain_ref[0])
+    staged[0][0] = low(d_out)
+    extras[0][...] = d_out
+    extras[1][...] = jnp.sum(d_gain, axis=0, keepdims=True)
+
+
+def attended_back(totals, consts, staged, extras):
+    w_ref, from_ref, gain_ref, x1_ref, d_out_ref, o_ref, lse_ref = consts
+    d_attn_ref, d_o_ref, stats_ref = staged
+    d_mid_ref, d_gain_ref = extras
+    x1 = x1_ref[0]
+    d_mid, d_gain = norm_backward(split_dot(totals[0][0], from_ref[...]), x1, scale_of(x1), gain_ref[0])
+    d_mid = d_mid + d_out_ref[...]
+    d_mid_ref[...] = d_mid
+    d_gain_ref[...] = jnp.sum(d_gain, axis=0, keepdims=True)
+    d_attn = low(d_mid)
+    d_attn_ref[0] = d_attn
+    d_o = low(straight(low(last_last(d_attn, w_ref[...])), from_ref[...]))
+    product = d_o.astype(jnp.float32) * o_ref[...].astype(jnp.float32)
+    lane = lax.broadcasted_iota(jnp.int32, (d_o.shape[0], 128), 1)
+    stats = jnp.where(lane < QUERY_HEADS, lse_ref[...], 0.0)
+    for p in range(PAIRS):
+        d_o_ref[p] = d_o[:, 128 * p : 128 * p + 128]
+        part = product[:, 128 * p : 128 * p + 128]
+        first = jnp.sum(jnp.where(lane < 64, part, 0.0), axis=-1, keepdims=True)
+        second = jnp.sum(jnp.where(lane < 64, 0.0, part), axis=-1, keepdims=True)
+        stats = jnp.where(lane == 16 + 2 * p, first, stats)
+        stats = jnp.where(lane == 17 + 2 * p, second, stats)
+    stats_ref[0] = stats
+
+
+def queries_back(totals, consts, staged, extras):
+    w_ref, from_ref, gain_ref, x_ref, d_mid_ref, cosine_ref, sine_ref = consts
+    dq_ref, d_row_ref = staged
+    g_kv_ref, d_gain_ref, d_bias_ref = extras
+    g_kv_ref[...] = totals[1][0]
+    parts = [turn_rows(totals[0][p], cosine_ref[...], sine_ref[...], -1.0) for p in range(PAIRS)]
+    dq = low(jnp.concatenate(parts, axis=1))
+    dq_ref[0] = dq
+    d_bias_ref[...] = jnp.sum(dq.astype(jnp.float32), axis=0, keepdims=True)
+    x = x_ref[0]
+    d_row, d_gain = norm_backward(split_dot(last_last(dq, w_ref[...]), from_ref[...]), x, scale_of(x), gain_ref[0])
+    d_row_ref[0] = low(d_row + d_mid_ref[...])
+    d_gain_ref[...] = jnp.sum(d_gain, axis=0, keepdims=True)
+
+
+def keep(totals, consts, staged, extras):
+    for total, extra in zip(totals, extras):
+        extra[...] = total[...]
 
 
 AXES = ("half", "mp", "batch")
-
-
-def norm_forward(x, gain):
-    scale = lax.rsqrt(jnp.mean(x * x, axis=-1, keepdims=True) + EPS_NORM)
-    return (x * scale * gain, scale)
-
-
-def norm_backward(d_out, x, scale, gain):
-    d_gain = d_out * x * scale
-    d_hat = d_out * gain
-    d_x = scale * (d_hat - x * scale * scale * jnp.mean(d_hat * x, axis=-1, keepdims=True))
-    return (d_x, d_gain)
 
 
 def frequencies():
     half_size = HEAD_SIZE // 2
     return THETA ** (-(jnp.arange(half_size, dtype=jnp.float32) * 2.0) / HEAD_SIZE)
-
-
-def rotate(x, cosine, sine, sign):
-    half_size = HEAD_SIZE // 2
-    first, second = x[..., :half_size], x[..., half_size:]
-    return jnp.concatenate(
-        [first * cosine - sign * second * sine, second * cosine + sign * first * sine], axis=-1
-    )
-
-
-def to_pairs(x):
-    lead, rows = x.shape[:-2], x.shape[-2]
-    x = x.reshape(lead + (rows, PAIRS, 128))
-    x = jnp.moveaxis(x, -2, -3)
-    return x.reshape((-1, rows, 128))
-
-
-def from_pairs(x, models):
-    rows = x.shape[1]
-    x = x.reshape(models, PAIRS, rows, 128)
-    return jnp.moveaxis(x, 1, 2).reshape(models, rows, MODEL_WIDTH)
 
 
 def bmm(x, w):
@@ -948,15 +1207,6 @@
     to_order = (padded[None, :] == (feat // feats * feats_up + feat % feats)[:, None]).astype(bf16)
     from_order = (padded[:, None] == (feat // feats * feats_up + feat % feats)[None, :]).astype(bf16)
 
-    def pad_feats(x):
-        return jnp.dot(x, to_order, preferred_element_type=f32).astype(bf16)
-
-    def cut_feats(x):
-        high = x.astype(bf16)
-        both = jnp.concatenate([high, (x - high.astype(f32)).astype(bf16)], axis=0)
-        both = jnp.dot(both, from_order, preferred_element_type=f32)
-        return both[: x.shape[0]] + both[x.shape[0] :]
-
     def placed(x):
         x = jnp.pad(x.astype(bf16), ((0, 0), (0, 128 - x.shape[1])))
         x = jnp.roll(x, lin * small_params.shape[1], axis=1)
@@ -973,7 +1223,6 @@
     smalls = [x.reshape(tall, feats_up, 128)[k] for x in smalls for k in range(tall)]
     early = lax.all_gather(jnp.concatenate([early] + smalls, axis=1), AXES, axis=0, tiled=True)
     at_small = 2 * QKV
-    w_q = (early[:, :MODEL_WIDTH], early[:, MODEL_WIDTH : 2 * MODEL_WIDTH])
     down_low = jnp.stack([down_weight.astype(bf16), ref_down])
 
     ids = tokens.transpose(0, 2, 1, 3).reshape(rollouts, length)
@@ -1006,8 +1255,8 @@
     out_both = to_up(jnp.concatenate([out_weight.astype(bf16), ref_out], axis=1))
     picked, out_both = lax.optimization_barrier((picked, out_both))
     late = lax.all_gather(out_both, AXES, axis=0, tiled=True)
-    w_out = (late[:, :MODEL_WIDTH], late[:, MODEL_WIDTH:])
-    (x0,) = reduce([picked], 1)
+    row = (own_rows, MODEL_WIDTH)
+    (x0,) = exchange("rows_found", 1, [picked], [], [], keep, [], [((2,) + row, f32)])
 
     w_kv = jnp.dot(to_order, early[:, 2 * MODEL_WIDTH : at_small], preferred_element_type=f32).astype(bf16)
     small_rows = small_params.shape[0]
@@ -1019,61 +1268,40 @@
     gain_final = flat_small[:, None, 2 * MODEL_WIDTH : 3 * MODEL_WIDTH]
     bias = flat_small[:, None, 3 * MODEL_WIDTH :]
 
-    freq = frequencies()
+    freq_wide = jnp.tile(frequencies(), 4).reshape(1, 128)
     my_pos = lax.dynamic_slice_in_dim(picks.reshape(-1), com * own_rows, own_rows)
-    angle = my_pos.astype(f32)[:, None] * freq[None, :]
-    cosine, sine = jnp.cos(angle)[:, None, :], jnp.sin(angle)[:, None, :]
-    a1, scale_one = norm_forward(x0, gain_attn)
-    a1 = a1.astype(bf16)
-    mixed = bmm(pad_feats(a1), w_q) + bias[:, :, :MODEL_WIDTH]
-    q = rotate(mixed.reshape(2, own_rows, QUERY_HEADS, HEAD_SIZE), cosine, sine, 1.0)
-    q = to_pairs(q.reshape(2, own_rows, MODEL_WIDTH).astype(bf16))
-    q_all, a1_all = gather([q, a1[:1]], 2)
+    angle = my_pos.astype(f32)[:, None] * freq_wide
+    cosine, sine = jnp.cos(angle), jnp.sin(angle)
+    q_all, a1_all = exchange(
+        "rows_queries", 2, [], [(early, 0, MODEL_WIDTH), (early, MODEL_WIDTH, MODEL_WIDTH)],
+        [to_order, gain_attn, bias[:, :, :MODEL_WIDTH], cosine, sine, x0], queries,
+        [(2 * PAIRS, own_rows, 128, bf16), (1,) + row + (bf16,)], [],
+    )
     q_all, gu_sent = lax.optimization_barrier((q_all, spread(gu_weight, ref_gu, devices, units, feats_up)))
     gu_cols = lax.all_to_all(gu_sent, AXES, split_axis=0, concat_axis=0, tiled=True)
     w_gu = tuple(gu_cols[:, model].reshape(devices * feats_up, 2 * units) for model in range(2))
 
-    freq_wide = jnp.tile(freq, 4).reshape(1, 128)
     o_part, st_part, kv_tok = attend(
         n_one, tile_lo, tile_hi, q_all, x_tok, w_kv, gain_attn, bias[:, :, MODEL_WIDTH:], freq_wide, frow_wide, flat_of,
         pos_of, length, rp,
     )
-    o_sum, st_sum = mix(o_part, st_part, 3)
-    lse = st_sum[0] + jnp.log(st_sum[1])
-    share = (1.0 / st_sum[1::2])[:, :, :QUERY_HEADS]
-    o = from_pairs(o_sum, 2).reshape(2, own_rows, QUERY_HEADS, HEAD_SIZE) * share[..., None]
-    o = o.reshape(2, own_rows, MODEL_WIDTH).astype(bf16)
-    x1 = x0 + bmm(pad_feats(o), w_out)
-    a2, scale_two = norm_forward(x1, gain_mlp)
-    a2_all, o_all = gather([pad_feats(a2.astype(bf16)), o[:1]], 4)
+    o_part, late = lax.optimization_barrier((o_part, late))
+    a2_all, o_all, x1, o_own, lse = exchange(
+        "rows_attended", 3, [o_part, st_part], [(late, 0, MODEL_WIDTH), (late, MODEL_WIDTH, MODEL_WIDTH)],
+        [to_order, gain_mlp, x0], attended,
+        [(2, own_rows, devices * feats_up, bf16), (1,) + row + (bf16,)],
+        [((2,) + row, f32), (row, bf16), ((own_rows, 128), f32)], mix_phase,
+    )
     gate_up = bmm(a2_all, w_gu)
     gate, up = gate_up[:, :, :units], gate_up[:, :, units:]
     hidden = (jax.nn.silu(gate) * up).astype(bf16)
-    (branch,) = reduce([bmm(hidden, down_low).astype(bf16)], 5)
-    x2 = x1 + branch
-    af, scale_final = norm_forward(x2, gain_final)
-    (af_all,) = gather([af.astype(bf16)], 6)
-
-    vocab = base + jnp.arange(block, dtype=i32)
-    hit = vocab[:, None] == targets[None, :]
-    tables = (low_table, ref_embed)
-    logits = [
-        lax.dot_general(tables[i], af_all[i], (((1,), (1,)), ((), ())), preferred_element_type=f32) for i in range(2)
-    ]
-    stats = []
-    for i in range(2):
-        peak = jnp.max(logits[i], axis=0)
-        stats.append(
-            jnp.stack(
-                [
-                    peak,
-                    jnp.sum(jnp.exp(logits[i] - peak[None, :]), axis=0),
-                    jnp.sum(jnp.where(hit, logits[i], 0.0), axis=0),
-                ]
-            )
-        )
-    stats = jnp.concatenate(stats, axis=0)
-    stats = jnp.concatenate([stats, jnp.zeros((2, n_rows), f32)], axis=0)
+    af_all, x2 = exchange(
+        "rows_finals", 5, [bmm(hidden, down_low).astype(bf16)], [], [gain_final, x1], finals, [(2,) + row + (bf16,)],
+        [((2,) + row, f32)],
+    )
+
+    aim = (targets - base).reshape(1, -1)
+    stats, logits = head(low_table, ref_embed, af_all, aim)
     (stats_all,) = gather([stats[None]], 7)
     stats_all = stats_all.reshape(devices, 8, n_rows)
     lps, lses = [], []
@@ -1089,12 +1317,11 @@
     d_reward = (jax.nn.sigmoid(reward) - labels.reshape(rollouts).astype(f32)) / rollouts
     d_lp = (valid * (d_reward * factor)[:, None]).reshape(-1)
 
-    probs = jnp.exp(logits[0] - lses[0][None, :])
-    d_logits = (d_lp[None, :] * (hit.astype(f32) - probs)).astype(bf16)
-    d_af = lax.dot_general(d_logits, low_table, (((0,), (0,)), ((), ())), preferred_element_type=f32)
-    (d_final,) = reduce([d_af.astype(bf16)[None]], 8)
-    d_out, g_gain_final = norm_backward(d_final[0], x2[0], scale_final[0], gain_final[0])
-    (d_branch,) = gather([d_out.astype(bf16)[None]], 9)
+    d_logits, d_af = head_back(logits, low_table, lses[0].reshape(1, -1), d_lp.reshape(1, -1), aim)
+    d_branch, d_out, g_gain_final = exchange(
+        "rows_finals_back", 8, [d_af], [], [gain_final, x2], finals_back, [(1,) + row + (bf16,)],
+        [(row, f32), ((1, MODEL_WIDTH), f32)],
+    )
     d_branch = d_branch[0]
     g_down = lax.dot_general(hidden[0], d_branch, (((0,), (0,)), ((), ())), preferred_element_type=f32)
     d_hidden = lax.dot_general(d_branch, down_low[0], (((1,), (1,)), ((), ())), preferred_element_type=f32)
@@ -1103,19 +1330,11 @@
     d_up = d_hidden * gate[0] * sigma
     d_gate_up = jnp.concatenate([d_gate, d_up], axis=1).astype(bf16)
     d_a2 = lax.dot_general(d_gate_up, w_gu[0], (((1,), (1,)), ((), ())), preferred_element_type=f32)
-    (d_normed,) = reduce([d_a2.astype(bf16)[None]], 10)
-    d_mid, g_gain_mlp = norm_backward(cut_feats(d_normed[0]), x1[0], scale_two[0], gain_mlp[0])
-    d_mid = d_mid + d_out
-    d_attn = d_mid.astype(bf16)
-    d_o = lax.dot_general(d_attn, w_out[0], (((1,), (1,)), ((), ())), preferred_element_type=f32)
-    d_o = cut_feats(d_o).astype(bf16)
-    delta = jnp.sum(
-        (d_o.astype(f32) * o[0].astype(f32)).reshape(own_rows, QUERY_HEADS, HEAD_SIZE), axis=-1
+    d_attn_all, d_o_all, row_stats_all, d_mid, g_gain_mlp = exchange(
+        "rows_attended_back", 10, [d_a2.astype(bf16)[None]], [(late, 0, MODEL_WIDTH)], [from_order, gain_mlp, x1, d_out, o_own, lse],
+        attended_back, [(1,) + row + (bf16,), (PAIRS, own_rows, 128, bf16), (1, own_rows, 128, f32)],
+        [(row, f32), ((1, MODEL_WIDTH), f32)],
     )
-    row_stats = jnp.concatenate(
-        [lse[:, :16], delta, jnp.zeros((own_rows, 128 - 16 - QUERY_HEADS), f32)], axis=1
-    )
-    d_attn_all, d_o_all, row_stats_all = gather([d_attn[None], to_pairs(d_o), row_stats[None]], 11)
     d_attn_all = d_attn_all[0]
 
     g_gu = lax.dot_general(a2_all[0], d_gate_up, (((0,), (0,)), ((), ())), preferred_element_type=f32)
@@ -1130,13 +1349,13 @@
     dq_part, g_gu = lax.optimization_barrier((dq_part, g_gu))
     g_kv_part = g_kv_part.reshape(2, n_y, 2, n_batch, feats, 256).transpose(2, 0, 1, 3, 4, 5)
     g_kv_part = jnp.pad(g_kv_part.reshape(devices, feats, 256), ((0, 0), (0, feats_up - feats), (0, 0)))
-    dq, g_kv = reduce([dq_part, g_kv_part.reshape(1, devices * feats_up, 256)], 12)
-    g_kv = g_kv[0, :feats]
-    dq = rotate(from_pairs(dq, 1).reshape(own_rows, QUERY_HEADS, HEAD_SIZE), cosine, sine, -1.0)
-    dq = dq.reshape(own_rows, MODEL_WIDTH).astype(bf16)
-    d_a1 = cut_feats(lax.dot_general(dq, w_q[0], (((1,), (1,)), ((), ())), preferred_element_type=f32))
-    d_row, g_gain_row = norm_backward(d_a1, x0[0], scale_one[0], gain_attn[0])
-    dq_all, d_row_all = gather([dq[None], (d_row + d_mid).astype(bf16)[None]], 13)
+    dq_all, d_row_all, g_kv, g_gain_row, g_bias_q = exchange(
+        "rows_queries_back", 12, [dq_part, g_kv_part.reshape(1, devices * feats_up, 256)],
+        [(early, 0, MODEL_WIDTH)], [from_order, gain_attn, x0, d_mid, cosine, sine], queries_back,
+        [(1,) + row + (bf16,), (1,) + row + (bf16,)],
+        [((feats_up, 256), f32), ((1, MODEL_WIDTH), f32), ((1, MODEL_WIDTH), f32)],
+    )
+    g_kv = g_kv[:feats]
     dq_all = dq_all[0]
 
     embed_grad, embed_square = table_grad(
@@ -1153,10 +1372,10 @@
 
     small_part = jnp.concatenate(
         [
-            jnp.sum(g_gain_kv, axis=0) + jnp.sum(g_gain_row, axis=0),
-            jnp.sum(g_gain_mlp, axis=0),
-            jnp.sum(g_gain_final, axis=0),
-            jnp.sum(dq.astype(f32), axis=0),
+            jnp.sum(g_gain_kv, axis=0) + g_gain_row[0],
+            g_gain_mlp[0],
+            g_gain_final[0],
+            g_bias_q[0],
             jnp.sum(g_bias_kv, axis=0),
         ]
     )

time: 590 us -> 566 us (0.959)
  matrix products: 58.1 us -> 16.9 us
  Pallas kernels: 352 us -> 382 us
  local copies, waits for them, and re-layouts: 49.7 us -> 29.2 us
  waiting for transfers between devices: 0.06 us -> 15.9 us
  other arithmetic: 89.2 us -> 80.6 us
    pallas_call x6 -> x9, Pallas kernels: 123 us -> 277 us  [the longest x7 242 us: exchange(): pl.pallas_call(functools.partial(exchange_kernel, n_in, columns, len(cons...]
    pallas_call x8 -> x2, Pallas kernels: 142 us -> 24.2 us  [gather(): pl.pallas_call(functools.partial(gather_kernel, n), out_shape=[jax.ShapeD...]
    dot_general x11 -> x0, matrix products: 32.8 us -> none  [the longest x2 13.3 us: body(): lax.dot_general(tables[i], af_all[i], (((1,), (1,)), ((), ())), preferred...]
    dot_general x3 -> x0, local copies, waits for them, and re-layouts: 11.8 us -> none  [bmm(): jnp.dot(x[i], w[i], preferred_element_type=jnp.float32)]
    dot_general x8 -> x4, matrix products: 11.8 us -> 2.06 us  [bmm(): jnp.dot(x[i], w[i], preferred_element_type=jnp.float32)]
    all_gather x1, waiting for transfers between devices: 0.02 us -> 8.49 us  [body(): late = lax.all_gather(out_both, AXES, axis=0, tiled=True)]
    reduce_sum x10 -> x1, other arithmetic: 7.35 us -> 0.01 us  [body(): jnp.sum(g_gain_kv, axis=0) + g_gain_row[0]]
    all_gather x1, waiting for transfers between devices: 0.01 us -> 7.33 us  [body(): lax.all_gather(jnp.concatenate([early] + smalls, axis=1), AXES, axis=0, t...]
  transfers between devices with their start and end apart: 4 -> 4, of which waited for: 0 -> 2; matrix products, arithmetic and copies ran while one was open for 12% -> 8% of each run, Pallas kernels for 30% -> 31%
where the time goes in v3:
time: 566 us; the launch traced here: 557 us
  Pallas kernels  382 us (67%)
  other arithmetic  80.6 us (14%)
  local copies, waits for them, and re-layouts  29.2 us (5%)
  between operations  21.8 us (4%)
  matrix products  16.9 us (3%)
  waiting for transfers between devices  15.9 us (3%)
  starting transfers between devices  10.3 us (2%)
    pallas_call x7, Pallas kernels, exchange(): pl.pallas_call(functools.partial(exchange_kernel, n_in, columns, len(cons...  242 us
    convert_element_type x5, other arithmetic, body(): new_lows.append(w_new.astype(bf16))  50.8 us
    pallas_call x2, Pallas kernels, gather(): pl.pallas_call(functools.partial(gather_kernel, n), out_shape=[jax.ShapeD...  24.2 us
    pallas_call x1, Pallas kernels, attend(): pl.pallas_call(functools.partial(attend_kernel, length, rp), grid=(2,), o...  24 us
    pallas_call x1, Pallas kernels, head(): pl.pallas_call(functools.partial(head_kernel, block, span), grid=(pl.cdiv...  20.1 us
    pallas_call x1, Pallas kernels, lookup(): pl.pallas_call(functools.partial(lookup_kernel, block, span), grid=(steps...  19.5 us
    pallas_call x1, Pallas kernels, attend_back(): pl.pallas_call(functools.partial(attend_back_kernel, length, rp), grid=(1...  18.7 us
    pallas_call x1, Pallas kernels, table_grad(): pl.pallas_call(functools.partial(table_grad_kernel, block, span), grid=(s...  16.8 us
  transfers between devices with their start and end apart: 4, of which 2 were waited for; matrix products, arithmetic and copies ran while one was open for 8% of the time, Pallas kernels for 31%

profile of v3, /device:TPU:0, one launch (start us, length us, event | category | flops | bytes accessed | tf_op | source)
XLA Modules:
  0.0 557.0 jit_solution(5907801749429920490)
XLA Ops:
  16.8 6.8 %sort.14 = (s32[8192]{0:T(1024)S(1)}, s32[8192]{0:T(1024)}) sort(s32[8192]{0:T(1024)S(1)} %fusion.71, s32[8192]{0:T(1024)S(1)} %iota.78), dimensions={0}, to_apply=%region_2.4 | sort | flops 106496 | bytes 131072 | tf_op jit(solution)/shard_map/sort | solution.py:1235
  25.7 19.5 %lookup.1 = (bf16[4748,896]{1,0:T(8,128)(2,1)}, bf16[2,512,896]{2,1,0:T(8,128)(2,1)}, bf16[2,8192,896]{2,1,0:T(8,128)(2,1)}) custom-call(s32[1]{0:T(128)} %bitcast.6.n_ref, s32[8192]{0:T(1024)} %get-tuple-element.248.rows_ref, f32[4748,896]{1,0:T(8,128)} %table_ref.1, bf16[4748,896]{1,0:T(8,128)(2,1)} %frozen_ref.5, s32[64,128]{1,0:T(8,128)} %get-tuple-element.247.flat_ref, ...), custom_call_target="tpu_custom_call" | custom-call | tf_op jit(solution)/shard_map/lookup/pallas_call | solution.py:390
  46.1 26.6 %rows_found.1.refs_7_.refs_6_.refs_5_ = f32[2,16,896]{2,1,0:T(8,128)} custom-call(bf16[2,512,896]{2,1,0:T(8,128)(2,1)} %get-tuple-element.78.refs_0_), custom_call_target="tpu_custom_call" | custom-call | tf_op jit(solution)/shard_map/rows_found/pallas_call | solution.py:276
  77.0 7.3 %all-gather.3.cloned.1.call-done.refs_0_.refs_1_.refs_2_ = bf16[1024,2560]{1,0:T(8,128)(2,1)} async-done(((bf16[32,2560]{1,0:T(8,128)(2,1)}), bf16[1024,2560]{1,0:T(8,128)(2,1)}) %all-gather.3.cloned.1.call-update) | async-done | bytes 5242896 | tf_op jit(solution)/shard_map/all_gather | solution.py:1224
  86.7 28.2 %rows_queries.1 = (bf16[14,512,128]{2,1,0:T(8,128)(2,1)}, bf16[1,512,896]{2,1,0:T(8,128)(2,1)}) custom-call(bf16[1024,2560]{1,0:T(8,128)(2,1)} %all-gather.3.cloned.1.call-done.refs_0_.refs_1_.refs_2_, bf16[1024,2560]{1,0:T(8,128)(2,1)} %all-gather.3.cloned.1.call-done.refs_0_.refs_1_.refs_2_, bf16[896,1024]{1,0:T(8,128)(2,1)} %fusion.2.refs_2_.refs_4_, ...), custom_call_target="tpu_custom_call" | custom-call | tf_op jit(solution)/shard_map/rows_queries/pallas_call | solution.py:276
  115.0 5.6 %all-to-all-start = ((bf16[32,2,32,304]{3,2,1,0:T(8,128)(2,1)}), bf16[32,2,32,304]{3,2,1,0:T(8,128)(2,1)}, u32[]{:S(2)}, u32[]{:S(2)}) async-start(bf16[32,2,32,304]{3,2,1,0:T(8,128)(2,1)} %spread.1), calls=%async_computation | async-start | bytes 3145728 | tf_op jit(solution)/shard_map/all_to_all | solution.py:1281
  127.5 3.3 fusion.5.w_ref
  130.8 24.0 %attend.1 = (bf16[14,512,128]{2,1,0:T(8,128)(2,1)}, f32[4,512,128]{2,1,0:T(8,128)}, bf16[2,8192,256]{2,1,0:T(8,128)(2,1)}) custom-call(s32[1]{0:T(128)} %bitcast.6.n_ref, s32[64]{0:T(128)} %and_select_fusion.1.lo_ref, s32[64]{0:T(128)} %fusion.67.hi_ref, bf16[14,512,128]{2,1,0:T(8,128)(2,1)} %get-tuple-element.81.q_ref, ...), custom_call_target="tpu_custom_call" | custom-call | tf_op jit(solution)/shard_map/attend/pallas_call | solution.py:553
  154.9 8.5 %all-gather.5.cloned.1.call-done.refs_2_.refs_3_.refs_1_ = bf16[1024,1792]{1,0:T(8,128)(2,1)} async-done(((bf16[32,1792]{1,0:T(8,128)(2,1)}), bf16[1024,1792]{1,0:T(8,128)(2,1)}) %all-gather.5.cloned.1.call-update) | async-done | bytes 3670032 | tf_op jit(solution)/shard_map/all_gather | solution.py:1257
  164.5 51.8 %rows_attended.1 = (bf16[2,512,1024]{2,1,0:T(8,128)(2,1)}, bf16[1,512,896]{2,1,0:T(8,128)(2,1)}, f32[2,16,896]{2,1,0:T(8,128)}, bf16[16,896]{1,0:T(8,128)(2,1)}, f32[16,128]{1,0:T(8,128)}) custom-call(bf16[14,512,128]{2,1,0:T(8,128)(2,1)} %get-tuple-element.85.refs_0_, f32[4,512,128]{2,1,0:T(8,128)} %get-tuple-element.86.refs_1_, ...), custom_call_target="tpu_custom_call" | custom-call | tf_op jit(solution)/shard_map/rows_attended/pallas_call | solution.py:276
  222.1 33.4 %rows_finals.1 = (bf16[2,512,896]{2,1,0:T(8,128)(2,1)}, f32[2,16,896]{2,1,0:T(8,128)}) custom-call(bf16[2,512,896]{2,1,0:T(8,128)(2,1)} %pad_maximum_fusion.refs_0_, f32[2,1,896]{2,1,0:T(1,128)} %broadcast_in_dim.75.refs_1_, f32[2,16,896]{2,1,0:T(8,128)} %get-tuple-element.91.refs_2_.refs_4_), custom_call_target="tpu_custom_call" | custom-call | tf_op jit(solution)/shard_map/rows_finals/pallas_call | solution.py:276
  255.6 20.1 %head.1 = (f32[8,512]{1,0:T(8,128)}, f32[4748,512]{1,0:T(8,128)}) custom-call(bf16[4748,896]{1,0:T(8,128)(2,1)} %get-tuple-element.89.own_ref, bf16[4748,896]{1,0:T(8,128)(2,1)} %frozen_ref.5, bf16[2,512,896]{2,1,0:T(8,128)(2,1)} %get-tuple-element.92.af_ref, s32[1,512]{1,0:T(1,128)} %sub.128.aim_ref), custom_call_target="tpu_custom_call" | custom-call | tf_op jit(solution)/shard_map/head/pallas_call | solution.py:890
  276.4 11.5 %gather_7.1 = f32[1,256,512]{2,1,0:T(8,128)S(1)} custom-call(f32[1,8,512]{2,1,0:T(8,128)S(1)} %bitcast.160), custom_call_target="tpu_custom_call" | custom-call | tf_op jit(solution)/shard_map/gather_7/pallas_call | solution.py:149
  291.2 15.0 %head_back.1 = (bf16[4748,512]{1,0:T(8,128)(2,1)}, bf16[1,512,896]{2,1,0:T(8,128)(2,1)}) custom-call(f32[4748,512]{1,0:T(8,128)} %get-tuple-element.93.logit_ref, bf16[4748,896]{1,0:T(8,128)(2,1)} %get-tuple-element.89.own_ref, f32[1,512]{1,0:T(1,128)} %bitcast.179, f32[1,512]{1,0:T(1,128)} %compare_select_fusion.dlp_ref, s32[1,512]{1,0:T(1,128)} %sub.128.aim_ref), custom_call_target="tpu_custom_call" | custom-call | tf_op jit(solution)/shard_map/head_back/pallas_call | solution.py:931
  306.2 25.1 %rows_finals_back.1 = (bf16[1,512,896]{2,1,0:T(8,128)(2,1)}, f32[16,896]{1,0:T(8,128)}, f32[1,896]{1,0:T(1,128)}) custom-call(bf16[1,512,896]{2,1,0:T(8,128)(2,1)} %get-tuple-element.95.refs_0_, f32[2,1,896]{2,1,0:T(1,128)} %broadcast_in_dim.75.refs_1_, f32[2,16,896]{2,1,0:T(8,128)} %get-tuple-element.96.refs_2_), custom_call_target="tpu_custom_call" | custom-call | tf_op jit(solution)/shard_map/rows_finals_back/pallas_call | solution.py:276
  337.4 34.2 %rows_attended_back.1 = (bf16[1,512,896]{2,1,0:T(8,128)(2,1)}, bf16[7,512,128]{2,1,0:T(8,128)(2,1)}, f32[1,512,128]{2,1,0:T(8,128)}, f32[16,896]{1,0:T(8,128)}, f32[1,896]{1,0:T(1,128)}) custom-call(bf16[1,512,1024]{2,1,0:T(8,128)(2,1)} %fusion.6.refs_0_, bf16[1024,1792]{1,0:T(8,128)(2,1)} %all-gather.5.cloned.1.call-done.refs_2_.refs_3_.refs_1_, ...), custom_call_target="tpu_custom_call" | custom-call | tf_op jit(solution)/shard_map/rows_attended_back/pallas_call | solution.py:276
  371.6 4.6 all-to-all-start.1
  379.5 18.7 %attend_back.1 = (bf16[7,512,128]{2,1,0:T(8,128)(2,1)}, f32[896,256]{1,0:T(8,128)}, f32[8,896]{1,0:T(8,128)}, f32[8,256]{1,0:T(8,128)}, bf16[8192,896]{1,0:T(8,128)(2,1)}) custom-call(s32[1]{0:T(128)} %bitcast.6.n_ref, s32[64]{0:T(128)} %and_select_fusion.1.lo_ref, s32[64]{0:T(128)} %fusion.67.hi_ref, bf16[7,512,128]{2,1,0:T(8,128)(2,1)} %slice.130.q_ref, ...), custom_call_target="tpu_custom_call" | custom-call | tf_op jit(solution)/shard_map/attend_back/pallas_call | solution.py:696
  407.6 2.9 multiply_reduce_fusion.1
  411.5 42.5 %rows_queries_back.1 = (bf16[1,512,896]{2,1,0:T(8,128)(2,1)}, bf16[1,512,896]{2,1,0:T(8,128)(2,1)}, f32[32,256]{1,0:T(8,128)}, f32[1,896]{1,0:T(1,128)}, f32[1,896]{1,0:T(1,128)}) custom-call(bf16[7,512,128]{2,1,0:T(8,128)(2,1)} %get-tuple-element.107.refs_0_, f32[1,1024,256]{2,1,0:T(8,128)} %bitcast.163, ...), custom_call_target="tpu_custom_call" | custom-call | tf_op jit(solution)/shard_map/rows_queries_back/pallas_call | solution.py:276
  455.4 16.8 %table_grad.1 = (bf16[4748,896]{1,0:T(8,128)(2,1)}, f32[8,896]{1,0:T(8,128)}) custom-call(s32[1]{0:T(128)} %bitcast.6.n_ref, s32[8192]{0:T(1024)} %get-tuple-element.248.rows_ref, bf16[4748,512]{1,0:T(8,128)(2,1)} %get-tuple-element.120.dl_ref, bf16[512,896]{1,0:T(8,128)(2,1)} %slice_bitcast_fusion.af_ref, bf16[512,896]{1,0:T(8,128)(2,1)} %bitcast.169, ...), custom_call_target="tpu_custom_call" | custom-call | tf_op jit(solution)/shard_map/table_grad/pallas_call | solution.py:790
  479.0 12.7 %gather_14.1 = f32[1,1024,128]{2,1,0:T(8,128)S(1)} custom-call(f32[1,32,128]{2,1,0:T(8,128)S(1)} %bitcast.159), custom_call_target="tpu_custom_call" | custom-call | tf_op jit(solution)/shard_map/gather_14/pallas_call | solution.py:149
  500.4 4.3 fusion.97
  506.3 42.3 %fusion.93 = (bf16[4748,896]{1,0:T(8,128)(2,1)}, f32[4748,896]{1,0:T(8,128)}, f32[4748,896]{1,0:T(8,128)}, f32[4748,896]{1,0:T(8,128)}) fusion(f32[4748,896]{1,0:T(8,128)} %table_ref.1, f32[]{:T(128)S(6)} %min.3, bf16[4748,896]{1,0:T(8,128)(2,1)} %get-tuple-element.125, f32[4748,896]{1,0:T(8,128)} %param.44, f32[4748,896]{1,0:T(8,128)} %param.50), kind=kLoop, calls=%fused_computation.210 | loop fusion | flops 72321536 | bytes 119117824 | tf_op jit(solution)/shard_map/convert_element_type | solution.py:1406
  (208 shorter events, 69.4 us)
Async XLA Ops:
  7.2 212.5 %copy-start = (bf16[152,896]{1,0:T(8,128)(2,1)S(1)}, bf16[152,896]{1,0:T(8,128)(2,1)}, u32[]{:S(2)}) copy-start(bf16[152,896]{1,0:T(8,128)(2,1)} %param.55) | copy-start | bytes 817156
  7.2 77.1 %all-gather.3.cloned.1.call-start = ((), (), s32[]{:S(2)}) async-start(), calls=%async_computation.2 | async-start | bytes 5406720 | tf_op jit(solution)/shard_map/all_gather | solution.py:1224
  12.3 151.1 %all-gather.5.cloned.1.call-start = ((), (), s32[]{:S(2)}) async-start(), calls=%async_computation.3 | async-start | bytes 3784704 | tf_op jit(solution)/shard_map/all_gather | solution.py:1257
  25.7 19.6 %copy-start.26 = (bf16[28,896]{1,0:T(8,128)(2,1)S(1)}, bf16[28,896]{1,0:T(8,128)(2,1)}, u32[]{:S(2)}) copy-start(bf16[28,896]{1,0:T(8,128)(2,1)} %param.53) | copy-start | bytes 150532
  45.2 27.5 %copy-start.2 = (f32[28,9728]{1,0:T(8,128)S(1)}, f32[28,9728]{1,0:T(8,128)}, u32[]{:S(2)}) copy-start(f32[28,9728]{1,0:T(8,128)} %own_ref.1) | copy-start | bytes 3268612
  45.2 27.5 %copy-start.5 = (bf16[28,9728]{1,0:T(8,128)(2,1)S(1)}, bf16[28,9728]{1,0:T(8,128)(2,1)}, u32[]{:S(2)}) copy-start(bf16[28,9728]{1,0:T(8,128)(2,1)} %frozen_ref.4) | copy-start | bytes 1634308
  115.0 6.5 %copy-start.23 = (s32[2,4,4,256]{3,2,1,0:T(4,128)S(1)}, s32[2,4,4,256]{3,2,1,0:T(4,128)}, u32[]{:S(2)}) copy-start(s32[2,4,4,256]{3,2,1,0:T(4,128)} %param.30) | copy-start | bytes 98308
  115.0 7.9 %copy-start.31 = (f32[30,4]{0,1:T(4,128)S(1)}, f32[30,4]{0,1:T(4,128)}, u32[]{:S(2)}) copy-start(f32[30,4]{0,1:T(4,128)} %param.51) | copy-start | bytes 1444
  115.0 8.0 %copy-start.32 = (f32[30,4]{0,1:T(4,128)S(1)}, f32[30,4]{0,1:T(4,128)}, u32[]{:S(2)}) copy-start(f32[30,4]{0,1:T(4,128)} %param.45) | copy-start | bytes 1444
  115.0 8.1 %copy-start.15 = (s32[64,128]{1,0:T(8,128)S(1)}, s32[64,128]{1,0:T(8,128)}, u32[]{:S(2)}) copy-start(s32[64,128]{1,0:T(8,128)} %get-tuple-element.247.flat_ref) | copy-start | bytes 98308
  115.0 101.3 %all-to-all-start = ((bf16[32,2,32,304]{3,2,1,0:T(8,128)(2,1)}), bf16[32,2,32,304]{3,2,1,0:T(8,128)(2,1)}, u32[]{:S(2)}, u32[]{:S(2)}) async-start(bf16[32,2,32,304]{3,2,1,0:T(8,128)(2,1)} %spread.1), calls=%async_computation | async-start | bytes 3145728 | tf_op jit(solution)/shard_map/all_to_all | solution.py:1281
  255.6 34.8 %copy-start.33 = (s32[2,4]{1,0:T(2,128)S(1)}, s32[2,4]{1,0:T(2,128)}, u32[]{:S(2)}) copy-start(s32[2,4]{1,0:T(2,128)} %param.32) | copy-start | bytes 100
  291.2 40.2 %copy-start.9 = (f32[152,896]{1,0:T(8,128)S(1)}, f32[152,896]{1,0:T(8,128)}, u32[]{:S(2)}) copy-start(f32[152,896]{1,0:T(8,128)} %param.37) | copy-start | bytes 1634308
  371.6 39.9 %all-to-all-start.1 = ((bf16[32,32,304]{2,1,0:T(8,128)(2,1)}), bf16[32,32,304]{2,1,0:T(8,128)(2,1)S(1)}, u32[]{:S(2)}, u32[]{:S(2)}) async-start(bf16[32,32,304]{2,1,0:T(8,128)(2,1)} %bitcast.166), calls=%async_computation.1 | async-start | bytes 1572864 | tf_op jit(solution)/shard_map/all_to_all | solution.py:1344
  405.2 5.3 copy-start.7
  411.5 42.5 %copy-start.3 = (bf16[32,32,304]{2,1,0:T(8,128)(2,1)}, bf16[32,32,304]{2,1,0:T(8,128)(2,1)S(1)}, u32[]{:S(2)}) copy-start(bf16[32,32,304]{2,1,0:T(8,128)(2,1)S(1)} %all-to-all-done.1.g_ref) | copy-start | bytes 1867780
  455.4 18.3 %copy-start.16 = (bf16[1,512,896]{2,1,0:T(8,128)(2,1)S(1)}, bf16[1,512,896]{2,1,0:T(8,128)(2,1)}, u32[]{:S(2)}) copy-start(bf16[1,512,896]{2,1,0:T(8,128)(2,1)} %get-tuple-element.110) | copy-start | bytes 2752516
  455.4 19.7 %copy-start.24 = (f32[32,256]{1,0:T(8,128)S(1)}, f32[32,256]{1,0:T(8,128)}, u32[]{:S(2)}) copy-start(f32[32,256]{1,0:T(8,128)} %get-tuple-element.111) | copy-start | bytes 98308
  473.7 24.1 %copy-start.17 = (f32[28,1152]{1,0:T(8,128)S(1)}, f32[28,1152]{1,0:T(8,128)}, u32[]{:S(2)}) copy-start(f32[28,1152]{1,0:T(8,128)} %param.34) | copy-start | bytes 387076
  473.7 24.1 %copy-start.21 = (f32[28,1152]{1,0:T(8,128)S(1)}, f32[28,1152]{1,0:T(8,128)}, u32[]{:S(2)}) copy-start(f32[28,1152]{1,0:T(8,128)} %param.40) | copy-start | bytes 387076
  473.7 24.1 %copy-start.22 = (f32[28,1152]{1,0:T(8,128)S(1)}, f32[28,1152]{1,0:T(8,128)}, u32[]{:S(2)}) copy-start(f32[28,1152]{1,0:T(8,128)} %param.46) | copy-start | bytes 387076
  479.0 19.7 %copy-start.20 = (f32[28,896]{1,0:T(8,128)S(1)}, f32[28,896]{1,0:T(8,128)}, u32[]{:S(2)}) copy-start(f32[28,896]{1,0:T(8,128)} %param.35) | copy-start | bytes 301060
  479.0 19.6 %copy-start.25 = (f32[28,896]{1,0:T(8,128)S(1)}, f32[28,896]{1,0:T(8,128)}, u32[]{:S(2)}) copy-start(f32[28,896]{1,0:T(8,128)} %param.41) | copy-start | bytes 301060
  506.3 42.3 %copy-start.1 = (bf16[152,896]{1,0:T(8,128)(2,1)S(1)}, bf16[152,896]{1,0:T(8,128)(2,1)}, u32[]{:S(2)}) copy-start(bf16[152,896]{1,0:T(8,128)(2,1)} %param.55) | copy-start | bytes 817156
  (14 other events, 45.6 us)
Sparse Core Ops, SparseCore 0:
  12.4 71.8 all-gather.2
  87.7 75.5 all-gather.4

commit v4 on v3

--- a/solution.py
+++ b/solution.py
@@ -331,10 +331,11 @@
 ):
     step = pl.program_id(0)
     f32, bf16 = jnp.float32, jnp.bfloat16
-    low = table_ref[...].astype(bf16)
+    inside = step * span + lax.broadcasted_iota(jnp.int32, (span, 1), 0) < block
+    low = jnp.where(inside, table_ref[...], 0.0).astype(bf16)
     low_ref[...] = low
     at = pl.multiple_of(step * span, span)
-    held[0, pl.ds(at, span), :] = low.astype(f32)
+    held[0, pl.ds(at, span), :] = table_ref[...]
     held[1, pl.ds(at, span), :] = frozen_ref[...].astype(f32)
 
     @pl.when(step == pl.num_programs(0) - 1)
@@ -391,7 +392,7 @@
         functools.partial(lookup_kernel, block, span),
         grid=(steps,),
         out_shape=[
-            jax.ShapeDtypeStruct((block, width), bf16),
+            jax.ShapeDtypeStruct((steps * span, width), bf16),
             jax.ShapeDtypeStruct((2, n_rows, width), bf16),
             jax.ShapeDtypeStruct((2, cap, width), bf16),
         ],
@@ -527,15 +528,13 @@
     def leave(r, _):
         rows = pl.ds(pl.multiple_of(r * rp, rp), rp)
         o_ref[:, rows, :] = o_scr[:, rows, :].astype(bf16)
-        tops = jnp.full((rp, 128), -1e30, f32)
-        totals = jnp.zeros((rp, 128), f32)
+        packed = jnp.where(model == 0, jnp.zeros((rp, 128), f32), st_ref[0, rows, :])
         for slot, head in enumerate(HEAD_SLOTS):
-            tops = jnp.where(lane_r == head, m_scr[slot, rows, :], tops)
             held = l_scr[head // 2, rows, :]
             held = held[:, 64:65] if head % 2 == 0 else held[:, 0:1]
-            totals = jnp.where(lane_r == head, held, totals)
-        st_ref[0, rows, :] = tops
-        st_ref[1, rows, :] = totals
+            packed = jnp.where(lane_r == head + 32 * model, m_scr[slot, rows, :], packed)
+            packed = jnp.where(lane_r == 16 + head + 32 * model, held, packed)
+        st_ref[0, rows, :] = packed
         return 0
 
     lax.fori_loop(0, m_scr.shape[1] // rp, leave, 0)
@@ -555,14 +554,14 @@
         grid=(2,),
         out_shape=[
             jax.ShapeDtypeStruct((2 * PAIRS, n_rows, 128), bf16),
-            jax.ShapeDtypeStruct((4, n_rows, 128), jnp.float32),
+            jax.ShapeDtypeStruct((1, n_rows, 128), jnp.float32),
             jax.ShapeDtypeStruct((2, cap, 256), bf16),
         ],
         in_specs=[
             smem, smem, smem, model((PAIRS, n_rows, 128)), anyw, pl.BlockSpec((width, 256), lambda i: (0, i)), model((1, 1, width)),
             model((1, 1, 256)), whole((1, 128)), whole(frow.shape), whole(flat.shape), whole(pos.shape),
         ],
-        out_specs=[model((PAIRS, n_rows, 128)), model((2, n_rows, 128)), anyw],
+        out_specs=[model((PAIRS, n_rows, 128)), whole((1, n_rows, 128)), anyw],
         scratch_shapes=[
             pltpu.VMEM((2, TILE, width), bf16),
             pltpu.VMEM((TILE, 256), bf16),
@@ -686,7 +685,7 @@
 
 
 def attend_back(n_local, lo, hi, q, do, stats, x, kv, w, gain, freq, frow, flat, pos, length, rp):
-    n_rows = q.shape[1]
+    n_rows = do.shape[1]
     width = x.shape[2]
     cap = x.shape[1]
     bf16, f32 = jnp.bfloat16, jnp.float32
@@ -726,7 +725,7 @@
 
 
 def table_grad_kernel(
-    block, span, n_ref, rows_ref, dl_ref, af_ref, drow_ref, frow_ref, flat_ref, dx_ref,
+    span, n_ref, rows_ref, dl_ref, af_ref, drow_ref, frow_ref, flat_ref, dx_ref,
     g_ref, sq_ref, added, moved, rough, sem,
 ):
     step = pl.program_id(0)
@@ -773,22 +772,20 @@
 
         lax.fori_loop(0, tiles, tile, 0)
 
-    inside = step * span + lax.broadcasted_iota(jnp.int32, (span, 1), 0) < block
-    logit = jnp.where(inside, dl_ref[...].astype(f32), 0.0).astype(bf16)
-    total = straight(logit, af_ref[...]) + added[pl.ds(pl.multiple_of(step * span, span), span), :]
+    total = straight(dl_ref[...], af_ref[0]) + added[pl.ds(pl.multiple_of(step * span, span), span), :]
     g_ref[...] = total.astype(bf16)
     square = total * total
     sq_ref[...] += jnp.sum(square.reshape(span // 8, 8, square.shape[1]), axis=0)
 
 
 def table_grad(n_local, rows, dl, af, drow, frow, flat, dx, block):
-    n_rows, width = af.shape
-    span = 512
-    steps = pl.cdiv(block, span)
+    _, n_rows, width = af.shape
+    span = wide(dl.shape[0])
+    steps = dl.shape[0] // span
     whole = lambda shape: pl.BlockSpec(shape, lambda i: (0,) * len(shape))
     smem = pl.BlockSpec(memory_space=pltpu.SMEM)
     return pl.pallas_call(
-        functools.partial(table_grad_kernel, block, span),
+        functools.partial(table_grad_kernel, span),
         grid=(steps,),
         out_shape=[
             jax.ShapeDtypeStruct((block, width), jnp.bfloat16),
@@ -797,7 +794,7 @@
         in_specs=[
             smem, smem,
             pl.BlockSpec((span, n_rows), lambda i: (i, 0)),
-            whole(af.shape), whole(drow.shape), whole(frow.shape), whole(flat.shape),
+            whole((1, n_rows, width)), whole(drow.shape), whole(frow.shape), whole(flat.shape),
             pl.BlockSpec(memory_space=pl.ANY),
         ],
         out_specs=[pl.BlockSpec((span, width), lambda i: (i, 0)), whole((8, width))],
@@ -857,6 +854,10 @@
     )(g)
 
 
+def wide(rows):
+    return 1024 if rows % 1024 == 0 else 512
+
+
 def head_kernel(block, span, own_ref, frozen_ref, af_ref, aim_ref, st_ref, logit_ref):
     step = pl.program_id(0)
     f32 = jnp.float32
@@ -868,12 +869,13 @@
         for model in range(2):
             st_ref[3 * model : 3 * model + 1, :] = jnp.full((1, n_rows), -1e30, f32)
 
-    row = step * span + lax.broadcasted_iota(jnp.int32, (span, n_rows), 0)
-    hit = (row == aim_ref[...]) & (row < block)
-    for model, ref in enumerate((own_ref, frozen_ref)):
-        logit = jnp.where(row < block, last_last(ref[...], af_ref[model]), -1e30)
-        if model == 0:
-            logit_ref[...] = logit
+    inside = step * span + lax.broadcasted_iota(jnp.int32, (span, 1), 0) < block
+    shift = jnp.where(inside, 0.0, -1e30)
+    frozen = jnp.where(inside, frozen_ref[...].astype(f32), 0.0).astype(jnp.bfloat16)
+    logits = [last_last(own_ref[...], af_ref[0]) + shift, last_last(frozen, af_ref[1]) + shift]
+    logit_ref[...] = logits[0]
+    hit = lax.broadcasted_iota(jnp.int32, (span, n_rows), 0) == aim_ref[...] - step * span
+    for model, logit in enumerate(logits):
         top, total, found = (pl.ds(3 * model + k, 1) for k in range(3))
         new = jnp.maximum(st_ref[top, :], jnp.max(logit, axis=0, keepdims=True))
         fall = jnp.exp(st_ref[top, :] - new)
@@ -883,14 +885,14 @@
 
 
 def head(own, frozen, af, aim):
-    block, width = own.shape
+    rows, width = own.shape
     n_rows = af.shape[1]
-    span = 512
+    span = wide(rows)
     whole = lambda shape: pl.BlockSpec(shape, lambda i: (0,) * len(shape))
     return pl.pallas_call(
-        functools.partial(head_kernel, block, span),
-        grid=(pl.cdiv(block, span),),
-        out_shape=[jax.ShapeDtypeStruct((8, n_rows), jnp.float32), jax.ShapeDtypeStruct((block, n_rows), jnp.float32)],
+        functools.partial(head_kernel, frozen.shape[0], span),
+        grid=(rows // span,),
+        out_shape=[jax.ShapeDtypeStruct((8, n_rows), jnp.float32), jax.ShapeDtypeStruct((rows, n_rows), jnp.float32)],
         in_specs=[
             pl.BlockSpec((span, width), lambda i: (i, 0)), pl.BlockSpec((span, width), lambda i: (i, 0)),
             whole(af.shape), whole(aim.shape),
@@ -901,22 +903,19 @@
     )(own, frozen, af, aim)
 
 
-def head_back_kernel(block, span, logit_ref, own_ref, lse_ref, dlp_ref, aim_ref, dl_ref, d_af_ref, acc):
+def head_back_kernel(logit_ref, own_ref, lse_ref, dlp_ref, aim_ref, dl_ref, d_af_ref, acc):
     step = pl.program_id(0)
-    f32, bf16 = jnp.float32, jnp.bfloat16
+    bf16 = jnp.bfloat16
 
     @pl.when(step == 0)
     def _():
         acc[...] = jnp.zeros_like(acc)
 
-    row = step * span + lax.broadcasted_iota(jnp.int32, logit_ref.shape, 0)
-    hot = jnp.where(row == aim_ref[...], 1.0, 0.0)
-    d_logit = dlp_ref[...] * (hot - jnp.exp(logit_ref[...] - lse_ref[...]))
-    d_logit = jnp.where(row < block, d_logit, 0.0).astype(bf16)
+    place = lax.broadcasted_iota(jnp.int32, logit_ref.shape, 0)
+    hot = jnp.where(place == aim_ref[...] - step * logit_ref.shape[0], 1.0, 0.0)
+    d_logit = (dlp_ref[...] * (hot - jnp.exp(logit_ref[...] - lse_ref[...]))).astype(bf16)
     dl_ref[...] = d_logit
-    inside = step * span + lax.broadcasted_iota(jnp.int32, (span, 1), 0) < block
-    table = jnp.where(inside, own_ref[...].astype(f32), 0.0).astype(bf16)
-    acc[...] += first_first(d_logit, table)
+    acc[...] += first_first(d_logit, own_ref[...])
 
     @pl.when(step == pl.num_programs(0) - 1)
     def _():
@@ -924,15 +923,15 @@
 
 
 def head_back(logits, own, lse, dlp, aim):
-    block, width = own.shape
+    rows, width = own.shape
     n_rows = logits.shape[1]
-    span = 512
+    span = wide(rows)
     whole = lambda shape: pl.BlockSpec(shape, lambda i: (0,) * len(shape))
     return pl.pallas_call(
-        functools.partial(head_back_kernel, block, span),
-        grid=(pl.cdiv(block, span),),
+        head_back_kernel,
+        grid=(rows // span,),
         out_shape=[
-            jax.ShapeDtypeStruct((block, n_rows), jnp.bfloat16),
+            jax.ShapeDtypeStruct((rows, n_rows), jnp.bfloat16),
             jax.ShapeDtypeStruct((1, n_rows, width), jnp.bfloat16),
         ],
         in_specs=[
@@ -946,25 +945,35 @@
     )(logits, own, lse, dlp, aim)
 
 
+def adam_step(w, g, m, v, clip):
+    g = g.astype(jnp.float32) * clip
+    m_new = MOM1 * m + (1.0 - MOM1) * g
+    v_new = MOM2 * v + (1.0 - MOM2) * g * g
+    update = m_new / (1.0 - MOM1**STEP) / (jnp.sqrt(v_new / (1.0 - MOM2**STEP)) + EPS_ADAM)
+    return w - RATE * (update + DECAY * w), m_new, v_new, g
+
+
 def blend(parts, lane):
     f32 = jnp.float32
-    n_models = len(parts[0][1]) // 2
-    planes, stats = [], []
+    n_models = len(parts[0][0]) // PAIRS
+    is_top = lax.rem(lane, 32) < 16
+    stats = [p[1][0] for p in parts]
+    top = stats[0]
+    for s in stats[1:]:
+        top = jnp.maximum(top, s)
+    weights = [jnp.exp(jnp.where(is_top, s - top, 0.0)) for s in stats]
+    total = sum(s * pltpu.roll(w, 16, 1) for s, w in zip(stats, weights))
+    planes = []
     for model in range(n_models):
-        tops = [p[1][2 * model] for p in parts]
-        top = tops[0]
-        for t in tops[1:]:
-            top = jnp.maximum(top, t)
-        weights = [jnp.exp(t - top) for t in tops]
-        stats += [top, sum(p[1][2 * model + 1] * w for p, w in zip(parts, weights))]
         for pair in range(PAIRS):
+            at = 32 * model + 2 * pair
             acc = None
             for p, w in zip(parts, weights):
-                each = jnp.where(lane < 64, w[:, 2 * pair : 2 * pair + 1], w[:, 2 * pair + 1 : 2 * pair + 2])
+                each = jnp.where(lane < 64, w[:, at : at + 1], w[:, at + 1 : at + 2])
                 term = p[0][model * PAIRS + pair].astype(f32) * each
                 acc = term if acc is None else acc + term
             planes.append(acc)
-    return planes, stats
+    return planes, [jnp.where(is_top, top, total)]
 
 
 def mix_phase(ins, outs, scr, send_sems, recv_sems, line, plane, other):
@@ -1074,14 +1083,16 @@
     x1_ref, own_ref, lse_ref = extras
     lane = lax.broadcasted_iota(jnp.int32, (own_ref.shape[0], 128), 1)
     for model, w_ref in enumerate((w_one, w_two)):
-        total = totals[1][2 * model + 1]
-        total = jnp.where(lane < QUERY_HEADS, total, 1.0)
+        stats = totals[1][0]
         if model == 0:
-            lse_ref[...] = totals[1][0] + jnp.log(total)
-        share = 1.0 / total
+            total = jnp.where(lane < QUERY_HEADS, pltpu.roll(stats, 112, 1), 1.0)
+            lse_ref[...] = stats + jnp.log(total)
+        first = 32 * model + 16
+        share = 1.0 / jnp.where((lane >= first) & (lane < first + QUERY_HEADS), stats, 1.0)
         parts = []
         for p in range(PAIRS):
-            each = jnp.where(lane < 64, share[:, 2 * p : 2 * p + 1], share[:, 2 * p + 1 : 2 * p + 2])
+            at = first + 2 * p
+            each = jnp.where(lane < 64, share[:, at : at + 1], share[:, at + 1 : at + 2])
             parts.append(low(totals[0][model * PAIRS + p] * each))
         o = jnp.concatenate(parts, axis=1)
         if model == 0:
@@ -1205,6 +1216,10 @@
     feat = jnp.arange(MODEL_WIDTH, dtype=i32)
     padded = jnp.arange(devices * feats_up, dtype=i32)
     to_order = (padded[None, :] == (feat // feats * feats_up + feat % feats)[:, None]).astype(bf16)
+    owner = feat // feats
+    mp_of = owner // n_batch % n_mp
+    exchanged = ((mp_of % 2 * 2 + owner // (n_mp * n_batch)) * n_y + mp_of // 2) * n_batch + owner % n_batch
+    to_exchange = (padded[:, None] == (exchanged * feats_up + feat % feats)[None, :]).astype(bf16)
     from_order = (padded[:, None] == (feat // feats * feats_up + feat % feats)[None, :]).astype(bf16)
 
     def placed(x):
@@ -1258,6 +1273,10 @@
     row = (own_rows, MODEL_WIDTH)
     (x0,) = exchange("rows_found", 1, [picked], [], [], keep, [], [((2,) + row, f32)])
 
+    x0, tile_lo, tile_hi, targets, valid, to_exchange, from_order, flat_of, pos_of = lax.optimization_barrier(
+        (x0, tile_lo, tile_hi, targets, valid, to_exchange, from_order, flat_of, pos_of)
+    )
+
     w_kv = jnp.dot(to_order, early[:, 2 * MODEL_WIDTH : at_small], preferred_element_type=f32).astype(bf16)
     small_rows = small_params.shape[0]
     flat_small = jnp.sum(early[:, at_small:].astype(f32).reshape(devices, feats_up, -1), axis=0)
@@ -1300,7 +1319,7 @@
         [((2,) + row, f32)],
     )
 
-    aim = (targets - base).reshape(1, -1)
+    aim = jnp.where((targets >= base) & (targets < base + block), targets - base, -1).reshape(1, -1)
     stats, logits = head(low_table, ref_embed, af_all, aim)
     (stats_all,) = gather([stats[None]], 7)
     stats_all = stats_all.reshape(devices, 8, n_rows)
@@ -1343,14 +1362,13 @@
     g_gu, d_o_all = lax.optimization_barrier((g_gu, d_o_all))
     g_gu = lax.all_to_all(g_gu, AXES, split_axis=0, concat_axis=0, tiled=True)
     dq_part, g_kv_part, g_gain_kv, g_bias_kv, dx_tok = attend_back(
-        n_one, tile_lo, tile_hi, q_all[:PAIRS], d_o_all, row_stats_all[0], x_tok, kv_tok, w_kv, gain_attn[:1],
+        n_one, tile_lo, tile_hi, q_all, d_o_all, row_stats_all[0], x_tok, kv_tok, w_kv, gain_attn[:1],
         freq_wide, frow_wide, flat_of, pos_of, length, rp,
     )
     dq_part, g_gu = lax.optimization_barrier((dq_part, g_gu))
-    g_kv_part = g_kv_part.reshape(2, n_y, 2, n_batch, feats, 256).transpose(2, 0, 1, 3, 4, 5)
-    g_kv_part = jnp.pad(g_kv_part.reshape(devices, feats, 256), ((0, 0), (0, feats_up - feats), (0, 0)))
+    g_kv_part = jnp.dot(to_exchange, g_kv_part.astype(bf16), preferred_element_type=f32).astype(bf16)
     dq_all, d_row_all, g_kv, g_gain_row, g_bias_q = exchange(
-        "rows_queries_back", 12, [dq_part, g_kv_part.reshape(1, devices * feats_up, 256)],
+        "rows_queries_back", 12, [dq_part, g_kv_part[None]],
         [(early, 0, MODEL_WIDTH)], [from_order, gain_attn, x0, d_mid, cosine, sine], queries_back,
         [(1,) + row + (bf16,), (1,) + row + (bf16,)],
         [((feats_up, 256), f32), ((1, MODEL_WIDTH), f32), ((1, MODEL_WIDTH), f32)],
@@ -1359,7 +1377,7 @@
     dq_all = dq_all[0]
 
     embed_grad, embed_square = table_grad(
-        n_one, row_of, d_logits, af_all[0], d_row_all[0], frow.reshape(1, -1).astype(f32), flat_of, dx_tok, block
+        n_one, row_of, d_logits, af_all, d_row_all[0], frow.reshape(1, -1).astype(f32), flat_of, dx_tok, block
     )
 
     def mine(rows, grads):
@@ -1394,16 +1412,13 @@
     clip = jnp.minimum(1.0, CLIP / (norm + 1e-06))
     new_weights, new_firsts, new_seconds, new_lows, clipped_list = ([], [], [], [], [])
     for w, g, m, v in zip(masters, owned_grads, firsts, seconds):
-        g = g.astype(f32) * clip
-        m_new = MOM1 * m + (1.0 - MOM1) * g
-        v_new = MOM2 * v + (1.0 - MOM2) * g * g
-        update = m_new / (1.0 - MOM1**STEP) / (jnp.sqrt(v_new / (1.0 - MOM2**STEP)) + EPS_ADAM)
-        w_new = w - RATE * (update + DECAY * w)
+        w_new, m_new, v_new, g = adam_step(w, g, m, v, clip)
+        w_low = w_new.astype(bf16)
         new_weights.append(w_new)
         new_firsts.append(m_new)
         new_seconds.append(v_new)
         clipped_list.append(g)
-        new_lows.append(w_new.astype(bf16))
+        new_lows.append(w_low)
     return (
         *new_weights[:5], clipped_list[5], *new_firsts, *new_seconds, *new_lows[:5], norm,
     )

time: 566 us -> 546 us (0.965)
  Pallas kernels: 382 us -> 371 us
  local copies, waits for them, and re-layouts: 29.2 us -> 18.8 us
    pallas_call x7, Pallas kernels: 242 us -> 235 us  [exchange(): pl.pallas_call(functools.partial(exchange_kernel, n_in, columns, len(cons...]
    convert_element_type x6 -> x8, other arithmetic: 52.7 us -> 52 us  [the longest x5 48.7 us: body(): w_low = w_new.astype(bf16)]
where the time goes in v4:
time: 546 us; the launch traced here: 535 us
  Pallas kernels  371 us (68%)
  other arithmetic  80.8 us (15%)
  between operations  21.7 us (4%)
  matrix products  19.2 us (4%)
  local copies, waits for them, and re-layouts  18.8 us (3%)
  waiting for transfers between devices  13.9 us (3%)
  starting transfers between devices  10 us (2%)
    pallas_call x7, Pallas kernels, exchange(): pl.pallas_call(functools.partial(exchange_kernel, n_in, columns, len(cons...  235 us
    convert_element_type x5, other arithmetic, body(): w_low = w_new.astype(bf16)  48.7 us
    pallas_call x1, Pallas kernels, attend(): pl.pallas_call(functools.partial(attend_kernel, length, rp), grid=(2,), o...  23.9 us
    pallas_call x2, Pallas kernels, gather(): pl.pallas_call(functools.partial(gather_kernel, n), out_shape=[jax.ShapeD...  23.4 us
    pallas_call x1, Pallas kernels, lookup(): pl.pallas_call(functools.partial(lookup_kernel, block, span), grid=(steps...  19.8 us
    pallas_call x1, Pallas kernels, head(): pl.pallas_call(functools.partial(head_kernel, frozen.shape[0], span), gri...  19.1 us
    pallas_call x1, Pallas kernels, attend_back(): pl.pallas_call(functools.partial(attend_back_kernel, length, rp), grid=(1...  18.7 us
    pallas_call x1, Pallas kernels, table_grad(): pl.pallas_call(functools.partial(table_grad_kernel, span), grid=(steps,),...  14.9 us
  transfers between devices with their start and end apart: 4, of which 2 were waited for; matrix products, arithmetic and copies ran while one was open for 8% of the time, Pallas kernels for 31%

profile of v4, /device:TPU:0, one launch (start us, length us, event | category | flops | bytes accessed | tf_op | source)
XLA Modules:
  0.0 535.3 jit_solution(6865011949565457409)
XLA Ops:
  17.4 6.8 %sort.14 = (s32[8192]{0:T(1024)S(1)}, s32[8192]{0:T(1024)}) sort(s32[8192]{0:T(1024)S(1)} %fusion.74, s32[8192]{0:T(1024)S(1)} %iota.80), dimensions={0}, to_apply=%region_2.4 | sort | flops 106496 | bytes 131072 | tf_op jit(solution)/shard_map/sort | solution.py:1250
  26.3 19.8 %lookup.1 = (bf16[5120,896]{1,0:T(8,128)(2,1)}, bf16[2,512,896]{2,1,0:T(8,128)(2,1)}, bf16[2,8192,896]{2,1,0:T(8,128)(2,1)}) custom-call(s32[1]{0:T(128)} %bitcast.6.n_ref, s32[8192]{0:T(1024)} %get-tuple-element.264.rows_ref, f32[4748,896]{1,0:T(8,128)} %table_ref.1, bf16[4748,896]{1,0:T(8,128)(2,1)} %frozen_ref.5, s32[64,128]{1,0:T(8,128)} %get-tuple-element.95.flat_ref, ...), custom_call_target="tpu_custom_call" | custom-call | tf_op jit(solution)/shard_map/lookup/pallas_call | solution.py:391
  46.8 27.0 %rows_found.1.refs_7_.refs_6_.refs_5_ = f32[2,16,896]{2,1,0:T(8,128)} custom-call(bf16[2,512,896]{2,1,0:T(8,128)(2,1)} %get-tuple-element.87.refs_0_), custom_call_target="tpu_custom_call" | custom-call | tf_op jit(solution)/shard_map/rows_found/pallas_call | solution.py:276
  76.6 3.2 fusion.3
  88.4 27.3 %rows_queries.1 = (bf16[14,512,128]{2,1,0:T(8,128)(2,1)}, bf16[1,512,896]{2,1,0:T(8,128)(2,1)}) custom-call(bf16[1024,2560]{1,0:T(8,128)(2,1)} %all-gather.3.cloned.1.call-done.refs_0_.refs_1_.refs_2_, bf16[1024,2560]{1,0:T(8,128)(2,1)} %all-gather.3.cloned.1.call-done.refs_0_.refs_1_.refs_2_, bf16[896,1024]{1,0:T(8,128)(2,1)} %fusion.2.refs_2_.refs_4_, ...), custom_call_target="tpu_custom_call" | custom-call | tf_op jit(solution)/shard_map/rows_queries/pallas_call | solution.py:276
  115.7 5.8 %all-to-all-start = ((bf16[32,2,32,304]{3,2,1,0:T(8,128)(2,1)}), bf16[32,2,32,304]{3,2,1,0:T(8,128)(2,1)}, u32[]{:S(2)}, u32[]{:S(2)}) async-start(bf16[32,2,32,304]{3,2,1,0:T(8,128)(2,1)} %spread.1), calls=%async_computation | async-start | bytes 3145728 | tf_op jit(solution)/shard_map/all_to_all | solution.py:1300
  124.5 3.3 fusion.6.w_ref
  127.8 23.9 %attend.1 = (bf16[14,512,128]{2,1,0:T(8,128)(2,1)}, f32[1,512,128]{2,1,0:T(8,128)}, bf16[2,8192,256]{2,1,0:T(8,128)(2,1)}) custom-call(s32[1]{0:T(128)} %bitcast.6.n_ref, s32[64]{0:T(128)} %and_select_fusion.1.lo_ref, s32[64]{0:T(128)} %fusion.70.hi_ref, bf16[14,512,128]{2,1,0:T(8,128)(2,1)} %get-tuple-element.93.q_ref, ...), custom_call_target="tpu_custom_call" | custom-call | tf_op jit(solution)/shard_map/attend/pallas_call | solution.py:552
  151.7 12.1 %all-gather.5.cloned.1.call-done.refs_2_.refs_3_.refs_1_ = bf16[1024,1792]{1,0:T(8,128)(2,1)} async-done(((bf16[32,1792]{1,0:T(8,128)(2,1)}), bf16[1024,1792]{1,0:T(8,128)(2,1)}) %all-gather.5.cloned.1.call-update) | async-done | bytes 3670032 | tf_op jit(solution)/shard_map/all_gather | solution.py:1272
  165.0 47.2 %rows_attended.1 = (bf16[2,512,1024]{2,1,0:T(8,128)(2,1)}, bf16[1,512,896]{2,1,0:T(8,128)(2,1)}, f32[2,16,896]{2,1,0:T(8,128)}, bf16[16,896]{1,0:T(8,128)(2,1)}, f32[16,128]{1,0:T(8,128)}) custom-call(bf16[14,512,128]{2,1,0:T(8,128)(2,1)} %get-tuple-element.99.refs_0_, f32[1,512,128]{2,1,0:T(8,128)} %get-tuple-element.100.refs_1_, ...), custom_call_target="tpu_custom_call" | custom-call | tf_op jit(solution)/shard_map/rows_attended/pallas_call | solution.py:276
  218.3 34.0 %rows_finals.1 = (bf16[2,512,896]{2,1,0:T(8,128)(2,1)}, f32[2,16,896]{2,1,0:T(8,128)}) custom-call(bf16[2,512,896]{2,1,0:T(8,128)(2,1)} %pad_maximum_fusion.refs_0_, f32[2,1,896]{2,1,0:T(1,128)} %broadcast_in_dim.87.refs_1_, f32[2,16,896]{2,1,0:T(8,128)} %get-tuple-element.105.refs_2_.refs_4_), custom_call_target="tpu_custom_call" | custom-call | tf_op jit(solution)/shard_map/rows_finals/pallas_call | solution.py:276
  252.2 19.1 %head.1 = (f32[8,512]{1,0:T(8,128)}, f32[5120,512]{1,0:T(8,128)}) custom-call(bf16[5120,896]{1,0:T(8,128)(2,1)} %get-tuple-element.103.own_ref, bf16[4748,896]{1,0:T(8,128)(2,1)} %frozen_ref.5, bf16[2,512,896]{2,1,0:T(8,128)(2,1)} %get-tuple-element.106.af_ref, s32[1,512]{1,0:T(1,128)} %bitcast.175), custom_call_target="tpu_custom_call" | custom-call | tf_op jit(solution)/shard_map/head/pallas_call | solution.py:892
  272.1 11.1 %gather_7.1 = f32[1,256,512]{2,1,0:T(8,128)S(1)} custom-call(f32[1,8,512]{2,1,0:T(8,128)S(1)} %bitcast.159), custom_call_target="tpu_custom_call" | custom-call | tf_op jit(solution)/shard_map/gather_7/pallas_call | solution.py:149
  285.2 13.6 %head_back.1 = (bf16[5120,512]{1,0:T(8,128)(2,1)}, bf16[1,512,896]{2,1,0:T(8,128)(2,1)}) custom-call(f32[5120,512]{1,0:T(8,128)} %get-tuple-element.108.logit_ref, bf16[5120,896]{1,0:T(8,128)(2,1)} %get-tuple-element.103.own_ref, f32[1,512]{1,0:T(1,128)} %bitcast.177, f32[1,512]{1,0:T(1,128)} %reshape_reshape.8.dlp_ref, s32[1,512]{1,0:T(1,128)} %bitcast.176), custom_call_target="tpu_custom_call" | custom-call | tf_op jit(solution)/shard_map/head_back/pallas_call | solution.py:930
  298.8 25.7 %rows_finals_back.1 = (bf16[1,512,896]{2,1,0:T(8,128)(2,1)}, f32[16,896]{1,0:T(8,128)}, f32[1,896]{1,0:T(1,128)}) custom-call(bf16[1,512,896]{2,1,0:T(8,128)(2,1)} %get-tuple-element.111.refs_0_, f32[2,1,896]{2,1,0:T(1,128)} %broadcast_in_dim.87.refs_1_, f32[2,16,896]{2,1,0:T(8,128)} %get-tuple-element.112.refs_2_), custom_call_target="tpu_custom_call" | custom-call | tf_op jit(solution)/shard_map/rows_finals_back/pallas_call | solution.py:276
  330.5 34.1 %rows_attended_back.1 = (bf16[1,512,896]{2,1,0:T(8,128)(2,1)}, bf16[7,512,128]{2,1,0:T(8,128)(2,1)}, f32[1,512,128]{2,1,0:T(8,128)}, f32[16,896]{1,0:T(8,128)}, f32[1,896]{1,0:T(1,128)}) custom-call(bf16[1,512,1024]{2,1,0:T(8,128)(2,1)} %fusion.7.refs_0_, bf16[1024,1792]{1,0:T(8,128)(2,1)} %all-gather.5.cloned.1.call-done.refs_2_.refs_3_.refs_1_, ...), custom_call_target="tpu_custom_call" | custom-call | tf_op jit(solution)/shard_map/rows_attended_back/pallas_call | solution.py:276
  364.6 4.1 all-to-all-start.1
  370.6 18.7 %attend_back.1 = (bf16[7,512,128]{2,1,0:T(8,128)(2,1)}, f32[896,256]{1,0:T(8,128)}, f32[8,896]{1,0:T(8,128)}, f32[8,256]{1,0:T(8,128)}, bf16[8192,896]{1,0:T(8,128)(2,1)}) custom-call(s32[1]{0:T(128)} %bitcast.6.n_ref, s32[64]{0:T(128)} %and_select_fusion.1.lo_ref, s32[64]{0:T(128)} %fusion.70.hi_ref, bf16[14,512,128]{2,1,0:T(8,128)(2,1)} %get-tuple-element.93.q_ref, ...), custom_call_target="tpu_custom_call" | custom-call | tf_op jit(solution)/shard_map/attend_back/pallas_call | solution.py:695
  393.1 3.2 fusion.11.refs_1_
  398.1 39.9 %rows_queries_back.1 = (bf16[1,512,896]{2,1,0:T(8,128)(2,1)}, bf16[1,512,896]{2,1,0:T(8,128)(2,1)}, f32[32,256]{1,0:T(8,128)}, f32[1,896]{1,0:T(1,128)}, f32[1,896]{1,0:T(1,128)}) custom-call(bf16[7,512,128]{2,1,0:T(8,128)(2,1)} %get-tuple-element.124.refs_0_, bf16[1,1024,256]{2,1,0:T(8,128)(2,1)} %fusion.11.refs_1_, ...), custom_call_target="tpu_custom_call" | custom-call | tf_op jit(solution)/shard_map/rows_queries_back/pallas_call | solution.py:276
  438.0 14.9 %table_grad.1 = (bf16[4748,896]{1,0:T(8,128)(2,1)}, f32[8,896]{1,0:T(8,128)}) custom-call(s32[1]{0:T(128)} %bitcast.6.n_ref, s32[8192]{0:T(1024)} %get-tuple-element.264.rows_ref, bf16[5120,512]{1,0:T(8,128)(2,1)} %get-tuple-element.138.dl_ref, bf16[2,512,896]{2,1,0:T(8,128)(2,1)} %get-tuple-element.106.af_ref, bf16[512,896]{1,0:T(8,128)(2,1)} %bitcast.165, ...), custom_call_target="tpu_custom_call" | custom-call | tf_op jit(solution)/shard_map/table_grad/pallas_call | solution.py:787
  460.1 12.3 %gather_14.1 = f32[1,1024,128]{2,1,0:T(8,128)S(1)} custom-call(f32[1,32,128]{2,1,0:T(8,128)S(1)} %bitcast.158), custom_call_target="tpu_custom_call" | custom-call | tf_op jit(solution)/shard_map/gather_14/pallas_call | solution.py:149
  478.3 42.6 %fusion.112 = (bf16[4748,896]{1,0:T(8,128)(2,1)}, f32[4748,896]{1,0:T(8,128)}, f32[4748,896]{1,0:T(8,128)}, f32[4748,896]{1,0:T(8,128)}) fusion(f32[4748,896]{1,0:T(8,128)} %table_ref.1, f32[]{:T(128)S(6)} %min.3, bf16[4748,896]{1,0:T(8,128)(2,1)} %get-tuple-element.143, f32[4748,896]{1,0:T(8,128)} %param.44, f32[4748,896]{1,0:T(8,128)} %param.50), kind=kLoop, calls=%fused_computation.248 | loop fusion | flops 72321536 | bytes 119117824 | tf_op jit(solution)/shard_map/convert_element_type | solution.py:1416
  523.2 2.8 fusion.116
  (202 shorter events, 60.9 us)
Async XLA Ops:
  7.2 209.2 %copy-start = (bf16[152,896]{1,0:T(8,128)(2,1)S(1)}, bf16[152,896]{1,0:T(8,128)(2,1)}, u32[]{:S(2)}) copy-start(bf16[152,896]{1,0:T(8,128)(2,1)} %param.55) | copy-start | bytes 817156
  7.2 78.8 %all-gather.3.cloned.1.call-start = ((), (), s32[]{:S(2)}) async-start(), calls=%async_computation.2 | async-start | bytes 5406720 | tf_op jit(solution)/shard_map/all_gather | solution.py:1239
  12.2 151.5 %all-gather.5.cloned.1.call-start = ((), (), s32[]{:S(2)}) async-start(), calls=%async_computation.3 | async-start | bytes 3784704 | tf_op jit(solution)/shard_map/all_gather | solution.py:1272
  26.3 19.8 %copy-start.25 = (bf16[28,896]{1,0:T(8,128)(2,1)S(1)}, bf16[28,896]{1,0:T(8,128)(2,1)}, u32[]{:S(2)}) copy-start(bf16[28,896]{1,0:T(8,128)(2,1)} %param.53) | copy-start | bytes 150532
  46.1 27.8 %copy-start.21 = (s32[2,4,4,256]{3,2,1,0:T(4,128)S(1)}, s32[2,4,4,256]{3,2,1,0:T(4,128)}, u32[]{:S(2)}) copy-start(s32[2,4,4,256]{3,2,1,0:T(4,128)} %param.30) | copy-start | bytes 98308
  46.1 28.5 %copy-start.13 = (s32[64,128]{1,0:T(8,128)S(1)}, s32[64,128]{1,0:T(8,128)}, u32[]{:S(2)}) copy-start(s32[64,128]{1,0:T(8,128)} %get-tuple-element.95.flat_ref) | copy-start | bytes 98308
  73.8 6.1 %copy-start.2 = (f32[28,9728]{1,0:T(8,128)S(1)}, f32[28,9728]{1,0:T(8,128)}, u32[]{:S(2)}) copy-start(f32[28,9728]{1,0:T(8,128)} %own_ref.1) | copy-start | bytes 3268612
  115.7 6.6 %copy-start.31 = (s32[2,4]{1,0:T(2,128)S(1)}, s32[2,4]{1,0:T(2,128)}, u32[]{:S(2)}) copy-start(s32[2,4]{1,0:T(2,128)} %param.32) | copy-start | bytes 100
  115.7 6.7 %copy-start.29 = (f32[30,4]{0,1:T(4,128)S(1)}, f32[30,4]{0,1:T(4,128)}, u32[]{:S(2)}) copy-start(f32[30,4]{0,1:T(4,128)} %param.51) | copy-start | bytes 1444
  115.7 6.8 %copy-start.30 = (f32[30,4]{0,1:T(4,128)S(1)}, f32[30,4]{0,1:T(4,128)}, u32[]{:S(2)}) copy-start(f32[30,4]{0,1:T(4,128)} %param.45) | copy-start | bytes 1444
  115.7 96.4 %all-to-all-start = ((bf16[32,2,32,304]{3,2,1,0:T(8,128)(2,1)}), bf16[32,2,32,304]{3,2,1,0:T(8,128)(2,1)}, u32[]{:S(2)}, u32[]{:S(2)}) async-start(bf16[32,2,32,304]{3,2,1,0:T(8,128)(2,1)} %spread.1), calls=%async_computation | async-start | bytes 3145728 | tf_op jit(solution)/shard_map/all_to_all | solution.py:1300
  285.2 39.3 %copy-start.6 = (f32[152,896]{1,0:T(8,128)S(1)}, f32[152,896]{1,0:T(8,128)}, u32[]{:S(2)}) copy-start(f32[152,896]{1,0:T(8,128)} %param.37) | copy-start | bytes 1634308
  330.4 40.1 %copy-start.26 = (f32[1,896]{1,0:T(1,128)S(1)}, f32[1,896]{1,0:T(1,128)}, u32[]{:S(2)}) copy-start(f32[1,896]{1,0:T(1,128)} %get-tuple-element.133) | copy-start | bytes 10756
  364.6 33.5 %all-to-all-start.1 = ((bf16[32,32,304]{2,1,0:T(8,128)(2,1)}), bf16[32,32,304]{2,1,0:T(8,128)(2,1)S(1)}, u32[]{:S(2)}, u32[]{:S(2)}) async-start(bf16[32,32,304]{2,1,0:T(8,128)(2,1)} %bitcast.162), calls=%async_computation.1 | async-start | bytes 1572864 | tf_op jit(solution)/shard_map/all_to_all | solution.py:1363
  438.0 16.3 %copy-start.28 = (f32[1,896]{1,0:T(1,128)S(1)}, f32[1,896]{1,0:T(1,128)}, u32[]{:S(2)}) copy-start(f32[1,896]{1,0:T(1,128)} %get-tuple-element.131) | copy-start | bytes 10756
  438.0 16.3 %copy-start.27 = (f32[1,896]{1,0:T(1,128)S(1)}, f32[1,896]{1,0:T(1,128)}, u32[]{:S(2)}) copy-start(f32[1,896]{1,0:T(1,128)} %get-tuple-element.134) | copy-start | bytes 10756
  438.0 18.1 %copy-start.22 = (f32[32,256]{1,0:T(8,128)S(1)}, f32[32,256]{1,0:T(8,128)}, u32[]{:S(2)}) copy-start(f32[32,256]{1,0:T(8,128)} %get-tuple-element.129) | copy-start | bytes 98308
  454.4 23.0 %copy-start.15 = (f32[28,1152]{1,0:T(8,128)S(1)}, f32[28,1152]{1,0:T(8,128)}, u32[]{:S(2)}) copy-start(f32[28,1152]{1,0:T(8,128)} %param.34) | copy-start | bytes 387076
  454.4 23.0 %copy-start.19 = (f32[28,1152]{1,0:T(8,128)S(1)}, f32[28,1152]{1,0:T(8,128)}, u32[]{:S(2)}) copy-start(f32[28,1152]{1,0:T(8,128)} %param.40) | copy-start | bytes 387076
  454.4 23.0 %copy-start.20 = (f32[28,1152]{1,0:T(8,128)S(1)}, f32[28,1152]{1,0:T(8,128)}, u32[]{:S(2)}) copy-start(f32[28,1152]{1,0:T(8,128)} %param.46) | copy-start | bytes 387076
  478.2 42.6 %copy-start.7 = (f32[152,896]{1,0:T(8,128)S(1)}, f32[152,896]{1,0:T(8,128)}, u32[]{:S(2)}) copy-start(f32[152,896]{1,0:T(8,128)} %param.37) | copy-start | bytes 1634308
  478.2 42.6 %copy-start.8 = (f32[152,896]{1,0:T(8,128)S(1)}, f32[152,896]{1,0:T(8,128)}, u32[]{:S(2)}) copy-start(f32[152,896]{1,0:T(8,128)} %get-tuple-element.277) | copy-start | bytes 1634308
  478.2 42.7 %copy-start.16 = (f32[152,896]{1,0:T(8,128)S(1)}, f32[152,896]{1,0:T(8,128)}, u32[]{:S(2)}) copy-start(f32[152,896]{1,0:T(8,128)} %param.43) | copy-start | bytes 1634308
  478.2 42.7 %copy-start.17 = (f32[152,896]{1,0:T(8,128)S(1)}, f32[152,896]{1,0:T(8,128)}, u32[]{:S(2)}) copy-start(f32[152,896]{1,0:T(8,128)} %param.49) | copy-start | bytes 1634308
  (12 other events, 35.3 us)
Sparse Core Ops, SparseCore 0:
  12.4 73.5 all-gather.2
  89.4 74.3 all-gather.4

commit v5 on v4

--- a/solution.py
+++ b/solution.py
@@ -871,7 +871,8 @@
 
     inside = step * span + lax.broadcasted_iota(jnp.int32, (span, 1), 0) < block
     shift = jnp.where(inside, 0.0, -1e30)
-    frozen = jnp.where(inside, frozen_ref[...].astype(f32), 0.0).astype(jnp.bfloat16)
+    frozen = frozen_ref[...]
+    frozen = jnp.where(jnp.broadcast_to(inside, frozen.shape), frozen, jnp.zeros_like(frozen))
     logits = [last_last(own_ref[...], af_ref[0]) + shift, last_last(frozen, af_ref[1]) + shift]
     logit_ref[...] = logits[0]
     hit = lax.broadcasted_iota(jnp.int32, (span, n_rows), 0) == aim_ref[...] - step * span
@@ -1247,7 +1248,7 @@
     bits = max(1, (block - 1).bit_length())
     local = (ids >= base) & (ids < base + block) & (spots[None, :] < lens[:, None])
     key = jnp.where(local, (flat_ids << bits) + (ids - base), jnp.int32(2**31 - 1)).reshape(-1)
-    key = lax.sort(key)
+    key = lax.sort(key, is_stable=False)
     n_local = jnp.sum(local.astype(i32))
     live = jnp.arange(rollouts * length, dtype=i32) < n_local
     row_of = jnp.where(live, key & ((1 << bits) - 1), 0)

time: 546 us -> 547 us (level)
  no operation moved by 1% of the time
where the time goes in v5:
time: 547 us; the launch traced here: 540 us
  Pallas kernels  375 us (69%)
  other arithmetic  78.7 us (14%)
  between operations  21.8 us (4%)
  local copies, waits for them, and re-layouts  20.5 us (4%)
  matrix products  19.8 us (4%)
  waiting for transfers between devices  13.3 us (2%)
  starting transfers between devices  10 us (2%)
    pallas_call x7, Pallas kernels, exchange(): pl.pallas_call(functools.partial(exchange_kernel, n_in, columns, len(cons...  237 us
    convert_element_type x5, other arithmetic, body(): w_low = w_new.astype(bf16)  48.7 us
    pallas_call x2, Pallas kernels, gather(): pl.pallas_call(functools.partial(gather_kernel, n), out_shape=[jax.ShapeD...  25.4 us
    pallas_call x1, Pallas kernels, attend(): pl.pallas_call(functools.partial(attend_kernel, length, rp), grid=(2,), o...  23.9 us
    pallas_call x1, Pallas kernels, lookup(): pl.pallas_call(functools.partial(lookup_kernel, block, span), grid=(steps...  19.8 us
    pallas_call x1, Pallas kernels, head(): pl.pallas_call(functools.partial(head_kernel, frozen.shape[0], span), gri...  19.6 us
    pallas_call x1, Pallas kernels, attend_back(): pl.pallas_call(functools.partial(attend_back_kernel, length, rp), grid=(1...  18.7 us
    pallas_call x1, Pallas kernels, table_grad(): pl.pallas_call(functools.partial(table_grad_kernel, span), grid=(steps,),...  15.1 us
  transfers between devices with their start and end apart: 4, of which 2 were waited for; matrix products, arithmetic and copies ran while one was open for 8% of the time, Pallas kernels for 31%

profile of v5, /device:TPU:0, one launch (start us, length us, event | category | flops | bytes accessed | tf_op | source)
XLA Modules:
  0.0 539.5 jit_solution(4950349216063328494)
XLA Ops:
  14.8 5.6 %sort.7 = s32[8192]{0:T(1024)S(1)} sort(s32[8192]{0:T(1024)S(1)} %fusion.74), dimensions={0}, to_apply=%region_2.4 | sort | flops 106496 | bytes 65536 | tf_op jit(solution)/shard_map/sort | solution.py:1251
  24.2 19.8 %lookup.1 = (bf16[5120,896]{1,0:T(8,128)(2,1)}, bf16[2,512,896]{2,1,0:T(8,128)(2,1)}, bf16[2,8192,896]{2,1,0:T(8,128)(2,1)}) custom-call(s32[1]{0:T(128)} %bitcast.6.n_ref, s32[8192]{0:T(1024)} %get-tuple-element.261.rows_ref, f32[4748,896]{1,0:T(8,128)} %table_ref.1, bf16[4748,896]{1,0:T(8,128)(2,1)} %frozen_ref.5, s32[64,128]{1,0:T(8,128)} %get-tuple-element.92.flat_ref, ...), custom_call_target="tpu_custom_call" | custom-call | tf_op jit(solution)/shard_map/lookup/pallas_call | solution.py:391
  44.8 28.0 %rows_found.1.refs_7_.refs_6_.refs_5_ = f32[2,16,896]{2,1,0:T(8,128)} custom-call(bf16[2,512,896]{2,1,0:T(8,128)(2,1)} %get-tuple-element.84.refs_0_), custom_call_target="tpu_custom_call" | custom-call | tf_op jit(solution)/shard_map/rows_found/pallas_call | solution.py:276
  75.5 3.2 fusion.3
  83.1 3.2 all-gather.3.cloned.1.call-done.refs_0_.refs_1_.refs_2_
  88.8 26.9 %rows_queries.1 = (bf16[14,512,128]{2,1,0:T(8,128)(2,1)}, bf16[1,512,896]{2,1,0:T(8,128)(2,1)}) custom-call(bf16[1024,2560]{1,0:T(8,128)(2,1)} %all-gather.3.cloned.1.call-done.refs_0_.refs_1_.refs_2_, bf16[1024,2560]{1,0:T(8,128)(2,1)} %all-gather.3.cloned.1.call-done.refs_0_.refs_1_.refs_2_, bf16[896,1024]{1,0:T(8,128)(2,1)} %fusion.2.refs_2_.refs_4_, ...), custom_call_target="tpu_custom_call" | custom-call | tf_op jit(solution)/shard_map/rows_queries/pallas_call | solution.py:276
  115.8 5.8 %all-to-all-start = ((bf16[32,2,32,304]{3,2,1,0:T(8,128)(2,1)}), bf16[32,2,32,304]{3,2,1,0:T(8,128)(2,1)}, u32[]{:S(2)}, u32[]{:S(2)}) async-start(bf16[32,2,32,304]{3,2,1,0:T(8,128)(2,1)} %spread.1), calls=%async_computation | async-start | bytes 3145728 | tf_op jit(solution)/shard_map/all_to_all | solution.py:1301
  126.1 3.3 fusion.6.w_ref
  129.4 23.9 %attend.1 = (bf16[14,512,128]{2,1,0:T(8,128)(2,1)}, f32[1,512,128]{2,1,0:T(8,128)}, bf16[2,8192,256]{2,1,0:T(8,128)(2,1)}) custom-call(s32[1]{0:T(128)} %bitcast.6.n_ref, s32[64]{0:T(128)} %and_select_fusion.1.lo_ref, s32[64]{0:T(128)} %fusion.70.hi_ref, bf16[14,512,128]{2,1,0:T(8,128)(2,1)} %get-tuple-element.90.q_ref, ...), custom_call_target="tpu_custom_call" | custom-call | tf_op jit(solution)/shard_map/attend/pallas_call | solution.py:552
  153.3 10.1 %all-gather.5.cloned.1.call-done.refs_2_.refs_3_.refs_1_ = bf16[1024,1792]{1,0:T(8,128)(2,1)} async-done(((bf16[32,1792]{1,0:T(8,128)(2,1)}), bf16[1024,1792]{1,0:T(8,128)(2,1)}) %all-gather.5.cloned.1.call-update) | async-done | bytes 3670032 | tf_op jit(solution)/shard_map/all_gather | solution.py:1273
  164.6 46.9 %rows_attended.1 = (bf16[2,512,1024]{2,1,0:T(8,128)(2,1)}, bf16[1,512,896]{2,1,0:T(8,128)(2,1)}, f32[2,16,896]{2,1,0:T(8,128)}, bf16[16,896]{1,0:T(8,128)(2,1)}, f32[16,128]{1,0:T(8,128)}) custom-call(bf16[14,512,128]{2,1,0:T(8,128)(2,1)} %get-tuple-element.96.refs_0_, f32[1,512,128]{2,1,0:T(8,128)} %get-tuple-element.97.refs_1_, ...), custom_call_target="tpu_custom_call" | custom-call | tf_op jit(solution)/shard_map/rows_attended/pallas_call | solution.py:276
  217.6 33.7 %rows_finals.1 = (bf16[2,512,896]{2,1,0:T(8,128)(2,1)}, f32[2,16,896]{2,1,0:T(8,128)}) custom-call(bf16[2,512,896]{2,1,0:T(8,128)(2,1)} %pad_maximum_fusion.refs_0_, f32[2,1,896]{2,1,0:T(1,128)} %broadcast_in_dim.87.refs_1_, f32[2,16,896]{2,1,0:T(8,128)} %get-tuple-element.102.refs_2_.refs_4_), custom_call_target="tpu_custom_call" | custom-call | tf_op jit(solution)/shard_map/rows_finals/pallas_call | solution.py:276
  251.3 19.6 %head.1 = (f32[8,512]{1,0:T(8,128)}, f32[5120,512]{1,0:T(8,128)}) custom-call(bf16[5120,896]{1,0:T(8,128)(2,1)} %get-tuple-element.100.own_ref, bf16[4748,896]{1,0:T(8,128)(2,1)} %frozen_ref.5, bf16[2,512,896]{2,1,0:T(8,128)(2,1)} %get-tuple-element.103.af_ref, s32[1,512]{1,0:T(1,128)} %bitcast.175), custom_call_target="tpu_custom_call" | custom-call | tf_op jit(solution)/shard_map/head/pallas_call | solution.py:893
  271.6 11.5 %gather_7.1 = f32[1,256,512]{2,1,0:T(8,128)S(1)} custom-call(f32[1,8,512]{2,1,0:T(8,128)S(1)} %bitcast.159), custom_call_target="tpu_custom_call" | custom-call | tf_op jit(solution)/shard_map/gather_7/pallas_call | solution.py:149
  285.0 13.6 %head_back.1 = (bf16[5120,512]{1,0:T(8,128)(2,1)}, bf16[1,512,896]{2,1,0:T(8,128)(2,1)}) custom-call(f32[5120,512]{1,0:T(8,128)} %get-tuple-element.105.logit_ref, bf16[5120,896]{1,0:T(8,128)(2,1)} %get-tuple-element.100.own_ref, f32[1,512]{1,0:T(1,128)} %bitcast.177, f32[1,512]{1,0:T(1,128)} %reshape_reshape.8.dlp_ref, s32[1,512]{1,0:T(1,128)} %bitcast.176), custom_call_target="tpu_custom_call" | custom-call | tf_op jit(solution)/shard_map/head_back/pallas_call | solution.py:931
  298.6 25.1 %rows_finals_back.1 = (bf16[1,512,896]{2,1,0:T(8,128)(2,1)}, f32[16,896]{1,0:T(8,128)}, f32[1,896]{1,0:T(1,128)}) custom-call(bf16[1,512,896]{2,1,0:T(8,128)(2,1)} %get-tuple-element.108.refs_0_, f32[2,1,896]{2,1,0:T(1,128)} %broadcast_in_dim.87.refs_1_, f32[2,16,896]{2,1,0:T(8,128)} %get-tuple-element.109.refs_2_), custom_call_target="tpu_custom_call" | custom-call | tf_op jit(solution)/shard_map/rows_finals_back/pallas_call | solution.py:276
  329.8 34.3 %rows_attended_back.1 = (bf16[1,512,896]{2,1,0:T(8,128)(2,1)}, bf16[7,512,128]{2,1,0:T(8,128)(2,1)}, f32[1,512,128]{2,1,0:T(8,128)}, f32[16,896]{1,0:T(8,128)}, f32[1,896]{1,0:T(1,128)}) custom-call(bf16[1,512,1024]{2,1,0:T(8,128)(2,1)} %fusion.7.refs_0_, bf16[1024,1792]{1,0:T(8,128)(2,1)} %all-gather.5.cloned.1.call-done.refs_2_.refs_3_.refs_1_, ...), custom_call_target="tpu_custom_call" | custom-call | tf_op jit(solution)/shard_map/rows_attended_back/pallas_call | solution.py:276
  364.1 4.2 all-to-all-start.1
  370.2 18.7 %attend_back.1 = (bf16[7,512,128]{2,1,0:T(8,128)(2,1)}, f32[896,256]{1,0:T(8,128)}, f32[8,896]{1,0:T(8,128)}, f32[8,256]{1,0:T(8,128)}, bf16[8192,896]{1,0:T(8,128)(2,1)}) custom-call(s32[1]{0:T(128)} %bitcast.6.n_ref, s32[64]{0:T(128)} %and_select_fusion.1.lo_ref, s32[64]{0:T(128)} %fusion.70.hi_ref, bf16[14,512,128]{2,1,0:T(8,128)(2,1)} %get-tuple-element.90.q_ref, ...), custom_call_target="tpu_custom_call" | custom-call | tf_op jit(solution)/shard_map/attend_back/pallas_call | solution.py:695
  393.3 3.2 fusion.11.refs_1_
  398.2 42.2 %rows_queries_back.1 = (bf16[1,512,896]{2,1,0:T(8,128)(2,1)}, bf16[1,512,896]{2,1,0:T(8,128)(2,1)}, f32[32,256]{1,0:T(8,128)}, f32[1,896]{1,0:T(1,128)}, f32[1,896]{1,0:T(1,128)}) custom-call(bf16[7,512,128]{2,1,0:T(8,128)(2,1)} %get-tuple-element.121.refs_0_, bf16[1,1024,256]{2,1,0:T(8,128)(2,1)} %fusion.11.refs_1_, ...), custom_call_target="tpu_custom_call" | custom-call | tf_op jit(solution)/shard_map/rows_queries_back/pallas_call | solution.py:276
  440.5 15.1 %table_grad.1 = (bf16[4748,896]{1,0:T(8,128)(2,1)}, f32[8,896]{1,0:T(8,128)}) custom-call(s32[1]{0:T(128)} %bitcast.6.n_ref, s32[8192]{0:T(1024)} %get-tuple-element.261.rows_ref, bf16[5120,512]{1,0:T(8,128)(2,1)} %get-tuple-element.135.dl_ref, bf16[2,512,896]{2,1,0:T(8,128)(2,1)} %get-tuple-element.103.af_ref, bf16[512,896]{1,0:T(8,128)(2,1)} %bitcast.165, ...), custom_call_target="tpu_custom_call" | custom-call | tf_op jit(solution)/shard_map/table_grad/pallas_call | solution.py:787
  462.7 13.9 %gather_14.1 = f32[1,1024,128]{2,1,0:T(8,128)S(1)} custom-call(f32[1,32,128]{2,1,0:T(8,128)S(1)} %bitcast.158), custom_call_target="tpu_custom_call" | custom-call | tf_op jit(solution)/shard_map/gather_14/pallas_call | solution.py:149
  482.5 42.6 %fusion.112 = (bf16[4748,896]{1,0:T(8,128)(2,1)}, f32[4748,896]{1,0:T(8,128)}, f32[4748,896]{1,0:T(8,128)}, f32[4748,896]{1,0:T(8,128)}) fusion(f32[4748,896]{1,0:T(8,128)} %table_ref.1, f32[]{:T(128)S(6)} %min.3, bf16[4748,896]{1,0:T(8,128)(2,1)} %get-tuple-element.140, f32[4748,896]{1,0:T(8,128)} %param.44, f32[4748,896]{1,0:T(8,128)} %param.50), kind=kLoop, calls=%fused_computation.248 | loop fusion | flops 72321536 | bytes 119117824 | tf_op jit(solution)/shard_map/convert_element_type | solution.py:1417
  (209 shorter events, 63.4 us)
Async XLA Ops:
  7.2 208.5 %copy-start = (bf16[152,896]{1,0:T(8,128)(2,1)S(1)}, bf16[152,896]{1,0:T(8,128)(2,1)}, u32[]{:S(2)}) copy-start(bf16[152,896]{1,0:T(8,128)(2,1)} %param.55) | copy-start | bytes 817156
  7.2 14.8 %copy-start.18 = (f32[28,896]{1,0:T(8,128)S(1)}, f32[28,896]{1,0:T(8,128)}, u32[]{:S(2)}) copy-start(f32[28,896]{1,0:T(8,128)} %param.35) | copy-start | bytes 301060
  7.2 79.2 %all-gather.3.cloned.1.call-start = ((), (), s32[]{:S(2)}) async-start(), calls=%async_computation.2 | async-start | bytes 5406720 | tf_op jit(solution)/shard_map/all_gather | solution.py:1240
  12.3 151.1 %all-gather.5.cloned.1.call-start = ((), (), s32[]{:S(2)}) async-start(), calls=%async_computation.3 | async-start | bytes 3784704 | tf_op jit(solution)/shard_map/all_gather | solution.py:1273
  24.2 19.8 %copy-start.26 = (bf16[28,896]{1,0:T(8,128)(2,1)S(1)}, bf16[28,896]{1,0:T(8,128)(2,1)}, u32[]{:S(2)}) copy-start(bf16[28,896]{1,0:T(8,128)(2,1)} %param.53) | copy-start | bytes 150532
  44.1 28.9 %copy-start.22 = (s32[2,4,4,256]{3,2,1,0:T(4,128)S(1)}, s32[2,4,4,256]{3,2,1,0:T(4,128)}, u32[]{:S(2)}) copy-start(s32[2,4,4,256]{3,2,1,0:T(4,128)} %param.30) | copy-start | bytes 98308
  44.1 29.5 %copy-start.13 = (s32[64,128]{1,0:T(8,128)S(1)}, s32[64,128]{1,0:T(8,128)}, u32[]{:S(2)}) copy-start(s32[64,128]{1,0:T(8,128)} %get-tuple-element.92.flat_ref) | copy-start | bytes 98308
  115.8 95.8 %all-to-all-start = ((bf16[32,2,32,304]{3,2,1,0:T(8,128)(2,1)}), bf16[32,2,32,304]{3,2,1,0:T(8,128)(2,1)}, u32[]{:S(2)}, u32[]{:S(2)}) async-start(bf16[32,2,32,304]{3,2,1,0:T(8,128)(2,1)} %spread.1), calls=%async_computation | async-start | bytes 3145728 | tf_op jit(solution)/shard_map/all_to_all | solution.py:1301
  251.3 33.0 %copy-start.35 = (f32[8]{0:T(128)S(1)}, f32[8]{0:T(128)}, u32[]{:S(2)}) copy-start(f32[8]{0:T(128)} %convert_element_type.120) | copy-start | bytes 100
  285.0 38.7 %copy-start.6 = (f32[152,896]{1,0:T(8,128)S(1)}, f32[152,896]{1,0:T(8,128)}, u32[]{:S(2)}) copy-start(f32[152,896]{1,0:T(8,128)} %param.37) | copy-start | bytes 1634308
  329.8 38.5 %copy-start.27 = (s32[1,512]{1,0:T(1,128)S(1)}, s32[1,512]{1,0:T(1,128)}, u32[]{:S(2)}) copy-start(s32[1,512]{1,0:T(1,128)} %reshape.395) | copy-start | bytes 6148
  329.8 38.5 %copy-start.28 = (s32[1,512]{1,0:T(1,128)S(1)}, s32[1,512]{1,0:T(1,128)}, u32[]{:S(2)}) copy-start(s32[1,512]{1,0:T(1,128)} %add.429) | copy-start | bytes 6148
  329.8 40.4 %copy-start.29 = (f32[1,896]{1,0:T(1,128)S(1)}, f32[1,896]{1,0:T(1,128)}, u32[]{:S(2)}) copy-start(f32[1,896]{1,0:T(1,128)} %get-tuple-element.130) | copy-start | bytes 10756
  364.1 34.2 %all-to-all-start.1 = ((bf16[32,32,304]{2,1,0:T(8,128)(2,1)}), bf16[32,32,304]{2,1,0:T(8,128)(2,1)S(1)}, u32[]{:S(2)}, u32[]{:S(2)}) async-start(bf16[32,32,304]{2,1,0:T(8,128)(2,1)} %bitcast.162), calls=%async_computation.1 | async-start | bytes 1572864 | tf_op jit(solution)/shard_map/all_to_all | solution.py:1364
  440.5 16.5 %copy-start.31 = (f32[1,896]{1,0:T(1,128)S(1)}, f32[1,896]{1,0:T(1,128)}, u32[]{:S(2)}) copy-start(f32[1,896]{1,0:T(1,128)} %get-tuple-element.128) | copy-start | bytes 10756
  440.5 16.5 %copy-start.30 = (f32[1,896]{1,0:T(1,128)S(1)}, f32[1,896]{1,0:T(1,128)}, u32[]{:S(2)}) copy-start(f32[1,896]{1,0:T(1,128)} %get-tuple-element.131) | copy-start | bytes 10756
  440.5 18.2 %copy-start.23 = (f32[32,256]{1,0:T(8,128)S(1)}, f32[32,256]{1,0:T(8,128)}, u32[]{:S(2)}) copy-start(f32[32,256]{1,0:T(8,128)} %get-tuple-element.126) | copy-start | bytes 98308
  457.0 24.6 %copy-start.15 = (f32[28,1152]{1,0:T(8,128)S(1)}, f32[28,1152]{1,0:T(8,128)}, u32[]{:S(2)}) copy-start(f32[28,1152]{1,0:T(8,128)} %param.34) | copy-start | bytes 387076
  457.0 24.6 %copy-start.20 = (f32[28,1152]{1,0:T(8,128)S(1)}, f32[28,1152]{1,0:T(8,128)}, u32[]{:S(2)}) copy-start(f32[28,1152]{1,0:T(8,128)} %param.40) | copy-start | bytes 387076
  457.0 24.6 %copy-start.21 = (f32[28,1152]{1,0:T(8,128)S(1)}, f32[28,1152]{1,0:T(8,128)}, u32[]{:S(2)}) copy-start(f32[28,1152]{1,0:T(8,128)} %param.46) | copy-start | bytes 387076
  482.5 42.6 %copy-start.7 = (f32[152,896]{1,0:T(8,128)S(1)}, f32[152,896]{1,0:T(8,128)}, u32[]{:S(2)}) copy-start(f32[152,896]{1,0:T(8,128)} %param.37) | copy-start | bytes 1634308
  482.5 42.6 %copy-start.8 = (f32[152,896]{1,0:T(8,128)S(1)}, f32[152,896]{1,0:T(8,128)}, u32[]{:S(2)}) copy-start(f32[152,896]{1,0:T(8,128)} %get-tuple-element.274) | copy-start | bytes 1634308
  482.5 42.7 %copy-start.16 = (f32[152,896]{1,0:T(8,128)S(1)}, f32[152,896]{1,0:T(8,128)}, u32[]{:S(2)}) copy-start(f32[152,896]{1,0:T(8,128)} %param.43) | copy-start | bytes 1634308
  482.5 42.7 %copy-start.17 = (f32[152,896]{1,0:T(8,128)S(1)}, f32[152,896]{1,0:T(8,128)}, u32[]{:S(2)}) copy-start(f32[152,896]{1,0:T(8,128)} %param.49) | copy-start | bytes 1634308
  (16 other events, 66.4 us)
Sparse Core Ops, SparseCore 0:
  12.4 73.9 all-gather.2
  89.8 73.5 all-gather.4
